TPU v7x, 128 devices: a whole 4x4x4 slice. The times are simulated.
128 devices in a mesh: plane: 8 (over x, core), band: 16 (over y, z).
Axes of the slice: x: 4, y: 4, z: 4, core: 2. Of those that a mesh axis runs over, the one named last changes fastest.
Arguments:
- slabs: bfloat16 [8, 1024, 4, 8192], P('plane', 'band'), may hold values from -1 to 1
- slot_block: int32 [8, 1024], P('plane', 'band'), may hold values from 0 to 31, as said below
- lens_weight: float32 [8], P('plane'), may hold values from 0.1 to 0.4
Outputs:
- ray_state: float32 [8, 6, 128, 8192], P('plane', None, 'band')
Inputs may be any that keep to these rules, and one draw needn't show every extreme that they name: `slot_block`: entry j of a device's list names the row-block that slot j adds to; the blocks of band b are b * 2 to b * 2 + 1. No device names blocks of one band in more than 8 slots, and in every plane some bands are named 8 times by every device of that plane.
All inputs are finite; a program needn't handle non-finite values.
Results may differ from a plain program's by a relative error of at most 0.006.
Values may be sent and summed in bfloat16 or wider, within the bound.
No kernel may reach another device: no remote copies, remote signals or barrier semaphores. Data moves between devices by JAX's collectives and lax.ppermute only.
A program may use at most 64 MiB of HBM per device.

v0:
```python
import jax
import jax.numpy as jnp
from jax import lax
from jax.sharding import PartitionSpec as P

NCOL = 8192
R = 8
BLK = 4
CAP = 8
SWEEPS = 20
BPB = 2


MASS = 0.05


def padded_2(array, sides, width):
    for axis, dim in sides:
        size, length = (lax.axis_size(axis), array.shape[dim])
        up = [(i, (i + 1) % size) for i in range(size - 1)]
        down = [(j, i) for i, j in up]
        last = lax.slice_in_dim(array, length - width, length, axis=dim)
        initial = lax.slice_in_dim(array, 0, width, axis=dim)
        before = lax.ppermute(last, axis, up)
        after = lax.ppermute(initial, axis, down)
        array = jnp.concatenate([before, array, after], axis=dim)
    return array


def from_behind(block, axis, distance):
    devices = range(lax.axis_size(axis))
    route = [(i - distance, i) for i in devices if i - distance in devices]
    return lax.ppermute(block, axis, route)


def relay_density(slabs, slot_block):
    bands = lax.axis_size("band")
    blocks = slot_block[0]
    count = blocks.shape[0]
    band_of = blocks // BPB
    offset = blocks % BPB
    position = jnp.arange(count, dtype=jnp.int32)
    same_band = band_of[:, None] == band_of[None, :]
    earlier = position[None, :] < position[:, None]
    rank = jnp.sum(jnp.logical_and(same_band, earlier).astype(jnp.int32), axis=1)
    flat_slot = band_of * CAP + rank
    send_rows = jnp.zeros((bands * CAP, BLK, NCOL), jnp.bfloat16).at[flat_slot].set(slabs[0])
    send_offsets = (
        jnp.zeros((bands * CAP,), jnp.bfloat16).at[flat_slot].set(offset.astype(jnp.bfloat16))
    )
    send_rows = send_rows.reshape(bands, CAP, BLK, NCOL)
    send_offsets = send_offsets.reshape(bands, CAP)
    got_rows, got_offsets = (
        lax.all_to_all(send_rows, "band", split_axis=0, concat_axis=0, tiled=True),
        lax.all_to_all(send_offsets, "band", split_axis=0, concat_axis=0, tiled=True),
    )
    got_rows = got_rows.reshape(bands * CAP, BLK * NCOL)
    got_offsets = got_offsets.reshape(bands * CAP).astype(jnp.int32)
    selector = (got_offsets[None, :] == jnp.arange(BPB, dtype=jnp.int32)[:, None]).astype(
        jnp.bfloat16
    )
    density = jnp.dot(selector, got_rows, preferred_element_type=jnp.float32)
    return density.reshape(R, NCOL)


def sweep_padded(padded, density_part):
    inner = padded[1:-1]
    neighbours = padded[:-2] + padded[2:] + jnp.roll(inner, 1, 1) + jnp.roll(inner, -1, 1)
    return (density_part + neighbours) / (4.0 + MASS)


def solve_potential(density):

    def body_sweep(index, potential):
        padded = padded_2(potential, (("band", 0),), 1)
        return sweep_padded(padded, density)

    return lax.fori_loop(0, SWEEPS, body_sweep, jnp.zeros((R, NCOL), jnp.float32))


def plane_maps(potential, weight):
    padded = padded_2(potential, (("band", 0),), 1)
    north = padded[2:]
    south = padded[:-2]
    east = jnp.roll(potential, -1, 1)
    west = jnp.roll(potential, 1, 1)
    grad_one = 0.5 * (east - west)
    grad_two = 0.5 * (north - south)
    second_one = east - 2.0 * potential + west
    second_two = north - 2.0 * potential + south
    mixed = 0.25 * (
        jnp.roll(north, -1, 1)
        - jnp.roll(north, 1, 1)
        - jnp.roll(south, -1, 1)
        + jnp.roll(south, 1, 1)
    )
    return (
        1.0 - weight * second_one,
        -weight * mixed,
        1.0 - weight * second_two,
        weight * grad_one,
        weight * grad_two,
    )


def apply_map(maps, state):
    p11, p12, p22, c1, c2 = maps
    a11, a12, a21, a22, s1, s2 = (state[0], state[1], state[2], state[3], state[4], state[5])
    return jnp.stack(
        [
            p11 * a11 + p12 * a21,
            p11 * a12 + p12 * a22,
            p12 * a11 + p22 * a21,
            p12 * a12 + p22 * a22,
            p11 * s1 + p12 * s2 + c1,
            p12 * s1 + p22 * s2 + c2,
        ]
    )


def body(slabs, slot_block, lens_weight):
    density = relay_density(slabs, slot_block)
    potential = solve_potential(density)
    maps = plane_maps(potential, lens_weight[0])
    ones = jnp.ones((R, NCOL), jnp.float32)
    zeros = jnp.zeros((R, NCOL), jnp.float32)
    identity_state = jnp.stack([ones, zeros, zeros, ones, zeros, zeros])
    state = apply_map(maps, identity_state)
    first = lax.axis_index("plane") == 0
    for hop_index in range(lax.axis_size("plane") - 1):
        incoming = from_behind(state, "plane", 1)
        incoming = jnp.where(first, identity_state, incoming)
        state = apply_map(maps, incoming)
    return (state - identity_state)[None]


def solution(mesh):
    in_specs = (P("plane", "band", None, None), P("plane", "band"), P("plane"))
    out_specs = P("plane", None, "band", None)
    return jax.shard_map(body, mesh=mesh, in_specs=in_specs, out_specs=out_specs, check_vma=False)
```

profile of v0, /device:TPU:28, one launch (start us, length us, event | category | flops | bytes accessed | tf_op | source)
XLA Modules:
  0.0 586.8 jit_solution(4121851323107347380)
XLA Ops:
  3.8 8.2 %all-to-all-start = ((bf16[16,1,8]{2,1,0:T(2,128)(2,1)}), bf16[16,1,8]{2,1,0:T(2,128)(2,1)S(1)}, u32[]{:S(2)}, u32[]{:S(2)}) async-start(bf16[16,1,8]{2,1,0:T(2,128)(2,1)} %all_to_all.12), calls=%async_computation | async-start | bytes 16384 | tf_op jit(solution)/shard_map/all_to_all | solution.py:55
  12.0 7.4 %broadcast_in_dim.5 = bf16[128,4,8192]{2,1,0:T(4,128)(2,1)} broadcast(bf16[]{:T(256)} %constant.49.clone.1), dimensions={} | broadcast | bytes 8388610 | tf_op jit(solution)/shard_map/broadcast_in_dim | solution.py:47
  19.4 19.0 %scatter_fusion = bf16[128,4,8192]{2,1,0:T(4,128)(2,1)} fusion(bf16[128,4,8192]{2,1,0:T(4,128)(2,1)} %broadcast_in_dim.5, s32[64]{0:T(128)S(1)} %fusion.24, bf16[64,4,8192]{2,1,0:T(4,128)(2,1)} %bitcast.394), kind=kCustom, calls=%fused_computation.1 | custom fusion | bytes 12583168 | tf_op jit(solution)/shard_map/scatter | solution.py:47
  38.5 7.1 %all-to-all-start.1 = ((bf16[16,8,4,8192]{3,2,1,0:T(4,128)(2,1)}), bf16[16,8,4,8192]{3,2,1,0:T(4,128)(2,1)}, u32[]{:S(2)}, u32[]{:S(2)}) async-start(bf16[16,8,4,8192]{3,2,1,0:T(4,128)(2,1)} %bitcast.392), calls=%async_computation.1 | async-start | bytes 16777216 | tf_op jit(solution)/shard_map/all_to_all | solution.py:54
  46.3 141.5 %all-to-all-done.1 = bf16[16,8,4,8192]{3,2,1,0:T(4,128)(2,1)} async-done(((bf16[16,8,4,8192]{3,2,1,0:T(4,128)(2,1)}), bf16[16,8,4,8192]{3,2,1,0:T(4,128)(2,1)}, u32[]{:S(2)}, u32[]{:S(2)}) %all-to-all-start.1) | async-done | bytes 8388640 | tf_op jit(solution)/shard_map/all_to_all | solution.py:54
  187.8 12.4 %copy.6 = bf16[16,8,4,8192]{3,1,2,0:T(8,128)(2,1)} copy(bf16[16,8,4,8192]{3,2,1,0:T(4,128)(2,1)} %all-to-all-done.1) | data formatting | bytes 16777216
  200.2 4.6 fusion.20
  205.0 206.7 %while.11 = (s32[]{:T(128)}, f32[8,8192]{1,0:T(8,128)S(1)}, f32[8,8192]{1,0:T(8,128)S(1)}, s32[]{:T(128)}, s32[]{:T(128)}) while((s32[]{:T(128)}, f32[8,8192]{1,0:T(8,128)S(1)}, f32[8,8192]{1,0:T(8,128)S(1)}, s32[]{:T(128)}, s32[]{:T(128)}) %tuple.46), condition=%wide.region_4.5_spmd.clone, body=%wide.region_3.4_spmd.clone.sunk | while | flops 655363 | bytes 3342487 | solution.py:78
  205.1 6.7 %collective-permute-start = (f32[1,8192]{1,0:T(1,128)S(1)}, f32[1,8192]{1,0:T(1,128)S(1)}, u32[]{:S(2)}, u32[]{:S(2)}) collective-permute-start(f32[1,8192]{1,0:T(1,128)S(1)} %get-tuple-element.97), channel_id=1, source_target_pairs={{1,0},{2,1},{3,2},{4,3},{5,4},{6,5},{7,6},{8,7},{9,8},{10,9},{11,1... | collective-permute-start | bytes 98312 | tf_op jit(solution)/shard_map/while/body/eval_jaxpr/ppermute | solution.py:25
  213.9 5.8 collective-permute-done.1
  221.9 3.9 collective-permute-start.1
  232.0 3.9 collective-permute-start.1
  242.1 3.9 collective-permute-start.1
  252.2 3.9 collective-permute-start.1
  292.6 3.9 collective-permute-start.1
  363.3 3.9 collective-permute-start.1
  383.5 3.9 collective-permute-start.1
  428.9 20.1 %collective-permute-done.4 = f32[6,8,8192]{2,1,0:T(8,128)} collective-permute-done((f32[6,8,8192]{2,1,0:T(8,128)}, f32[6,8,8192]{2,1,0:T(8,128)}, u32[]{:S(2)}, u32[]{:S(2)}) %collective-permute-start.4) | collective-permute-done | bytes 1572896 | tf_op jit(solution)/shard_map/ppermute | solution.py:33
  453.0 19.8 %collective-permute-done.5 = f32[6,8,8192]{2,1,0:T(8,128)S(1)} collective-permute-done((f32[6,8,8192]{2,1,0:T(8,128)S(1)}, f32[6,8,8192]{2,1,0:T(8,128)S(1)}, u32[]{:S(2)}, u32[]{:S(2)}) %collective-permute-start.5) | collective-permute-done | bytes 1572896 | tf_op jit(solution)/shard_map/ppermute | solution.py:33
  475.4 19.8 %collective-permute-done.6 = f32[6,8,8192]{2,1,0:T(8,128)S(1)} collective-permute-done((f32[6,8,8192]{2,1,0:T(8,128)S(1)}, f32[6,8,8192]{2,1,0:T(8,128)S(1)}, u32[]{:S(2)}, u32[]{:S(2)}) %collective-permute-start.6) | collective-permute-done | bytes 1572896 | tf_op jit(solution)/shard_map/ppermute | solution.py:33
  497.8 19.8 %collective-permute-done.7 = f32[6,8,8192]{2,1,0:T(8,128)S(1)} collective-permute-done((f32[6,8,8192]{2,1,0:T(8,128)S(1)}, f32[6,8,8192]{2,1,0:T(8,128)S(1)}, u32[]{:S(2)}, u32[]{:S(2)}) %collective-permute-start.7) | collective-permute-done | bytes 1572896 | tf_op jit(solution)/shard_map/ppermute | solution.py:33
  520.2 19.8 %collective-permute-done.8 = f32[6,8,8192]{2,1,0:T(8,128)S(1)} collective-permute-done((f32[6,8,8192]{2,1,0:T(8,128)S(1)}, f32[6,8,8192]{2,1,0:T(8,128)S(1)}, u32[]{:S(2)}, u32[]{:S(2)}) %collective-permute-start.8) | collective-permute-done | bytes 1572896 | tf_op jit(solution)/shard_map/ppermute | solution.py:33
  542.6 19.8 %collective-permute-done.9 = f32[6,8,8192]{2,1,0:T(8,128)S(1)} collective-permute-done((f32[6,8,8192]{2,1,0:T(8,128)S(1)}, f32[6,8,8192]{2,1,0:T(8,128)S(1)}, u32[]{:S(2)}, u32[]{:S(2)}) %collective-permute-start.9) | collective-permute-done | bytes 1572896 | tf_op jit(solution)/shard_map/ppermute | solution.py:33
  565.0 19.8 %collective-permute-done.10 = f32[6,8,8192]{2,1,0:T(8,128)S(1)} collective-permute-done((f32[6,8,8192]{2,1,0:T(8,128)S(1)}, f32[6,8,8192]{2,1,0:T(8,128)S(1)}, u32[]{:S(2)}, u32[]{:S(2)}) %collective-permute-start.10) | collective-permute-done | bytes 1572896 | tf_op jit(solution)/shard_map/ppermute | solution.py:33
  (260 shorter events, 205.6 us)
Async XLA Ops:
  3.8 34.6 %all-to-all-start = ((bf16[16,1,8]{2,1,0:T(2,128)(2,1)}), bf16[16,1,8]{2,1,0:T(2,128)(2,1)S(1)}, u32[]{:S(2)}, u32[]{:S(2)}) async-start(bf16[16,1,8]{2,1,0:T(2,128)(2,1)} %all_to_all.12), calls=%async_computation | async-start | bytes 16384 | tf_op jit(solution)/shard_map/all_to_all | solution.py:55
  38.5 149.4 %all-to-all-start.1 = ((bf16[16,8,4,8192]{3,2,1,0:T(4,128)(2,1)}), bf16[16,8,4,8192]{3,2,1,0:T(4,128)(2,1)}, u32[]{:S(2)}, u32[]{:S(2)}) async-start(bf16[16,8,4,8192]{3,2,1,0:T(4,128)(2,1)} %bitcast.392), calls=%async_computation.1 | async-start | bytes 16777216 | tf_op jit(solution)/shard_map/all_to_all | solution.py:54
  205.1 8.8 %collective-permute-start = (f32[1,8192]{1,0:T(1,128)S(1)}, f32[1,8192]{1,0:T(1,128)S(1)}, u32[]{:S(2)}, u32[]{:S(2)}) collective-permute-start(f32[1,8192]{1,0:T(1,128)S(1)} %get-tuple-element.97), channel_id=1, source_target_pairs={{1,0},{2,1},{3,2},{4,3},{5,4},{6,5},{7,6},{8,7},{9,8},{10,9},{11,1... | collective-permute-start | bytes 98312 | tf_op jit(solution)/shard_map/while/body/eval_jaxpr/ppermute | solution.py:25
  221.9 7.9 %collective-permute-start.1 = (f32[1,8192]{1,0:T(1,128)S(1)}, f32[1,8192]{1,0:T(1,128)S(1)}, u32[]{:S(2)}, u32[]{:S(2)}) collective-permute-start(f32[1,8192]{1,0:T(1,128)S(1)} %get-tuple-element.98), channel_id=1, source_target_pairs={{0,1},{1,2},{2,3},{3,4},{4,5},{5,6},{6,7},{7,8},{8,9},{9,10},{10,1... | collective-permute-start | bytes 98312 | tf_op jit(solution)/shard_map/while/body/eval_jaxpr/ppermute | solution.py:24
  242.1 7.9 %collective-permute-start.1 = (f32[1,8192]{1,0:T(1,128)S(1)}, f32[1,8192]{1,0:T(1,128)S(1)}, u32[]{:S(2)}, u32[]{:S(2)}) collective-permute-start(f32[1,8192]{1,0:T(1,128)S(1)} %get-tuple-element.98), channel_id=1, source_target_pairs={{0,1},{1,2},{2,3},{3,4},{4,5},{5,6},{6,7},{7,8},{8,9},{9,10},{10,1... | collective-permute-start | bytes 98312 | tf_op jit(solution)/shard_map/while/body/eval_jaxpr/ppermute | solution.py:24
  252.2 8.0 %collective-permute-start.1 = (f32[1,8192]{1,0:T(1,128)S(1)}, f32[1,8192]{1,0:T(1,128)S(1)}, u32[]{:S(2)}, u32[]{:S(2)}) collective-permute-start(f32[1,8192]{1,0:T(1,128)S(1)} %get-tuple-element.98), channel_id=1, source_target_pairs={{0,1},{1,2},{2,3},{3,4},{4,5},{5,6},{6,7},{7,8},{8,9},{9,10},{10,1... | collective-permute-start | bytes 98312 | tf_op jit(solution)/shard_map/while/body/eval_jaxpr/ppermute | solution.py:24
  272.4 7.9 %collective-permute-start.1 = (f32[1,8192]{1,0:T(1,128)S(1)}, f32[1,8192]{1,0:T(1,128)S(1)}, u32[]{:S(2)}, u32[]{:S(2)}) collective-permute-start(f32[1,8192]{1,0:T(1,128)S(1)} %get-tuple-element.98), channel_id=1, source_target_pairs={{0,1},{1,2},{2,3},{3,4},{4,5},{5,6},{6,7},{7,8},{8,9},{9,10},{10,1... | collective-permute-start | bytes 98312 | tf_op jit(solution)/shard_map/while/body/eval_jaxpr/ppermute | solution.py:24
  282.5 7.9 %collective-permute-start.1 = (f32[1,8192]{1,0:T(1,128)S(1)}, f32[1,8192]{1,0:T(1,128)S(1)}, u32[]{:S(2)}, u32[]{:S(2)}) collective-permute-start(f32[1,8192]{1,0:T(1,128)S(1)} %get-tuple-element.98), channel_id=1, source_target_pairs={{0,1},{1,2},{2,3},{3,4},{4,5},{5,6},{6,7},{7,8},{8,9},{9,10},{10,1... | collective-permute-start | bytes 98312 | tf_op jit(solution)/shard_map/while/body/eval_jaxpr/ppermute | solution.py:24
  292.6 7.9 %collective-permute-start.1 = (f32[1,8192]{1,0:T(1,128)S(1)}, f32[1,8192]{1,0:T(1,128)S(1)}, u32[]{:S(2)}, u32[]{:S(2)}) collective-permute-start(f32[1,8192]{1,0:T(1,128)S(1)} %get-tuple-element.98), channel_id=1, source_target_pairs={{0,1},{1,2},{2,3},{3,4},{4,5},{5,6},{6,7},{7,8},{8,9},{9,10},{10,1... | collective-permute-start | bytes 98312 | tf_op jit(solution)/shard_map/while/body/eval_jaxpr/ppermute | solution.py:24
  302.7 7.9 %collective-permute-start.1 = (f32[1,8192]{1,0:T(1,128)S(1)}, f32[1,8192]{1,0:T(1,128)S(1)}, u32[]{:S(2)}, u32[]{:S(2)}) collective-permute-start(f32[1,8192]{1,0:T(1,128)S(1)} %get-tuple-element.98), channel_id=1, source_target_pairs={{0,1},{1,2},{2,3},{3,4},{4,5},{5,6},{6,7},{7,8},{8,9},{9,10},{10,1... | collective-permute-start | bytes 98312 | tf_op jit(solution)/shard_map/while/body/eval_jaxpr/ppermute | solution.py:24
  322.9 7.9 %collective-permute-start.1 = (f32[1,8192]{1,0:T(1,128)S(1)}, f32[1,8192]{1,0:T(1,128)S(1)}, u32[]{:S(2)}, u32[]{:S(2)}) collective-permute-start(f32[1,8192]{1,0:T(1,128)S(1)} %get-tuple-element.98), channel_id=1, source_target_pairs={{0,1},{1,2},{2,3},{3,4},{4,5},{5,6},{6,7},{7,8},{8,9},{9,10},{10,1... | collective-permute-start | bytes 98312 | tf_op jit(solution)/shard_map/while/body/eval_jaxpr/ppermute | solution.py:24
  333.0 8.0 %collective-permute-start.1 = (f32[1,8192]{1,0:T(1,128)S(1)}, f32[1,8192]{1,0:T(1,128)S(1)}, u32[]{:S(2)}, u32[]{:S(2)}) collective-permute-start(f32[1,8192]{1,0:T(1,128)S(1)} %get-tuple-element.98), channel_id=1, source_target_pairs={{0,1},{1,2},{2,3},{3,4},{4,5},{5,6},{6,7},{7,8},{8,9},{9,10},{10,1... | collective-permute-start | bytes 98312 | tf_op jit(solution)/shard_map/while/body/eval_jaxpr/ppermute | solution.py:24
  343.1 7.9 %collective-permute-start.1 = (f32[1,8192]{1,0:T(1,128)S(1)}, f32[1,8192]{1,0:T(1,128)S(1)}, u32[]{:S(2)}, u32[]{:S(2)}) collective-permute-start(f32[1,8192]{1,0:T(1,128)S(1)} %get-tuple-element.98), channel_id=1, source_target_pairs={{0,1},{1,2},{2,3},{3,4},{4,5},{5,6},{6,7},{7,8},{8,9},{9,10},{10,1... | collective-permute-start | bytes 98312 | tf_op jit(solution)/shard_map/while/body/eval_jaxpr/ppermute | solution.py:24
  363.3 7.9 %collective-permute-start.1 = (f32[1,8192]{1,0:T(1,128)S(1)}, f32[1,8192]{1,0:T(1,128)S(1)}, u32[]{:S(2)}, u32[]{:S(2)}) collective-permute-start(f32[1,8192]{1,0:T(1,128)S(1)} %get-tuple-element.98), channel_id=1, source_target_pairs={{0,1},{1,2},{2,3},{3,4},{4,5},{5,6},{6,7},{7,8},{8,9},{9,10},{10,1... | collective-permute-start | bytes 98312 | tf_op jit(solution)/shard_map/while/body/eval_jaxpr/ppermute | solution.py:24
  373.4 7.9 %collective-permute-start.1 = (f32[1,8192]{1,0:T(1,128)S(1)}, f32[1,8192]{1,0:T(1,128)S(1)}, u32[]{:S(2)}, u32[]{:S(2)}) collective-permute-start(f32[1,8192]{1,0:T(1,128)S(1)} %get-tuple-element.98), channel_id=1, source_target_pairs={{0,1},{1,2},{2,3},{3,4},{4,5},{5,6},{6,7},{7,8},{8,9},{9,10},{10,1... | collective-permute-start | bytes 98312 | tf_op jit(solution)/shard_map/while/body/eval_jaxpr/ppermute | solution.py:24
  383.5 7.9 %collective-permute-start.1 = (f32[1,8192]{1,0:T(1,128)S(1)}, f32[1,8192]{1,0:T(1,128)S(1)}, u32[]{:S(2)}, u32[]{:S(2)}) collective-permute-start(f32[1,8192]{1,0:T(1,128)S(1)} %get-tuple-element.98), channel_id=1, source_target_pairs={{0,1},{1,2},{2,3},{3,4},{4,5},{5,6},{6,7},{7,8},{8,9},{9,10},{10,1... | collective-permute-start | bytes 98312 | tf_op jit(solution)/shard_map/while/body/eval_jaxpr/ppermute | solution.py:24
  393.6 7.9 %collective-permute-start.1 = (f32[1,8192]{1,0:T(1,128)S(1)}, f32[1,8192]{1,0:T(1,128)S(1)}, u32[]{:S(2)}, u32[]{:S(2)}) collective-permute-start(f32[1,8192]{1,0:T(1,128)S(1)} %get-tuple-element.98), channel_id=1, source_target_pairs={{0,1},{1,2},{2,3},{3,4},{4,5},{5,6},{6,7},{7,8},{8,9},{9,10},{10,1... | collective-permute-start | bytes 98312 | tf_op jit(solution)/shard_map/while/body/eval_jaxpr/ppermute | solution.py:24
  426.9 22.0 %collective-permute-start.4 = (f32[6,8,8192]{2,1,0:T(8,128)}, f32[6,8,8192]{2,1,0:T(8,128)}, u32[]{:S(2)}, u32[]{:S(2)}) collective-permute-start(f32[6,8,8192]{2,1,0:T(8,128)} %get-tuple-element.41), channel_id=1, source_target_pairs={{0,16},{16,32},{32,48},{48,64},{64,80},{80,96},{96,112},{1,17},{17... | collective-permute-start | bytes 4718600 | tf_op jit(solution)/shard_map/ppermute | solution.py:33
  451.1 21.7 %collective-permute-start.5 = (f32[6,8,8192]{2,1,0:T(8,128)S(1)}, f32[6,8,8192]{2,1,0:T(8,128)S(1)}, u32[]{:S(2)}, u32[]{:S(2)}) collective-permute-start(f32[6,8,8192]{2,1,0:T(8,128)S(1)} %bitcast_dynamic-update-slice_fusion.36), channel_id=1, source_target_pairs={{0,16},{16,32},{32,48},{48,64},{64,80},{80,96},{96,112},{1,17},{17... | collective-permute-start | bytes 4718600 | tf_op jit(solution)/shard_map/ppermute | solution.py:33
  473.5 21.7 %collective-permute-start.6 = (f32[6,8,8192]{2,1,0:T(8,128)S(1)}, f32[6,8,8192]{2,1,0:T(8,128)S(1)}, u32[]{:S(2)}, u32[]{:S(2)}) collective-permute-start(f32[6,8,8192]{2,1,0:T(8,128)S(1)} %bitcast_dynamic-update-slice_fusion.30), channel_id=1, source_target_pairs={{0,16},{16,32},{32,48},{48,64},{64,80},{80,96},{96,112},{1,17},{17... | collective-permute-start | bytes 4718600 | tf_op jit(solution)/shard_map/ppermute | solution.py:33
  495.9 21.7 %collective-permute-start.7 = (f32[6,8,8192]{2,1,0:T(8,128)S(1)}, f32[6,8,8192]{2,1,0:T(8,128)S(1)}, u32[]{:S(2)}, u32[]{:S(2)}) collective-permute-start(f32[6,8,8192]{2,1,0:T(8,128)S(1)} %bitcast_dynamic-update-slice_fusion.24), channel_id=1, source_target_pairs={{0,16},{16,32},{32,48},{48,64},{64,80},{80,96},{96,112},{1,17},{17... | collective-permute-start | bytes 4718600 | tf_op jit(solution)/shard_map/ppermute | solution.py:33
  518.3 21.7 %collective-permute-start.8 = (f32[6,8,8192]{2,1,0:T(8,128)S(1)}, f32[6,8,8192]{2,1,0:T(8,128)S(1)}, u32[]{:S(2)}, u32[]{:S(2)}) collective-permute-start(f32[6,8,8192]{2,1,0:T(8,128)S(1)} %bitcast_dynamic-update-slice_fusion.18), channel_id=1, source_target_pairs={{0,16},{16,32},{32,48},{48,64},{64,80},{80,96},{96,112},{1,17},{17... | collective-permute-start | bytes 4718600 | tf_op jit(solution)/shard_map/ppermute | solution.py:33
  540.6 21.7 %collective-permute-start.9 = (f32[6,8,8192]{2,1,0:T(8,128)S(1)}, f32[6,8,8192]{2,1,0:T(8,128)S(1)}, u32[]{:S(2)}, u32[]{:S(2)}) collective-permute-start(f32[6,8,8192]{2,1,0:T(8,128)S(1)} %bitcast_dynamic-update-slice_fusion.12), channel_id=1, source_target_pairs={{0,16},{16,32},{32,48},{48,64},{64,80},{80,96},{96,112},{1,17},{17... | collective-permute-start | bytes 4718600 | tf_op jit(solution)/shard_map/ppermute | solution.py:33
  563.0 21.7 %collective-permute-start.10 = (f32[6,8,8192]{2,1,0:T(8,128)S(1)}, f32[6,8,8192]{2,1,0:T(8,128)S(1)}, u32[]{:S(2)}, u32[]{:S(2)}) collective-permute-start(f32[6,8,8192]{2,1,0:T(8,128)S(1)} %bitcast_dynamic-update-slice_fusion.6), channel_id=1, source_target_pairs={{0,16},{16,32},{32,48},{48,64},{64,80},{80,96},{96,112},{1,17},{17... | collective-permute-start | bytes 4718600 | tf_op jit(solution)/shard_map/ppermute | solution.py:33
  (27 other events, 176.6 us)
where the time goes:
time: 588 us; the launch traced here: 587 us
  waiting for transfers between devices  362 us (62%)
  starting transfers between devices  154 us (26%)
  local copies, waits for them, and re-layouts  46.4 us (8%)
  other arithmetic  18 us (3%)
    all_to_all x1, waiting for transfers between devices, relay_density(): lax.all_to_all(send_rows, 'band', split_axis=0, concat_axis=0, tiled=True)  141 us
    ppermute x7, waiting for transfers between devices, from_behind(): return lax.ppermute(block, axis, route)  139 us
    ppermute x21, waiting for transfers between devices, padded_2(): before = lax.ppermute(last, axis, up)  81 us
    ppermute x21, starting transfers between devices, padded_2(): before = lax.ppermute(last, axis, up)  80.4 us
    ppermute x21, starting transfers between devices, padded_2(): after = lax.ppermute(initial, axis, down)  45.1 us
    scatter x1, local copies, waits for them, and re-layouts, relay_density(): jnp.zeros((bands * CAP, BLK, NCOL), jnp.bfloat16).at[flat_slot]  19 us
    ppermute x7, starting transfers between devices, from_behind(): return lax.ppermute(block, axis, route)  13.4 us
    unnamed x2, local copies, waits for them, and re-layouts  12.4 us
  transfers between devices with their start and end apart: 51, of which 29 were waited for; matrix products, arithmetic and copies ran while one was open for 5% of the time, Pallas kernels for 0%

commit v1 on v0

v1 whole, which is shorter than its diff:
```python
import jax
import jax.numpy as jnp
from jax import lax
from jax.experimental import pallas as pl
from jax.experimental.pallas import tpu as pltpu
from jax.sharding import PartitionSpec as P

NCOL = 8192
NROW = 128
R = 8
BLK = 4
SLOTS = 64
SWEEPS = 20
PLANES = 8
BANDS = 16
MASS = 0.05

OWN = NCOL // BANDS
HALO = 24
SPAN = OWN + 2 * HALO
TILE = 128
ROWS = R + 2
MSG = ROWS * OWN // TILE
TOP = 14.0


def partial_kernel(slot_ref, slab_ref, out_ref, scale_ref, select_ref, most_ref):
    step = pl.program_id(0)

    @pl.when(step == 0)
    def _():
        lane = lax.broadcasted_iota(jnp.int32, (8, NROW), 1)
        sub = lax.broadcasted_iota(jnp.int32, (8, NROW), 0)
        for pair in range(SLOTS // 4):
            halves = []
            for half in range(2):
                first = 4 * pair + 2 * half
                block = jnp.where(sub < BLK, slot_ref[0, first], slot_ref[0, first + 1])
                row = block * BLK + (sub & (BLK - 1))
                halves.append(jnp.where(lane == row, 1.0, 0.0))
            select_ref[16 * pair : 16 * pair + 16] = jnp.concatenate(halves, 0).astype(jnp.bfloat16)
        most_ref[...] = jnp.zeros_like(most_ref)

    slabs = slab_ref[...].reshape(SLOTS * BLK, OWN)
    part = lax.dot_general(
        slabs, select_ref[...], (((0,), (0,)), ((), ())), preferred_element_type=jnp.float32
    )
    after = lax.rem(step + 1, BANDS)
    before = lax.rem(step + BANDS - 1, BANDS)
    out_ref[step, HALO : HALO + OWN] = part
    out_ref[after, 0:HALO] = part[OWN - HALO :]
    out_ref[before, HALO + OWN :] = part[:HALO]
    most_ref[...] = jnp.maximum(
        most_ref[...], jnp.max(jnp.abs(part).reshape(OWN // 8, 8, NROW), axis=0)
    )

    @pl.when(step == BANDS - 1)
    def _():
        most = jnp.max(most_ref[...])
        most = jnp.full((8, NROW), most, jnp.float32)
        power = jnp.ceil(jnp.log2(jnp.maximum(most, 2.0**-100)))
        scale_ref[...] = jnp.exp2(TOP - power)
        mark = power * jnp.exp2(power - TOP)
        for band in range(BANDS):
            out_ref[band, 0:1] = mark[0:1]


def partial_densities(slabs, slot_block):
    return pl.pallas_call(
        partial_kernel,
        grid=(BANDS,),
        in_specs=[
            pl.BlockSpec(memory_space=pltpu.SMEM),
            pl.BlockSpec((SLOTS, BLK, OWN), lambda step: (0, 0, step)),
        ],
        out_specs=[
            pl.BlockSpec((BANDS, SPAN, NROW), lambda step: (0, 0, 0)),
            pl.BlockSpec((8, NROW), lambda step: (0, 0)),
        ],
        out_shape=[
            jax.ShapeDtypeStruct((BANDS, SPAN, NROW), jnp.float32),
            jax.ShapeDtypeStruct((8, NROW), jnp.float32),
        ],
        scratch_shapes=[
            pltpu.VMEM((SLOTS * BLK, NROW), jnp.bfloat16),
            pltpu.VMEM((8, NROW), jnp.float32),
        ],
        compiler_params=pltpu.CompilerParams(vmem_limit_bytes=24 * 2**20),
        name="partial_densities",
    )(slot_block, slabs)


STRIP = 80


def relax_kernel(weight_ref, density_ref, out_ref, even_ref, odd_ref, turned_ref):
    zero = jnp.zeros((8, NROW), jnp.float32)
    for ref in (even_ref, odd_ref):
        ref[0:8] = zero
        ref[8 + SPAN :] = zero
    turned_ref[0:8] = zero
    turned_ref[8 + NROW :] = zero
    lane = lax.broadcasted_iota(jnp.int32, (STRIP, NROW), 1)
    not_first = lane > 0
    not_last = lane < NROW - 1
    share = 1.0 / (4.0 + MASS)
    even_ref[8 : 8 + SPAN] = density_ref[...] * share

    def sweep(src, dst):
        for start in range(8, 8 + SPAN, STRIP):
            here = src[start : start + STRIP]
            total = src[start - 1 : start - 1 + STRIP] + src[start + 1 : start + 1 + STRIP]
            total += jnp.where(not_first, pltpu.roll(here, 1, 1), 0.0)
            total += jnp.where(not_last, pltpu.roll(here, NROW - 1, 1), 0.0)
            total += density_ref[start - 8 : start - 8 + STRIP]
            dst[start : start + STRIP] = total * share

    def two_sweeps(_, carry):
        sweep(even_ref, odd_ref)
        sweep(odd_ref, even_ref)
        return carry

    lax.fori_loop(0, (SWEEPS - 1) // 2, two_sweeps, 0)
    sweep(even_ref, odd_ref)
    weight = weight_ref[0]
    for tile in range(OWN // TILE):
        first = 8 + HALO + tile * TILE
        turned_ref[8 : 8 + NROW] = (odd_ref[first : first + TILE] * weight).T
        for band in range(BANDS):
            out_ref[band, tile * ROWS : (tile + 1) * ROWS] = turned_ref[
                R * band + 7 : R * band + 7 + ROWS
            ]


def relaxed(density, weight):
    return pl.pallas_call(
        relax_kernel,
        in_specs=[
            pl.BlockSpec(memory_space=pltpu.SMEM),
            pl.BlockSpec(memory_space=pltpu.VMEM),
        ],
        out_specs=pl.BlockSpec(memory_space=pltpu.VMEM),
        out_shape=jax.ShapeDtypeStruct((BANDS, MSG, TILE), jnp.float32),
        scratch_shapes=[
            pltpu.VMEM((SPAN + 16, NROW), jnp.float32),
            pltpu.VMEM((SPAN + 16, NROW), jnp.float32),
            pltpu.VMEM((NROW + 16, TILE), jnp.float32),
        ],
        compiler_params=pltpu.CompilerParams(vmem_limit_bytes=24 * 2**20),
        name="relaxed",
    )(weight, density)


GROUP = OWN // TILE


def chain_kernel(*refs):
    pieces, out_ref, held, sems = refs[:PLANES], refs[PLANES], refs[-2], refs[-1]
    me = lax.axis_index("plane")
    chip, core = me // 2, lax.rem(me, 2)
    order = []
    for back in range(4):
        for other in range(2):
            plane = 2 * lax.rem(chip - back + 4, 4) + (core + other * (1 - 2 * core))
            order.append(plane)
            copy = pltpu.make_async_copy(pieces[2 * back + other], held.at[plane], sems.at[plane])
            copy.start()
    for plane in range(PLANES):
        pltpu.make_async_copy(pieces[0], held.at[plane], sems.at[plane]).wait()
    lane = lax.broadcasted_iota(jnp.int32, (R, TILE), 1)
    is_first = lane == 0
    is_last = lane == TILE - 1

    def group_body(group, carry):
        here = pl.multiple_of(group * MSG, 8)
        behind = pl.multiple_of(lax.rem(group + BANDS - 1, BANDS) * MSG, 8)
        ahead = pl.multiple_of(lax.rem(group + 1, BANDS) * MSG, 8)
        starts = [behind + MSG - ROWS] + [here + t * ROWS for t in range(GROUP)] + [ahead]

        def plane_body(plane, state):
            mid, rise, both = [], [], []
            for start in starts:
                south = held[plane, pl.ds(start, R)]
                centre = held[plane, pl.ds(start + 1, R)]
                north = held[plane, pl.ds(start + 2, R)]
                mid.append(centre)
                rise.append(north - south)
                both.append(north + south)
            easts = [[pltpu.roll(x, TILE - 1, 1) for x in xs[1:]] for xs in (mid, rise)]
            wests = [[pltpu.roll(x, 1, 1) for x in xs[:-1]] for xs in (mid, rise)]
            new = []
            for t in range(GROUP):
                east, rise_east = (jnp.where(is_last, e[t + 1], e[t]) for e in easts)
                west, rise_west = (jnp.where(is_first, w[t], w[t + 1]) for w in wests)
                twice = 2.0 * mid[t + 1]
                c1 = 0.5 * (east - west)
                c2 = 0.5 * rise[t + 1]
                p11 = 1.0 - (east - twice + west)
                p22 = 1.0 - (both[t + 1] - twice)
                p12 = 0.25 * (rise_west - rise_east)
                a11, a12, a21, a22, s1, s2 = state[6 * t : 6 * t + 6]
                new += [
                    p11 * a11 + p12 * a21,
                    p11 * a12 + p12 * a22,
                    p12 * a11 + p22 * a21,
                    p12 * a12 + p22 * a22,
                    p11 * s1 + p12 * s2 + c1,
                    p12 * s1 + p22 * s2 + c2,
                ]
            return tuple(new)

        one = jnp.ones((R, TILE), jnp.float32)
        zero = jnp.zeros((R, TILE), jnp.float32)
        state = lax.fori_loop(0, me + 1, plane_body, (one, zero, zero, one, zero, zero) * GROUP)
        for t in range(GROUP):
            columns = pl.ds(pl.multiple_of(group * OWN + t * TILE, TILE), TILE)
            for entry in range(6):
                value = state[6 * t + entry]
                out_ref[0, entry, :, columns] = value - 1.0 if entry in (0, 3) else value
        return carry

    lax.fori_loop(0, BANDS, group_body, 0)


def chained(pieces):
    return pl.pallas_call(
        chain_kernel,
        in_specs=[pl.BlockSpec(memory_space=pl.ANY)] * PLANES,
        out_specs=pl.BlockSpec(memory_space=pltpu.VMEM),
        out_shape=jax.ShapeDtypeStruct((1, 6, R, NCOL), jnp.float32),
        scratch_shapes=[
            pltpu.VMEM((PLANES, BANDS * MSG, TILE), jnp.float32),
            pltpu.SemaphoreType.DMA((PLANES,)),
        ],
        compiler_params=pltpu.CompilerParams(vmem_limit_bytes=24 * 2**20),
        name="chained",
    )(*pieces)


def from_chip(block, back):
    return lax.ppermute(block, "plane", [(i, (i + 2 * back) % PLANES) for i in range(PLANES)])


def from_other_core(block):
    return lax.ppermute(block, "plane", [(i, i ^ 1) for i in range(PLANES)])


def body(slabs, slot_block, lens_weight):
    parts, scale = partial_densities(slabs[0], slot_block)
    sent = (parts * scale[0, 0]).astype(jnp.float16)
    got = lax.all_to_all(sent, "band", split_axis=0, concat_axis=0, tiled=True)
    unscale = jnp.exp2(got[:, 0:1, 0:1].astype(jnp.float32) - TOP)
    density = jnp.sum(got.astype(jnp.float32) * unscale, axis=0)
    messages = relaxed(density, lens_weight)
    rows = lax.all_to_all(messages, "band", split_axis=0, concat_axis=0, tiled=True)
    rows = rows.reshape(BANDS * MSG, TILE)
    chips = [rows] + [from_chip(rows, back) for back in (1, 2, 3)]
    pieces = []
    for piece in chips:
        pieces += [piece, from_other_core(piece)]
    return chained(pieces)


def solution(mesh):
    in_specs = (P("plane", "band", None, None), P("plane", "band"), P("plane"))
    out_specs = P("plane", None, "band", None)
    return jax.shard_map(body, mesh=mesh, in_specs=in_specs, out_specs=out_specs, check_vma=False)
```

time: 588 us -> 101 us (0.17)
  the two profiles are of different devices: /device:TPU:28 before, /device:TPU:7 now
where the time goes in v1:
time: 101 us
  waiting for transfers between devices  31.6 us (31%)
  starting transfers between devices  26.5 us (26%)
  Pallas kernels  25 us (25%)
  blocking collectives  10.6 us (10%)
  local copies, waits for them, and re-layouts  3.36 us (3%)
  other arithmetic  3.25 us (3%)
    all_to_all x1, waiting for transfers between devices, body(): got = lax.all_to_all(sent, 'band', split_axis=0, concat_axis=0, tiled=True)  30.2 us
    ppermute x4, starting transfers between devices, from_other_core(): return lax.ppermute(block, 'plane', [(i, i ^ 1) for i in range(PLANES)])  16.4 us
    pallas_call x1, Pallas kernels, chained(): pl.pallas_call(chain_kernel, in_specs=[pl.BlockSpec(memory_space=pl.ANY)]...  15.4 us
    all_to_all x1, blocking collectives, body(): lax.all_to_all(messages, 'band', split_axis=0, concat_axis=0, tiled=True)  10.6 us
    all_to_all x1, starting transfers between devices, body(): got = lax.all_to_all(sent, 'band', split_axis=0, concat_axis=0, tiled=True)  7.77 us
    pallas_call x1, Pallas kernels, partial_densities(): pl.pallas_call(partial_kernel, grid=(BANDS,), in_specs=[pl.BlockSpec(memo...  5.94 us
    pallas_call x1, Pallas kernels, relaxed(): pl.pallas_call(relax_kernel, in_specs=[pl.BlockSpec(memory_space=pltpu.SM...  3.63 us
    unnamed x4, local copies, waits for them, and re-layouts  2.84 us
  transfers between devices with their start and end apart: 8, of which 3 were waited for; matrix products, arithmetic and copies ran while one was open for 0% of the time, Pallas kernels for 0%

profile of v1, /device:TPU:7, one launch (start us, length us, event | category | flops | bytes accessed | tf_op | source)
XLA Modules:
  0.0 101.0 jit_solution(6178032285816269489)
XLA Ops:
  0.0 2.2 %copy-done = bf16[1,64,4,8192]{3,2,1,0:T(4,128)(2,1)S(1)} copy-done((bf16[1,64,4,8192]{3,2,1,0:T(4,128)(2,1)S(1)}, bf16[1,64,4,8192]{3,2,1,0:T(4,128)(2,1)}, u32[]{:S(2)}) %copy-start) | copy-done | bytes 4194328
  2.2 0.7 copy-done.1
  2.8 5.9 %partial_densities.1 = (f32[16,560,128]{2,1,0:T(8,128)S(1)}, f32[8,128]{1,0:T(8,128)S(1)}) custom-call(s32[1,64]{1,0:T(1,128)S(1)} %copy-done.1, bf16[64,4,8192]{2,1,0:T(4,128)(2,1)S(1)} %bitcast.3), custom_call_target="tpu_custom_call" | custom-call | tf_op jit(solution)/shard_map/partial_densities/pallas_call | solution.py:69
  8.8 0.5 slice.6
  9.3 2.5 %multiply_convert_fusion = f16[16,560,128]{2,1,0:T(8,128)(2,1)} fusion(f32[16,560,128]{2,1,0:T(8,128)S(1)} %get-tuple-element.7, f32[]{:T(128)} %bitcast.1), kind=kLoop, calls=%fused_computation.1 | loop fusion | flops 2293760 | bytes 6881284 | tf_op jit(solution)/shard_map/convert_element_type | solution.py:250
  11.8 7.8 %all-to-all-start = ((f16[16,560,128]{2,1,0:T(8,128)(2,1)}), f16[16,560,128]{2,1,0:T(8,128)(2,1)S(1)}, u32[]{:S(2)}, u32[]{:S(2)}) async-start(f16[16,560,128]{2,1,0:T(8,128)(2,1)} %multiply_convert_fusion), calls=%async_computation | async-start | bytes 4587520 | tf_op jit(solution)/shard_map/all_to_all | solution.py:251
  20.2 30.2 %all-to-all-done = f16[16,560,128]{2,1,0:T(8,128)(2,1)S(1)} async-done(((f16[16,560,128]{2,1,0:T(8,128)(2,1)}), f16[16,560,128]{2,1,0:T(8,128)(2,1)S(1)}, u32[]{:S(2)}, u32[]{:S(2)}) %all-to-all-start) | async-done | bytes 2293792 | tf_op jit(solution)/shard_map/all_to_all | solution.py:251
  50.4 0.2 fusion.3
  50.6 0.6 multiply_reduce_fusion.density_ref
  51.2 3.6 %relaxed.1 = f32[16,40,128]{2,1,0:T(8,128)S(1)} custom-call(f32[1]{0:T(128)S(6)} %copy.4.weight_ref, f32[560,128]{1,0:T(8,128)S(1)} %multiply_reduce_fusion.density_ref), custom_call_target="tpu_custom_call" | custom-call | tf_op jit(solution)/shard_map/relaxed/pallas_call | solution.py:136
  54.8 10.6 %all_to_all.10 = f32[16,40,128]{2,1,0:T(8,128)S(1)} all-to-all(f32[16,40,128]{2,1,0:T(8,128)S(1)} %relaxed.1), channel_id=1, replica_groups=mesh['plane'=8,'band'=16] {'band'}, dimensions={0} | all-to-all | bytes 655360 | tf_op jit(solution)/shard_map/all_to_all | solution.py:255
  65.4 0.2 collective-permute-start.1
  65.6 2.1 %collective-permute-start.3 = (f32[640,128]{1,0:T(8,128)S(1)}, f32[640,128]{1,0:T(8,128)S(1)}, u32[]{:S(2)}, u32[]{:S(2)}) collective-permute-start(f32[640,128]{1,0:T(8,128)S(1)} %bitcast.5), channel_id=1, source_target_pairs={{0,64},{16,80},{32,96},{48,112},{64,0},{80,16},{96,32},{112,48},{1... | collective-permute-start | bytes 983048 | tf_op jit(solution)/shard_map/ppermute | solution.py:241
  67.8 5.0 %collective-permute-start = (f32[640,128]{1,0:T(8,128)S(1)}, f32[640,128]{1,0:T(8,128)S(1)}, u32[]{:S(2)}, u32[]{:S(2)}) collective-permute-start(f32[640,128]{1,0:T(8,128)S(1)} %bitcast.7), channel_id=1, source_target_pairs={{0,16},{16,0},{32,48},{48,32},{64,80},{80,64},{96,112},{112,96},{1... | collective-permute-start | bytes 983048 | tf_op jit(solution)/shard_map/ppermute | solution.py:245
  72.8 0.0 collective-permute-done.1.refs_2_
  72.8 6.3 %collective-permute-start.2 = (f32[640,128]{1,0:T(8,128)S(1)}, f32[640,128]{1,0:T(8,128)S(1)}, u32[]{:S(2)}, u32[]{:S(2)}) collective-permute-start(f32[640,128]{1,0:T(8,128)S(1)} %collective-permute-done.1.refs_2_), channel_id=1, source_target_pairs={{0,16},{16,0},{32,48},{48,32},{64,80},{80,64},{96,112},{112,96},{1... | collective-permute-start | bytes 983048 | tf_op jit(solution)/shard_map/ppermute | solution.py:245
  79.1 1.8 %collective-permute-start.4 = (f32[640,128]{1,0:T(8,128)S(1)}, f32[640,128]{1,0:T(8,128)S(1)}, u32[]{:S(2)}, u32[]{:S(2)}) collective-permute-start(f32[640,128]{1,0:T(8,128)S(1)} %collective-permute-done.3.refs_4_), channel_id=1, source_target_pairs={{0,16},{16,0},{32,48},{48,32},{64,80},{80,64},{96,112},{112,96},{1... | collective-permute-start | bytes 983048 | tf_op jit(solution)/shard_map/ppermute | solution.py:245
  80.9 0.1 collective-permute-done.5.refs_6_
  81.0 3.3 %collective-permute-start.6 = (f32[640,128]{1,0:T(8,128)S(1)}, f32[640,128]{1,0:T(8,128)S(1)}, u32[]{:S(2)}, u32[]{:S(2)}) collective-permute-start(f32[640,128]{1,0:T(8,128)S(1)} %collective-permute-done.5.refs_6_), channel_id=1, source_target_pairs={{0,16},{16,0},{32,48},{48,32},{64,80},{80,64},{96,112},{112,96},{1... | collective-permute-start | bytes 983048 | tf_op jit(solution)/shard_map/ppermute | solution.py:245
  84.3 0.0 collective-permute-done.refs_1_
  84.3 0.0 collective-permute-done.2.refs_3_
  84.3 0.0 collective-permute-done.4.refs_5_
  84.3 1.2 %collective-permute-done.6.refs_7_ = f32[640,128]{1,0:T(8,128)S(1)} collective-permute-done((f32[640,128]{1,0:T(8,128)S(1)}, f32[640,128]{1,0:T(8,128)S(1)}, u32[]{:S(2)}, u32[]{:S(2)}) %collective-permute-start.6) | collective-permute-done | bytes 327712 | tf_op jit(solution)/shard_map/ppermute | solution.py:245
  85.6 15.4 %chained.1 = f32[1,6,8,8192]{3,2,1,0:T(8,128)} custom-call(f32[640,128]{1,0:T(8,128)S(1)} %bitcast.8, f32[640,128]{1,0:T(8,128)S(1)} %collective-permute-done.refs_1_, f32[640,128]{1,0:T(8,128)S(1)} %collective-permute-done.1.refs_2_, f32[640,128]{1,0:T(8,128)S(1)} %collective-permute-done.2.refs_3_, f32[640,128]{1,0:T(8,128)S(1)} %collective-permute-done.3.refs_4_, ...), custom_call_target="tpu_custom_call" | custom-call | tf_op jit(solution)/shard_map/chained/pallas_call | solution.py:226
  (4 shorter events, 0.0 us)
Async XLA Ops:
  0.0 2.2 %copy-start = (bf16[1,64,4,8192]{3,2,1,0:T(4,128)(2,1)S(1)}, bf16[1,64,4,8192]{3,2,1,0:T(4,128)(2,1)}, u32[]{:S(2)}) copy-start(bf16[1,64,4,8192]{3,2,1,0:T(4,128)(2,1)} %param.3) | copy-start | bytes 12582916
  2.2 0.7 copy-start.1
  11.8 38.6 %all-to-all-start = ((f16[16,560,128]{2,1,0:T(8,128)(2,1)}), f16[16,560,128]{2,1,0:T(8,128)(2,1)S(1)}, u32[]{:S(2)}, u32[]{:S(2)}) async-start(f16[16,560,128]{2,1,0:T(8,128)(2,1)} %multiply_convert_fusion), calls=%async_computation | async-start | bytes 4587520 | tf_op jit(solution)/shard_map/all_to_all | solution.py:251
  65.4 7.4 %collective-permute-start.1 = (f32[640,128]{1,0:T(8,128)S(1)}, f32[640,128]{1,0:T(8,128)S(1)}, u32[]{:S(2)}, u32[]{:S(2)}) collective-permute-start(f32[640,128]{1,0:T(8,128)S(1)} %bitcast.4), channel_id=1, source_target_pairs={{0,32},{16,48},{32,64},{48,80},{64,96},{80,112},{96,0},{112,16},{1... | collective-permute-start | bytes 983048 | tf_op jit(solution)/shard_map/ppermute | solution.py:241
  65.6 13.4 %collective-permute-start.3 = (f32[640,128]{1,0:T(8,128)S(1)}, f32[640,128]{1,0:T(8,128)S(1)}, u32[]{:S(2)}, u32[]{:S(2)}) collective-permute-start(f32[640,128]{1,0:T(8,128)S(1)} %bitcast.5), channel_id=1, source_target_pairs={{0,64},{16,80},{32,96},{48,112},{64,0},{80,16},{96,32},{112,48},{1... | collective-permute-start | bytes 983048 | tf_op jit(solution)/shard_map/ppermute | solution.py:241
  67.8 13.3 %collective-permute-start.5 = (f32[640,128]{1,0:T(8,128)S(1)}, f32[640,128]{1,0:T(8,128)S(1)}, u32[]{:S(2)}, u32[]{:S(2)}) collective-permute-start(f32[640,128]{1,0:T(8,128)S(1)} %bitcast.6), channel_id=1, source_target_pairs={{0,96},{16,112},{32,0},{48,16},{64,32},{80,48},{96,64},{112,80},{1... | collective-permute-start | bytes 983048 | tf_op jit(solution)/shard_map/ppermute | solution.py:241
  67.8 16.5 %collective-permute-start = (f32[640,128]{1,0:T(8,128)S(1)}, f32[640,128]{1,0:T(8,128)S(1)}, u32[]{:S(2)}, u32[]{:S(2)}) collective-permute-start(f32[640,128]{1,0:T(8,128)S(1)} %bitcast.7), channel_id=1, source_target_pairs={{0,16},{16,0},{32,48},{48,32},{64,80},{80,64},{96,112},{112,96},{1... | collective-permute-start | bytes 983048 | tf_op jit(solution)/shard_map/ppermute | solution.py:245
  72.8 11.5 %collective-permute-start.2 = (f32[640,128]{1,0:T(8,128)S(1)}, f32[640,128]{1,0:T(8,128)S(1)}, u32[]{:S(2)}, u32[]{:S(2)}) collective-permute-start(f32[640,128]{1,0:T(8,128)S(1)} %collective-permute-done.1.refs_2_), channel_id=1, source_target_pairs={{0,16},{16,0},{32,48},{48,32},{64,80},{80,64},{96,112},{112,96},{1... | collective-permute-start | bytes 983048 | tf_op jit(solution)/shard_map/ppermute | solution.py:245
  79.1 5.2 %collective-permute-start.4 = (f32[640,128]{1,0:T(8,128)S(1)}, f32[640,128]{1,0:T(8,128)S(1)}, u32[]{:S(2)}, u32[]{:S(2)}) collective-permute-start(f32[640,128]{1,0:T(8,128)S(1)} %collective-permute-done.3.refs_4_), channel_id=1, source_target_pairs={{0,16},{16,0},{32,48},{48,32},{64,80},{80,64},{96,112},{112,96},{1... | collective-permute-start | bytes 983048 | tf_op jit(solution)/shard_map/ppermute | solution.py:245
  81.0 4.5 %collective-permute-start.6 = (f32[640,128]{1,0:T(8,128)S(1)}, f32[640,128]{1,0:T(8,128)S(1)}, u32[]{:S(2)}, u32[]{:S(2)}) collective-permute-start(f32[640,128]{1,0:T(8,128)S(1)} %collective-permute-done.5.refs_6_), channel_id=1, source_target_pairs={{0,16},{16,0},{32,48},{48,32},{64,80},{80,64},{96,112},{112,96},{1... | collective-permute-start | bytes 983048 | tf_op jit(solution)/shard_map/ppermute | solution.py:245

commit v2 on v1

v2 whole, which is shorter than its diff:
```python
import functools

import jax
import jax.numpy as jnp
from jax import lax
from jax.experimental import pallas as pl
from jax.experimental.pallas import tpu as pltpu
from jax.sharding import PartitionSpec as P

NCOL = 8192
NROW = 128
R = 8
BLK = 4
SLOTS = 64
SWEEPS = 20
PLANES = 8
BANDS = 16
SIDE = 4
MASS = 0.05

OWN = NCOL // BANDS
HALO = 24
SPAN = OWN + 2 * HALO
TILE = 128
ROWS = R + 2
MSG = ROWS * OWN // TILE
TOP = 13.0
VMEM_BYTES = 54 * 2**20


ORDER = (2, 1, 3, 0)


def partial_kernel(slot_ref, slab_ref, *refs):
    out_refs, (power_ref, held, edges, select_ref, sems) = refs[:SIDE], refs[SIDE:]
    core = lax.rem(lax.axis_index("plane"), 2)
    me = lax.axis_index("band")
    my_y, my_z = me // SIDE, lax.rem(me, SIDE)

    def band_at(step, other):
        over_y = jnp.where(core == 0, other, step)
        over_z = jnp.where(core == 0, step, other)
        return SIDE * lax.rem(my_y + over_y, SIDE) + lax.rem(my_z + over_z, SIDE)

    def place(band):
        over_y = lax.rem(band // SIDE - my_y + SIDE, SIDE)
        over_z = lax.rem(lax.rem(band, SIDE) - my_z + SIDE, SIDE)
        return jnp.where(core == 0, SIDE * over_z + over_y, SIDE * over_y + over_z)

    def fetch(step, other):
        columns = pl.ds(pl.multiple_of(band_at(step, other) * OWN, OWN), OWN)
        index = SIDE * step + other
        return pltpu.make_async_copy(slab_ref.at[:, :, columns], held.at[index], sems.at[index])

    for step in ORDER:
        for other in range(SIDE):
            fetch(step, other).start()
    lane = lax.broadcasted_iota(jnp.int32, (8, NROW), 1)
    sub = lax.broadcasted_iota(jnp.int32, (8, NROW), 0)
    picks = []
    for pair in range(SLOTS // 2):
        block = jnp.where(sub < BLK, slot_ref[0, 2 * pair], slot_ref[0, 2 * pair + 1])
        row = block * BLK + (sub & (BLK - 1))
        picks.append(jnp.where(lane == row, 1.0, 0.0))
    select_ref[...] = jnp.concatenate(picks, 0).astype(jnp.bfloat16)

    most = jnp.zeros((8, NROW), jnp.float32)
    for step in ORDER:

        def chunk(other, most):
            fetch(step, other).wait()
            slabs = held[SIDE * step + other].reshape(SLOTS * BLK, OWN)
            part = lax.dot_general(
                slabs, select_ref[...], (((0,), (0,)), ((), ())), preferred_element_type=jnp.float32
            )
            out_refs[step][other, 0:OWN] = part
            band = band_at(step, other)
            edges[place(lax.rem(band + 1, BANDS)), 0:HALO] = part[OWN - HALO :]
            edges[place(lax.rem(band + BANDS - 1, BANDS)), HALO:] = part[:HALO]
            return jnp.maximum(most, jnp.max(jnp.abs(part).reshape(OWN // 8, 8, NROW), axis=0))

        most = lax.fori_loop(0, SIDE, chunk, most)
    for step in range(SIDE):
        for other in range(SIDE):
            out_refs[step][other, OWN:] = edges[SIDE * step + other]
    most = jnp.full((8, NROW), jnp.max(most), jnp.float32)
    power_ref[...] = jnp.ceil(jnp.log2(jnp.maximum(most, 2.0**-100)))[0:1]


def partial_densities(slabs, slot_block):
    part = pltpu.VMEM((SIDE, SPAN, NROW), jnp.float32)
    return pl.pallas_call(
        partial_kernel,
        in_specs=[pl.BlockSpec(memory_space=pltpu.SMEM), pl.BlockSpec(memory_space=pl.ANY)],
        out_specs=[pl.BlockSpec(memory_space=pltpu.VMEM)] * (SIDE + 1),
        out_shape=[part] * SIDE + [jax.ShapeDtypeStruct((1, NROW), jnp.float32)],
        scratch_shapes=[
            pltpu.VMEM((BANDS, SLOTS, BLK, OWN), jnp.bfloat16),
            pltpu.VMEM((BANDS, 2 * HALO, NROW), jnp.float32),
            pltpu.VMEM((SLOTS * BLK, NROW), jnp.bfloat16),
            pltpu.SemaphoreType.DMA((BANDS,)),
        ],
        compiler_params=pltpu.CompilerParams(vmem_limit_bytes=VMEM_BYTES),
        name="partial_densities",
    )(slot_block, slabs)


STRIP = 80


def relax_kernel(weight_ref, part_ref, out_ref, density_ref, even_ref, odd_ref, turned_ref):
    zero = jnp.zeros((8, NROW), jnp.float32)
    for ref in (even_ref, odd_ref):
        ref[0:8] = zero
        ref[8 + SPAN :] = zero
    turned_ref[0:8] = zero
    turned_ref[8 + NROW :] = zero
    lane = lax.broadcasted_iota(jnp.int32, (STRIP, NROW), 1)
    not_first = lane > 0
    not_last = lane < NROW - 1
    share = 1.0 / (4.0 + MASS)

    def begin(start, block):
        density_ref[start : start + block.shape[0]] = block
        even_ref[8 + start : 8 + start + block.shape[0]] = block * share

    begin(0, part_ref[OWN : OWN + HALO])
    begin(HALO + OWN, part_ref[OWN + HALO :])
    for tile in range(OWN // TILE):
        begin(HALO + tile * TILE, part_ref[tile * TILE : (tile + 1) * TILE])

    def sweep(src, dst):
        for start in range(8, 8 + SPAN, STRIP):
            here = src[start : start + STRIP]
            total = src[start - 1 : start - 1 + STRIP] + src[start + 1 : start + 1 + STRIP]
            total += jnp.where(not_first, pltpu.roll(here, 1, 1), 0.0)
            total += jnp.where(not_last, pltpu.roll(here, NROW - 1, 1), 0.0)
            total += density_ref[start - 8 : start - 8 + STRIP]
            dst[start : start + STRIP] = total * share

    def two_sweeps(_, carry):
        sweep(even_ref, odd_ref)
        sweep(odd_ref, even_ref)
        return carry

    lax.fori_loop(0, (SWEEPS - 1) // 2, two_sweeps, 0)
    sweep(even_ref, odd_ref)
    weight = weight_ref[0]
    for tile in range(OWN // TILE):
        first = 8 + HALO + tile * TILE
        turned_ref[8 : 8 + NROW] = (odd_ref[first : first + TILE] * weight).T
        for band in range(BANDS):
            out_ref[BANDS - 1 - band, tile * ROWS : (tile + 1) * ROWS] = turned_ref[
                R * band + 7 : R * band + 7 + ROWS
            ]


def relaxed(density, weight):
    return pl.pallas_call(
        relax_kernel,
        in_specs=[
            pl.BlockSpec(memory_space=pltpu.SMEM),
            pl.BlockSpec(memory_space=pltpu.VMEM),
        ],
        out_specs=pl.BlockSpec(memory_space=pltpu.VMEM),
        out_shape=jax.ShapeDtypeStruct((BANDS, MSG, TILE), jnp.float32),
        scratch_shapes=[
            pltpu.VMEM((SPAN, NROW), jnp.float32),
            pltpu.VMEM((SPAN + 16, NROW), jnp.float32),
            pltpu.VMEM((SPAN + 16, NROW), jnp.float32),
            pltpu.VMEM((NROW + 16, TILE), jnp.float32),
        ],
        compiler_params=pltpu.CompilerParams(vmem_limit_bytes=24 * 2**20),
        name="relaxed",
    )(weight, density)


GROUP = OWN // TILE


def plane_maps(ref, starts, is_first, is_last):
    mid, rise, both = [], [], []
    for start in starts:
        south, north = ref[pl.ds(start, R)], ref[pl.ds(start + 2, R)]
        mid.append(ref[pl.ds(start + 1, R)])
        rise.append(north - south)
        both.append(north + south)
    easts = [[pltpu.roll(x, TILE - 1, 1) for x in xs[1:]] for xs in (mid, rise)]
    wests = [[pltpu.roll(x, 1, 1) for x in xs[:-1]] for xs in (mid, rise)]
    maps = []
    for t in range(GROUP):
        east, rise_east = (jnp.where(is_last, e[t + 1], e[t]) for e in easts)
        west, rise_west = (jnp.where(is_first, w[t], w[t + 1]) for w in wests)
        twice = 2.0 * mid[t + 1]
        p11 = 1.0 - (east - twice + west)
        p22 = 1.0 - (both[t + 1] - twice)
        p12 = 0.25 * (rise_west - rise_east)
        maps.append((p11, p12, p22, 0.5 * (east - west), 0.5 * rise[t + 1]))
    return maps


def after_map(state, maps):
    a11, a12, a21, a22, s1, s2 = state
    p11, p12, p22, c1, c2 = maps
    return (
        a11 * p11 + a12 * p12,
        a11 * p12 + a12 * p22,
        a21 * p11 + a22 * p12,
        a21 * p12 + a22 * p22,
        a11 * c1 + a12 * c2 + s1,
        a21 * c1 + a22 * c2 + s2,
    )


def after_state(state, first):
    a11, a12, a21, a22, s1, s2 = state
    b11, b12, b21, b22, t1, t2 = first
    return (
        a11 * b11 + a12 * b21,
        a11 * b12 + a12 * b22,
        a21 * b11 + a22 * b21,
        a21 * b12 + a22 * b22,
        a11 * t1 + a12 * t2 + s1,
        a21 * t1 + a22 * t2 + s2,
    )


def chain_step(state_ref, out_ref, pieces, first_ref=None, last=False):
    lane = lax.broadcasted_iota(jnp.int32, (R, TILE), 1)
    is_first = lane == 0
    is_last = lane == TILE - 1

    def group_body(group, carry):
        here = pl.multiple_of(group * MSG, 8)
        behind = pl.multiple_of(lax.rem(group + 1, BANDS) * MSG, 8)
        ahead = pl.multiple_of(lax.rem(group + BANDS - 1, BANDS) * MSG, 8)
        starts = [behind + MSG - ROWS] + [here + t * ROWS for t in range(GROUP)] + [ahead]
        first = (BANDS - 1 - group) * OWN
        columns = [pl.ds(pl.multiple_of(first + t * TILE, TILE), TILE) for t in range(GROUP)]
        maps = [plane_maps(piece, starts, is_first, is_last) for piece in pieces]
        for t in range(GROUP):
            if state_ref is None:
                p11, p12, p22, c1, c2 = maps[0][t]
                state = (p11, p12, p12, p22, c1, c2)
                rest = maps[1:]
            else:
                state = tuple(state_ref[entry, :, columns[t]] for entry in range(6))
                rest = maps
            for one in rest:
                state = after_map(state, one[t])
            if first_ref is not None:
                state = after_state(state, [first_ref[entry, :, columns[t]] for entry in range(6)])
            if last:
                state = tuple(x - 1.0 if e in (0, 3) else x for e, x in enumerate(state))
            for entry in range(6):
                out_ref[entry, :, columns[t]] = state[entry]
        return carry

    lax.fori_loop(0, BANDS, group_body, 0)


def recent_kernel(back, own_ref, other_ref, one_ref, one_other_ref, out_ref):
    me = lax.axis_index("plane")
    chip, core = me // 2, lax.rem(me, 2)
    for which in (0, 1):
        near = [own_ref, other_ref] if which else [own_ref]
        far = [one_ref, one_other_ref] if which else [one_other_ref, one_ref]

        @pl.when(jnp.logical_and(chip < back, core == which))
        def _():
            chain_step(None, out_ref, near)

        @pl.when(jnp.logical_and(chip >= back, core == which))
        def _():
            chain_step(None, out_ref, near + far)


def first_kernel(back, own_ref, other_ref, out_ref):
    me = lax.axis_index("plane")
    chip, core = me // 2, lax.rem(me, 2)
    for which in (0, 1):
        pieces = [own_ref, other_ref] if which else [other_ref, own_ref]

        @pl.when(jnp.logical_and(chip >= back, core == which))
        def _():
            chain_step(None, out_ref, pieces)


def finish_kernel(back, state_ref, own_ref, other_ref, first_ref, out_ref):
    me = lax.axis_index("plane")
    chip, core = me // 2, lax.rem(me, 2)
    out_ref = out_ref.at[0]

    @pl.when(chip < back)
    def _():
        chain_step(state_ref, out_ref, [], last=True)

    for which in (0, 1):
        pieces = [own_ref, other_ref] if which else [other_ref, own_ref]

        @pl.when(jnp.logical_and(chip == back, core == which))
        def _():
            chain_step(state_ref, out_ref, pieces, last=True)

        @pl.when(jnp.logical_and(chip > back, core == which))
        def _():
            chain_step(state_ref, out_ref, pieces, first_ref, last=True)


def chain_call(kernel, name, operands, shape):
    vmem = pl.BlockSpec(memory_space=pltpu.VMEM)
    return pl.pallas_call(
        kernel,
        in_specs=[vmem] * len(operands),
        out_specs=vmem,
        out_shape=jax.ShapeDtypeStruct(shape, jnp.float32),
        cost_estimate=pl.CostEstimate(
            flops=80 * R * NCOL,
            bytes_accessed=sum(4 * x.size for x in operands) + 24 * R * NCOL,
            transcendentals=0,
        ),
        compiler_params=pltpu.CompilerParams(vmem_limit_bytes=16 * 2**20),
        name=name,
    )(*operands)


def from_chip(block, back):
    return lax.ppermute(block, "plane", [(i, (i + 2 * back) % PLANES) for i in range(PLANES)])


def from_other_core(block):
    return lax.ppermute(block, "plane", [(i, i ^ 1) for i in range(PLANES)])


def along_band(block, steps, first):
    route = []
    for plane in range(PLANES):
        for y in range(SIDE):
            for z in range(SIDE):
                if (plane % 2 == 0) == first:
                    target = SIDE * y + (z + steps) % SIDE
                else:
                    target = SIDE * ((y + steps) % SIDE) + z
                route.append((plane * BANDS + SIDE * y + z, plane * BANDS + target))
    return lax.ppermute(block, ("plane", "band"), route)


def coded(values, power):
    row = lax.broadcasted_iota(jnp.int32, values.shape, values.ndim - 2)
    scaled = values * jnp.exp2(TOP - power)
    return jnp.where(row == OWN, power, scaled).astype(jnp.float16)


def power_of(code):
    return code.reshape(-1, SPAN, NROW)[0, OWN : OWN + 1].astype(jnp.float32)


def decoded(code, factor):
    return code.astype(jnp.float32) * factor


def reduced_density(slabs, slot_block):
    *parts, power = partial_densities(slabs, slot_block)
    codes = {}
    for step, after in ((2, 1), (1, 3), (3, 0)):
        code = coded(parts[step], power)
        code, parts[after] = lax.optimization_barrier((code, parts[after]))
        codes[step] = along_band(code, step, True)
    powers = [power_of(codes[step]) for step in (1, 2, 3)]
    power = functools.reduce(jnp.maximum, powers, power)
    factors = [jnp.exp2(power - TOP) for power in powers]
    sums = {}
    for other in (2, 1, 3, 0):
        total = parts[0][other]
        for step in (1, 2, 3):
            total += decoded(codes[step][other], factors[step - 1])
        sums[other] = total if other == 0 else along_band(coded(total, power), other, False)
    for other in (1, 2, 3):
        total = sums[0]
        factor = jnp.exp2(power_of(sums[other]) - TOP)
        sums[0] = total + decoded(sums[other], factor)
    return sums[0]


def body(slabs, slot_block, lens_weight):
    density = reduced_density(slabs[0], slot_block)
    messages = relaxed(density, lens_weight)
    backwards = [list(range(BANDS))[::-1]]
    rows = lax.all_to_all(
        messages, "band", split_axis=0, concat_axis=0, axis_index_groups=backwards, tiled=True
    )
    rows = rows.reshape(BANDS * MSG, TILE)
    two, one, three = (from_chip(rows, back) for back in (2, 1, 3))
    shape = (6, R, NCOL)
    recent = functools.partial(recent_kernel, 1)
    operands = (rows, from_other_core(rows), one, from_other_core(one))
    recent = chain_call(recent, "chain_recent", operands, shape)
    first = functools.partial(first_kernel, 3)
    first = chain_call(first, "chain_first", (three, from_other_core(three)), shape)
    finish = functools.partial(finish_kernel, 2)
    operands = (recent, two, from_other_core(two), first)
    return chain_call(finish, "chain_finish", operands, (1,) + shape)


def solution(mesh):
    in_specs = (P("plane", "band", None, None), P("plane", "band"), P("plane"))
    out_specs = P("plane", None, "band", None)
    return jax.shard_map(body, mesh=mesh, in_specs=in_specs, out_specs=out_specs, check_vma=False)
```

time: 101 us -> 80 us (0.79)
  Pallas kernels: 25 us -> 18.1 us
  waiting for transfers between devices: 31.6 us -> 25.2 us
  starting transfers between devices: 26.5 us -> 22.6 us
  local copies, waits for them, and re-layouts: 3.36 us -> 0.01 us
    all_to_all x1 -> x0, waiting for transfers between devices: 30.2 us -> none  [body(): got = lax.all_to_all(sent, 'band', split_axis=0, concat_axis=0, tiled=True)]
    ppermute x0 -> x6, waiting for transfers between devices: none -> 18.7 us  [along_band(): return lax.ppermute(block, ('plane', 'band'), route)]
    ppermute x0 -> x6, starting transfers between devices: none -> 9.36 us  [along_band(): return lax.ppermute(block, ('plane', 'band'), route)]
    all_to_all x1 -> x0, starting transfers between devices: 7.77 us -> none  [body(): got = lax.all_to_all(sent, 'band', split_axis=0, concat_axis=0, tiled=True)]
    pallas_call x2 -> x4, Pallas kernels: 21.4 us -> 14.5 us  [the longest x3 7.67 us: chain_call(): pl.pallas_call(kernel, in_specs=[vmem] * len(operands), out_specs=vmem, o...]
    ppermute x4, starting transfers between devices: 16.4 us -> 10.6 us  [from_other_core(): return lax.ppermute(block, 'plane', [(i, i ^ 1) for i in range(PLANES)])]
    ppermute x3, waiting for transfers between devices: 0.14 us -> 5.83 us  [from_chip(): lax.ppermute(block, 'plane', [(i, (i + 2 * back) % PLANES) for i in range...]
    unnamed x4 -> x2, local copies, waits for them, and re-layouts: 2.84 us -> 0.01 us
  transfers between devices with their start and end apart: 8 -> 13, of which waited for: 3 -> 7; matrix products, arithmetic and copies ran while one was open for 0% -> 0% of each run, Pallas kernels for 0% -> 6%
where the time goes in v2:
time: 80 us; the launch traced here: 79.8 us
  waiting for transfers between devices  25.2 us (32%)
  starting transfers between devices  22.6 us (28%)
  Pallas kernels  18.1 us (23%)
  blocking collectives  10.5 us (13%)
  other arithmetic  2.62 us (3%)
    ppermute x6, waiting for transfers between devices, along_band(): return lax.ppermute(block, ('plane', 'band'), route)  18.7 us
    ppermute x4, starting transfers between devices, from_other_core(): return lax.ppermute(block, 'plane', [(i, i ^ 1) for i in range(PLANES)])  10.6 us
    all_to_all x1, blocking collectives, body(): lax.all_to_all(messages, 'band', split_axis=0, concat_axis=0, axis_index_...  10.5 us
    ppermute x6, starting transfers between devices, along_band(): return lax.ppermute(block, ('plane', 'band'), route)  9.36 us
    pallas_call x3, Pallas kernels, chain_call(): pl.pallas_call(kernel, in_specs=[vmem] * len(operands), out_specs=vmem, o...  7.67 us
    pallas_call x1, Pallas kernels, partial_densities(): pl.pallas_call(partial_kernel, in_specs=[pl.BlockSpec(memory_space=pltpu....  6.79 us
    ppermute x3, waiting for transfers between devices, from_chip(): lax.ppermute(block, 'plane', [(i, (i + 2 * back) % PLANES) for i in range...  5.83 us
    pallas_call x1, Pallas kernels, relaxed(): pl.pallas_call(relax_kernel, in_specs=[pl.BlockSpec(memory_space=pltpu.SM...  3.65 us
  transfers between devices with their start and end apart: 13, of which 7 were waited for; matrix products, arithmetic and copies ran while one was open for 0% of the time, Pallas kernels for 6%

profile of v2, /device:TPU:7, one launch (start us, length us, event | category | flops | bytes accessed | tf_op | source)
XLA Modules:
  0.0 79.8 jit_solution(10241031014787044463)
XLA Ops:
  0.0 6.8 %partial_densities.1 = (f32[4,560,128]{2,1,0:T(8,128)S(1)}, f32[4,560,128]{2,1,0:T(8,128)S(1)}, f32[4,560,128]{2,1,0:T(8,128)S(1)}, f32[4,560,128]{2,1,0:T(8,128)S(1)}, f32[1,128]{1,0:T(1,128)}) custom-call(s32[1,64]{1,0:T(1,128)} %slot_ref.1, bf16[64,4,8192]{2,1,0:T(4,128)(2,1)} %bitcast.109), custom_call_target="tpu_custom_call" | custom-call | tf_op jit(solution)/shard_map/partial_densities/pallas_call | solution.py:92
  6.8 0.7 exponential_bitcast_fusion.4
  7.5 0.9 %select_convert_fusion.2 = f16[4,560,128]{2,1,0:T(8,128)(2,1)S(1)} fusion(f32[4,560,128]{2,1,0:T(8,128)S(1)} %get-tuple-element.17, f32[128]{0:T(128)S(1)} %exponential_bitcast_fusion.4, f32[128]{0:T(128)} %bitcast.113, pred[560]{0:T(1024)(128)(4,1)S(1)} %iota_compare_fusion), kind=kLoop, calls=%fused_computation.2 | loop fusion | flops 860160 | bytes 1721904 | tf_op jit(solution)/shard_map/convert_element_type | solution.py:351
  8.8 2.8 %collective-permute-start.2 = (f16[4,560,128]{2,1,0:T(8,128)(2,1)S(1)}, f16[4,560,128]{2,1,0:T(8,128)(2,1)S(1)}, u32[]{:S(2)}, u32[]{:S(2)}) collective-permute-start(f16[4,560,128]{2,1,0:T(8,128)(2,1)S(1)} %select_convert_fusion), channel_id=1, source_target_pairs={{0,3},{1,0},{2,1},{3,2},{4,7},{5,4},{6,5},{7,6},{8,11},{9,8},{10,9... | collective-permute-start | bytes 1720328 | tf_op jit(solution)/shard_map/ppermute | solution.py:345
  11.6 1.6 %collective-permute-start.1 = (f16[4,560,128]{2,1,0:T(8,128)(2,1)S(1)}, f16[4,560,128]{2,1,0:T(8,128)(2,1)S(1)}, u32[]{:S(2)}, u32[]{:S(2)}) collective-permute-start(f16[4,560,128]{2,1,0:T(8,128)(2,1)S(1)} %select_convert_fusion.2), channel_id=1, source_target_pairs={{0,2},{1,3},{2,0},{3,1},{4,6},{5,7},{6,4},{7,5},{8,10},{9,11},{10,... | collective-permute-start | bytes 1720328 | tf_op jit(solution)/shard_map/ppermute | solution.py:345
  13.3 11.2 %collective-permute-done.2 = f16[4,560,128]{2,1,0:T(8,128)(2,1)S(1)} collective-permute-done((f16[4,560,128]{2,1,0:T(8,128)(2,1)S(1)}, f16[4,560,128]{2,1,0:T(8,128)(2,1)S(1)}, u32[]{:S(2)}, u32[]{:S(2)}) %collective-permute-start.2) | collective-permute-done | bytes 573472 | tf_op jit(solution)/shard_map/ppermute | solution.py:345
  24.4 3.4 %collective-permute-done = f16[4,560,128]{2,1,0:T(8,128)(2,1)S(1)} collective-permute-done((f16[4,560,128]{2,1,0:T(8,128)(2,1)S(1)}, f16[4,560,128]{2,1,0:T(8,128)(2,1)S(1)}, u32[]{:S(2)}, u32[]{:S(2)}) %collective-permute-start) | collective-permute-done | bytes 573472 | tf_op jit(solution)/shard_map/ppermute | solution.py:345
  27.9 0.4 fusion.15
  28.3 1.4 %collective-permute-start.3 = (f16[560,128]{1,0:T(8,128)(2,1)S(1)}, f16[560,128]{1,0:T(8,128)(2,1)S(1)}, u32[]{:S(2)}, u32[]{:S(2)}) collective-permute-start(f16[560,128]{1,0:T(8,128)(2,1)S(1)} %get-tuple-element.29), channel_id=1, source_target_pairs={{0,4},{1,5},{2,6},{3,7},{4,8},{5,9},{6,10},{7,11},{8,12},{9,13},{1... | collective-permute-start | bytes 430088 | tf_op jit(solution)/shard_map/ppermute | solution.py:345
  30.4 2.2 %collective-permute-start.5 = (f16[560,128]{1,0:T(8,128)(2,1)S(1)}, f16[560,128]{1,0:T(8,128)(2,1)S(1)}, u32[]{:S(2)}, u32[]{:S(2)}) collective-permute-start(f16[560,128]{1,0:T(8,128)(2,1)S(1)} %get-tuple-element.30), channel_id=1, source_target_pairs={{0,12},{1,13},{2,14},{3,15},{4,0},{5,1},{6,2},{7,3},{8,4},{9,5},{1... | collective-permute-start | bytes 430088 | tf_op jit(solution)/shard_map/ppermute | solution.py:345
  32.6 1.3 %collective-permute-start.4 = (f16[560,128]{1,0:T(8,128)(2,1)S(1)}, f16[560,128]{1,0:T(8,128)(2,1)S(1)}, u32[]{:S(2)}, u32[]{:S(2)}) collective-permute-start(f16[560,128]{1,0:T(8,128)(2,1)S(1)} %get-tuple-element.31), channel_id=1, source_target_pairs={{0,8},{1,9},{2,10},{3,11},{4,12},{5,13},{6,14},{7,15},{8,0},{9,1},... | collective-permute-start | bytes 430088 | tf_op jit(solution)/shard_map/ppermute | solution.py:345
  33.9 0.5 collective-permute-done.3
  34.6 3.4 %collective-permute-done.4 = f16[560,128]{1,0:T(8,128)(2,1)S(1)} collective-permute-done((f16[560,128]{1,0:T(8,128)(2,1)S(1)}, f16[560,128]{1,0:T(8,128)(2,1)S(1)}, u32[]{:S(2)}, u32[]{:S(2)}) %collective-permute-start.4) | collective-permute-done | bytes 143392 | tf_op jit(solution)/shard_map/ppermute | solution.py:345
  38.2 3.6 %relaxed.1 = f32[16,40,128]{2,1,0:T(8,128)S(1)} custom-call(f32[1]{0:T(128)S(6)} %copy.4.weight_ref, f32[560,128]{1,0:T(8,128)S(1)} %fusion.21.part_ref), custom_call_target="tpu_custom_call" | custom-call | tf_op jit(solution)/shard_map/relaxed/pallas_call | solution.py:159
  41.9 10.5 %all_to_all.5 = f32[16,40,128]{2,1,0:T(8,128)S(1)} all-to-all(f32[16,40,128]{2,1,0:T(8,128)S(1)} %relaxed.1), channel_id=1, replica_groups={{15,14,13,12,11,10,9,8,7,6,5,4,3,2,1,0},{31,30,29,28,27,26,25,24,23,22,..., dimensions={0} | all-to-all | bytes 655360 | tf_op jit(solution)/shard_map/all_to_all | solution.py:389
  52.3 0.6 collective-permute-start.11
  52.9 2.1 %collective-permute-start.7 = (f32[640,128]{1,0:T(8,128)S(1)}, f32[640,128]{1,0:T(8,128)S(1)}, u32[]{:S(2)}, u32[]{:S(2)}) collective-permute-start(f32[640,128]{1,0:T(8,128)S(1)} %bitcast.105), channel_id=1, source_target_pairs={{0,32},{16,48},{32,64},{48,80},{64,96},{80,112},{96,0},{112,16},{1... | collective-permute-start | bytes 983048 | tf_op jit(solution)/shard_map/ppermute | solution.py:328
  55.0 5.8 %collective-permute-done.11.own_ref = f32[640,128]{1,0:T(8,128)S(1)} collective-permute-done((f32[640,128]{1,0:T(8,128)S(1)}, f32[640,128]{1,0:T(8,128)S(1)}, u32[]{:S(2)}, u32[]{:S(2)}) %collective-permute-start.11) | collective-permute-done | bytes 327712 | tf_op jit(solution)/shard_map/ppermute | solution.py:328
  60.8 10.0 %collective-permute-start.12 = (f32[640,128]{1,0:T(8,128)S(1)}, f32[640,128]{1,0:T(8,128)S(1)}, u32[]{:S(2)}, u32[]{:S(2)}) collective-permute-start(f32[640,128]{1,0:T(8,128)S(1)} %collective-permute-done.11.own_ref), channel_id=1, source_target_pairs={{0,16},{16,0},{32,48},{48,32},{64,80},{80,64},{96,112},{112,96},{1... | collective-permute-start | bytes 983048 | tf_op jit(solution)/shard_map/ppermute | solution.py:332
  70.8 0.5 collective-permute-start.8
  71.4 0.7 collective-permute-done.12.other_ref
  72.1 1.8 %chain_first.1.first_ref = f32[6,8,8192]{2,1,0:T(8,128)S(1)} custom-call(f32[640,128]{1,0:T(8,128)S(1)} %collective-permute-done.11.own_ref, f32[640,128]{1,0:T(8,128)S(1)} %collective-permute-done.12.other_ref), custom_call_target="tpu_custom_call" | custom-call | flops 5242880 | bytes 2228224 | tf_op jit(solution)/shard_map/chain_first/pallas_call | solution.py:312
  74.0 2.6 %chain_recent.1.state_ref = f32[6,8,8192]{2,1,0:T(8,128)S(1)} custom-call(f32[640,128]{1,0:T(8,128)S(1)} %bitcast.108, f32[640,128]{1,0:T(8,128)S(1)} %collective-permute-done.6.other_ref, f32[640,128]{1,0:T(8,128)S(1)} %collective-permute-done.7.one_ref, f32[640,128]{1,0:T(8,128)S(1)} %collective-permute-done.8.one_other_ref), custom_call_target="tpu_custom_call" | custom-call | flops 5242880 | bytes 2883584 | tf_op jit(solution)/shard_map/chain_recent/pallas_call | solution.py:312
  76.6 3.2 %chain_finish.1 = f32[1,6,8,8192]{3,2,1,0:T(8,128)} custom-call(f32[6,8,8192]{2,1,0:T(8,128)S(1)} %chain_recent.1.state_ref, f32[640,128]{1,0:T(8,128)S(1)} %collective-permute-done.9.own_ref, f32[640,128]{1,0:T(8,128)S(1)} %collective-permute-done.10.other_ref, f32[6,8,8192]{2,1,0:T(8,128)S(1)} %chain_first.1.first_ref), custom_call_target="tpu_custom_call" | custom-call | flops 5242880 | bytes 5373952 | tf_op jit(solution)/shard_map/chain_finish/pallas_call | solution.py:312
  (24 shorter events, 1.1 us)
Async XLA Ops:
  6.8 1.6 %copy-start = (f32[1,128]{1,0:T(1,128)S(1)}, f32[1,128]{1,0:T(1,128)}, u32[]{:S(2)}) copy-start(f32[1,128]{1,0:T(1,128)} %get-tuple-element.16) | copy-start | bytes 1540
  8.8 15.6 %collective-permute-start.2 = (f16[4,560,128]{2,1,0:T(8,128)(2,1)S(1)}, f16[4,560,128]{2,1,0:T(8,128)(2,1)S(1)}, u32[]{:S(2)}, u32[]{:S(2)}) collective-permute-start(f16[4,560,128]{2,1,0:T(8,128)(2,1)S(1)} %select_convert_fusion), channel_id=1, source_target_pairs={{0,3},{1,0},{2,1},{3,2},{4,7},{5,4},{6,5},{7,6},{8,11},{9,8},{10,9... | collective-permute-start | bytes 1720328 | tf_op jit(solution)/shard_map/ppermute | solution.py:345
  11.6 16.2 %collective-permute-start = (f16[4,560,128]{2,1,0:T(8,128)(2,1)S(1)}, f16[4,560,128]{2,1,0:T(8,128)(2,1)S(1)}, u32[]{:S(2)}, u32[]{:S(2)}) collective-permute-start(f16[4,560,128]{2,1,0:T(8,128)(2,1)S(1)} %select_convert_fusion.1), channel_id=1, source_target_pairs={{0,1},{1,2},{2,3},{3,0},{4,5},{5,6},{6,7},{7,4},{8,9},{9,10},{10,1... | collective-permute-start | bytes 1720328 | tf_op jit(solution)/shard_map/ppermute | solution.py:345
  11.6 16.2 %collective-permute-start.1 = (f16[4,560,128]{2,1,0:T(8,128)(2,1)S(1)}, f16[4,560,128]{2,1,0:T(8,128)(2,1)S(1)}, u32[]{:S(2)}, u32[]{:S(2)}) collective-permute-start(f16[4,560,128]{2,1,0:T(8,128)(2,1)S(1)} %select_convert_fusion.2), channel_id=1, source_target_pairs={{0,2},{1,3},{2,0},{3,1},{4,6},{5,7},{6,4},{7,5},{8,10},{9,11},{10,... | collective-permute-start | bytes 1720328 | tf_op jit(solution)/shard_map/ppermute | solution.py:345
  28.3 6.0 %collective-permute-start.3 = (f16[560,128]{1,0:T(8,128)(2,1)S(1)}, f16[560,128]{1,0:T(8,128)(2,1)S(1)}, u32[]{:S(2)}, u32[]{:S(2)}) collective-permute-start(f16[560,128]{1,0:T(8,128)(2,1)S(1)} %get-tuple-element.29), channel_id=1, source_target_pairs={{0,4},{1,5},{2,6},{3,7},{4,8},{5,9},{6,10},{7,11},{8,12},{9,13},{1... | collective-permute-start | bytes 430088 | tf_op jit(solution)/shard_map/ppermute | solution.py:345
  30.4 4.3 %collective-permute-start.5 = (f16[560,128]{1,0:T(8,128)(2,1)S(1)}, f16[560,128]{1,0:T(8,128)(2,1)S(1)}, u32[]{:S(2)}, u32[]{:S(2)}) collective-permute-start(f16[560,128]{1,0:T(8,128)(2,1)S(1)} %get-tuple-element.30), channel_id=1, source_target_pairs={{0,12},{1,13},{2,14},{3,15},{4,0},{5,1},{6,2},{7,3},{8,4},{9,5},{1... | collective-permute-start | bytes 430088 | tf_op jit(solution)/shard_map/ppermute | solution.py:345
  32.6 5.5 %collective-permute-start.4 = (f16[560,128]{1,0:T(8,128)(2,1)S(1)}, f16[560,128]{1,0:T(8,128)(2,1)S(1)}, u32[]{:S(2)}, u32[]{:S(2)}) collective-permute-start(f16[560,128]{1,0:T(8,128)(2,1)S(1)} %get-tuple-element.31), channel_id=1, source_target_pairs={{0,8},{1,9},{2,10},{3,11},{4,12},{5,13},{6,14},{7,15},{8,0},{9,1},... | collective-permute-start | bytes 430088 | tf_op jit(solution)/shard_map/ppermute | solution.py:345
  52.3 8.5 %collective-permute-start.11 = (f32[640,128]{1,0:T(8,128)S(1)}, f32[640,128]{1,0:T(8,128)S(1)}, u32[]{:S(2)}, u32[]{:S(2)}) collective-permute-start(f32[640,128]{1,0:T(8,128)S(1)} %bitcast.104), channel_id=1, source_target_pairs={{0,96},{16,112},{32,0},{48,16},{64,32},{80,48},{96,64},{112,80},{1... | collective-permute-start | bytes 983048 | tf_op jit(solution)/shard_map/ppermute | solution.py:328
  52.9 17.9 %collective-permute-start.7 = (f32[640,128]{1,0:T(8,128)S(1)}, f32[640,128]{1,0:T(8,128)S(1)}, u32[]{:S(2)}, u32[]{:S(2)}) collective-permute-start(f32[640,128]{1,0:T(8,128)S(1)} %bitcast.105), channel_id=1, source_target_pairs={{0,32},{16,48},{32,64},{48,80},{64,96},{80,112},{96,0},{112,16},{1... | collective-permute-start | bytes 983048 | tf_op jit(solution)/shard_map/ppermute | solution.py:328
  55.0 16.3 %collective-permute-start.9 = (f32[640,128]{1,0:T(8,128)S(1)}, f32[640,128]{1,0:T(8,128)S(1)}, u32[]{:S(2)}, u32[]{:S(2)}) collective-permute-start(f32[640,128]{1,0:T(8,128)S(1)} %bitcast.106), channel_id=1, source_target_pairs={{0,64},{16,80},{32,96},{48,112},{64,0},{80,16},{96,32},{112,48},{1... | collective-permute-start | bytes 983048 | tf_op jit(solution)/shard_map/ppermute | solution.py:328
  60.8 11.2 %collective-permute-start.12 = (f32[640,128]{1,0:T(8,128)S(1)}, f32[640,128]{1,0:T(8,128)S(1)}, u32[]{:S(2)}, u32[]{:S(2)}) collective-permute-start(f32[640,128]{1,0:T(8,128)S(1)} %collective-permute-done.11.own_ref), channel_id=1, source_target_pairs={{0,16},{16,0},{32,48},{48,32},{64,80},{80,64},{96,112},{112,96},{1... | collective-permute-start | bytes 983048 | tf_op jit(solution)/shard_map/ppermute | solution.py:332
  70.8 3.1 %collective-permute-start.6 = (f32[640,128]{1,0:T(8,128)S(1)}, f32[640,128]{1,0:T(8,128)S(1)}, u32[]{:S(2)}, u32[]{:S(2)}) collective-permute-start(f32[640,128]{1,0:T(8,128)S(1)} %bitcast.107), channel_id=1, source_target_pairs={{0,16},{16,0},{32,48},{48,32},{64,80},{80,64},{96,112},{112,96},{1... | collective-permute-start | bytes 983048 | tf_op jit(solution)/shard_map/ppermute | solution.py:332
  70.8 3.1 %collective-permute-start.8 = (f32[640,128]{1,0:T(8,128)S(1)}, f32[640,128]{1,0:T(8,128)S(1)}, u32[]{:S(2)}, u32[]{:S(2)}) collective-permute-start(f32[640,128]{1,0:T(8,128)S(1)} %collective-permute-done.7.one_ref), channel_id=1, source_target_pairs={{0,16},{16,0},{32,48},{48,32},{64,80},{80,64},{96,112},{112,96},{1... | collective-permute-start | bytes 983048 | tf_op jit(solution)/shard_map/ppermute | solution.py:332
  71.3 5.2 %collective-permute-start.10 = (f32[640,128]{1,0:T(8,128)S(1)}, f32[640,128]{1,0:T(8,128)S(1)}, u32[]{:S(2)}, u32[]{:S(2)}) collective-permute-start(f32[640,128]{1,0:T(8,128)S(1)} %collective-permute-done.9.own_ref), channel_id=1, source_target_pairs={{0,16},{16,0},{32,48},{48,32},{64,80},{80,64},{96,112},{112,96},{1... | collective-permute-start | bytes 983048 | tf_op jit(solution)/shard_map/ppermute | solution.py:332

commit v3 on v2

--- a/solution.py
+++ b/solution.py
@@ -28,33 +28,34 @@
 VMEM_BYTES = 54 * 2**20
 
 
-ORDER = (2, 1, 3, 0)
-
-
-def partial_kernel(slot_ref, slab_ref, *refs):
-    out_refs, (power_ref, held, edges, select_ref, sems) = refs[:SIDE], refs[SIDE:]
-    core = lax.rem(lax.axis_index("plane"), 2)
-    me = lax.axis_index("band")
-    my_y, my_z = me // SIDE, lax.rem(me, SIDE)
-
-    def band_at(step, other):
-        over_y = jnp.where(core == 0, other, step)
-        over_z = jnp.where(core == 0, step, other)
-        return SIDE * lax.rem(my_y + over_y, SIDE) + lax.rem(my_z + over_z, SIDE)
-
-    def place(band):
-        over_y = lax.rem(band // SIDE - my_y + SIDE, SIDE)
-        over_z = lax.rem(lax.rem(band, SIDE) - my_z + SIDE, SIDE)
-        return jnp.where(core == 0, SIDE * over_z + over_y, SIDE * over_y + over_z)
-
-    def fetch(step, other):
-        columns = pl.ds(pl.multiple_of(band_at(step, other) * OWN, OWN), OWN)
-        index = SIDE * step + other
-        return pltpu.make_async_copy(slab_ref.at[:, :, columns], held.at[index], sems.at[index])
-
-    for step in ORDER:
-        for other in range(SIDE):
-            fetch(step, other).start()
+FAR, NEAR = 2, (1, 3, 0)
+ORDER = (1, 3, 2, 0)
+
+
+class Relay:
+    def __init__(self):
+        self.core = lax.rem(lax.axis_index("plane"), 2)
+        self.me = lax.axis_index("band")
+
+    def band_at(self, step, other):
+        over_y = jnp.where(self.core == 0, other, step)
+        over_z = jnp.where(self.core == 0, step, other)
+        return self.me ^ (SIDE * over_y + over_z)
+
+    def place(self, band):
+        over_y, over_z = (self.me ^ band) // SIDE, (self.me ^ band) % SIDE
+        return jnp.where(self.core == 0, SIDE * over_z + over_y, SIDE * over_y + over_z)
+
+
+def before(band):
+    return lax.rem(band + BANDS - 1, BANDS)
+
+
+def after(band):
+    return lax.rem(band + 1, BANDS)
+
+
+def fill_select(slot_ref, select_ref, turned_ref):
     lane = lax.broadcasted_iota(jnp.int32, (8, NROW), 1)
     sub = lax.broadcasted_iota(jnp.int32, (8, NROW), 0)
     picks = []
@@ -62,81 +63,203 @@
         block = jnp.where(sub < BLK, slot_ref[0, 2 * pair], slot_ref[0, 2 * pair + 1])
         row = block * BLK + (sub & (BLK - 1))
         picks.append(jnp.where(lane == row, 1.0, 0.0))
-    select_ref[...] = jnp.concatenate(picks, 0).astype(jnp.bfloat16)
+    select = jnp.concatenate(picks, 0)
+    select_ref[...] = select.astype(jnp.bfloat16)
+    turned_ref[...] = select.T.astype(jnp.bfloat16)
+
+
+def summed_turned(slabs, select_ref):
+    return lax.dot_general(
+        slabs, select_ref[...], (((0,), (0,)), ((), ())), preferred_element_type=jnp.float32
+    )
+
+
+def summed(slabs, turned_ref):
+    return jnp.dot(turned_ref[...], slabs, preferred_element_type=jnp.float32)
+
+
+def larger(most, part):
+    return jnp.maximum(most, jnp.max(jnp.abs(part).reshape(-1, 8, NROW), axis=0))
+
+
+def outer_tiles(slabs):
+    return jnp.concatenate([slabs[:, :TILE], slabs[:, -TILE:]], axis=1)
+
+
+def store_part(out_ref, other, slabs, select_ref, turned_ref, most):
+    outer = summed_turned(outer_tiles(slabs), select_ref)
+    out_ref[other, 0:TILE] = outer[:TILE]
+    out_ref[other, OWN - TILE : OWN] = outer[TILE:]
+    inner = summed(slabs[:, TILE : OWN - TILE], turned_ref)
+    for tile in range(1, OWN // TILE - 1):
+        part = inner[:, (tile - 1) * TILE : tile * TILE]
+        out_ref[other, tile * TILE : (tile + 1) * TILE] = part
+        most = larger(most, part)
+    return outer[:HALO], outer[2 * TILE - HALO :], larger(most, outer)
+
+
+def power_above(most):
+    most = jnp.full((8, NROW), jnp.max(most), jnp.float32)
+    return jnp.ceil(jnp.log2(jnp.maximum(most, 2.0**-100)))[0:1]
+
+
+def far_kernel(slot_ref, slab_ref, out_ref, edges_ref, power_ref, held, select_ref, turned_ref, sems):
+    relay = Relay()
+
+    def fetches(other):
+        band = relay.band_at(FAR, other)
+        pieces = [
+            (before(band) * OWN + OWN - TILE, TILE, 0),
+            (band * OWN, OWN, TILE),
+            (after(band) * OWN, TILE, TILE + OWN),
+        ]
+        return [
+            pltpu.make_async_copy(
+                slab_ref.at[:, :, pl.ds(pl.multiple_of(first, TILE), width)],
+                held.at[other, :, :, pl.ds(to, width)],
+                sems.at[other, piece],
+            )
+            for piece, (first, width, to) in enumerate(pieces)
+        ]
+
+    for other in range(SIDE):
+        for copy in fetches(other):
+            copy.start()
+    fill_select(slot_ref, select_ref, turned_ref)
+
+    def chunk(other, most):
+        for copy in fetches(other):
+            copy.wait()
+        band = relay.band_at(FAR, other)
+        slabs = held[other].reshape(SLOTS * BLK, OWN + 2 * TILE)
+        low, high, most = store_part(
+            out_ref, other, slabs[:, TILE : TILE + OWN], select_ref, turned_ref, most
+        )
+        edges_ref[relay.place(after(band)), 0:HALO] = high
+        edges_ref[relay.place(before(band)), HALO:] = low
+        outer = summed_turned(outer_tiles(slabs), select_ref)
+        left, right = outer[TILE - HALO : TILE], outer[TILE : TILE + HALO]
+        out_ref[other, OWN : OWN + HALO] = left
+        out_ref[other, OWN + HALO :] = right
+        return larger(larger(most, left), right)
+
+    most = lax.fori_loop(0, SIDE, chunk, jnp.zeros((8, NROW), jnp.float32))
+    power_ref[...] = power_above(most)
+
+
+def near_kernel(slot_ref, slab_ref, far_edges_ref, *refs):
+    out_refs, refs = refs[: len(NEAR)], refs[len(NEAR) :]
+    power_ref, held, edges, select_ref, turned_ref, sems = refs
+    relay = Relay()
+
+    def band_of(slot):
+        step = jnp.where(slot < SIDE, NEAR[0], jnp.where(slot < 2 * SIDE, NEAR[1], NEAR[2]))
+        return relay.band_at(step, lax.rem(slot, SIDE))
+
+    def fetch(slot):
+        columns = pl.ds(pl.multiple_of(band_of(slot) * OWN, OWN), OWN)
+        return pltpu.make_async_copy(slab_ref.at[:, :, columns], held.at[slot], sems.at[slot])
+
+    for slot in range(len(NEAR) * SIDE):
+        fetch(slot).start()
+    fill_select(slot_ref, select_ref, turned_ref)
+    edges[...] = far_edges_ref[...]
+
+    def chunks(index, most):
+        def chunk(other, most):
+            slot = SIDE * index + other
+            fetch(slot).wait()
+            slabs = held[slot].reshape(SLOTS * BLK, OWN)
+            low, high, most = store_part(
+                out_refs[index], other, slabs, select_ref, turned_ref, most
+            )
+            edges[relay.place(after(band_of(slot))), 0:HALO] = high
+            edges[relay.place(before(band_of(slot))), HALO:] = low
+            return most
+
+        return lax.fori_loop(0, SIDE, chunk, most)
 
     most = jnp.zeros((8, NROW), jnp.float32)
-    for step in ORDER:
-
-        def chunk(other, most):
-            fetch(step, other).wait()
-            slabs = held[SIDE * step + other].reshape(SLOTS * BLK, OWN)
-            part = lax.dot_general(
-                slabs, select_ref[...], (((0,), (0,)), ((), ())), preferred_element_type=jnp.float32
-            )
-            out_refs[step][other, 0:OWN] = part
-            band = band_at(step, other)
-            edges[place(lax.rem(band + 1, BANDS)), 0:HALO] = part[OWN - HALO :]
-            edges[place(lax.rem(band + BANDS - 1, BANDS)), HALO:] = part[:HALO]
-            return jnp.maximum(most, jnp.max(jnp.abs(part).reshape(OWN // 8, 8, NROW), axis=0))
-
-        most = lax.fori_loop(0, SIDE, chunk, most)
-    for step in range(SIDE):
+    for index in range(len(NEAR)):
+        most = chunks(index, most)
+    for index, step in enumerate(NEAR):
         for other in range(SIDE):
-            out_refs[step][other, OWN:] = edges[SIDE * step + other]
-    most = jnp.full((8, NROW), jnp.max(most), jnp.float32)
-    power_ref[...] = jnp.ceil(jnp.log2(jnp.maximum(most, 2.0**-100)))[0:1]
-
-
-def partial_densities(slabs, slot_block):
-    part = pltpu.VMEM((SIDE, SPAN, NROW), jnp.float32)
+            block = edges[SIDE * step + other]
+            out_refs[index][other, OWN:] = block
+            most = larger(most, block)
+    power_ref[...] = power_above(most)
+
+
+def sum_call(kernel, name, operands, parts, more, held, sems):
+    vmem = pl.BlockSpec(memory_space=pltpu.VMEM)
     return pl.pallas_call(
-        partial_kernel,
-        in_specs=[pl.BlockSpec(memory_space=pltpu.SMEM), pl.BlockSpec(memory_space=pl.ANY)],
-        out_specs=[pl.BlockSpec(memory_space=pltpu.VMEM)] * (SIDE + 1),
-        out_shape=[part] * SIDE + [jax.ShapeDtypeStruct((1, NROW), jnp.float32)],
-        scratch_shapes=[
-            pltpu.VMEM((BANDS, SLOTS, BLK, OWN), jnp.bfloat16),
-            pltpu.VMEM((BANDS, 2 * HALO, NROW), jnp.float32),
+        kernel,
+        in_specs=[pl.BlockSpec(memory_space=pltpu.SMEM), pl.BlockSpec(memory_space=pl.ANY)]
+        + [vmem] * (len(operands) - 2),
+        out_specs=[vmem] * (parts + len(more)),
+        out_shape=[pltpu.VMEM((SIDE, SPAN, NROW), jnp.float32)] * parts + more,
+        scratch_shapes=held
+        + [
             pltpu.VMEM((SLOTS * BLK, NROW), jnp.bfloat16),
-            pltpu.SemaphoreType.DMA((BANDS,)),
+            pltpu.VMEM((NROW, SLOTS * BLK), jnp.bfloat16),
+            pltpu.SemaphoreType.DMA(sems),
         ],
         compiler_params=pltpu.CompilerParams(vmem_limit_bytes=VMEM_BYTES),
-        name="partial_densities",
-    )(slot_block, slabs)
-
-
-STRIP = 80
-
-
-def relax_kernel(weight_ref, part_ref, out_ref, density_ref, even_ref, odd_ref, turned_ref):
+        name=name,
+    )(*operands)
+
+
+POWER = pltpu.VMEM((1, NROW), jnp.float32)
+EDGES = pltpu.VMEM((BANDS, 2 * HALO, NROW), jnp.float32)
+
+
+def far_sums(slabs, slot_block):
+    held = pltpu.VMEM((SIDE, SLOTS, BLK, OWN + 2 * TILE), jnp.bfloat16)
+    operands = (slot_block, slabs)
+    return sum_call(far_kernel, "far_sums", operands, 1, [EDGES, POWER], [held], (SIDE, 3))
+
+
+def near_sums(slabs, slot_block, edges):
+    count = SIDE * len(NEAR)
+    held = pltpu.VMEM((count, SLOTS, BLK, OWN), jnp.bfloat16)
+    operands = (slot_block, slabs, edges)
+    return sum_call(near_kernel, "near_sums", operands, 3, [POWER], [held, EDGES], (count,))
+
+
+STEPS = SPAN // 8
+
+
+def relax_kernel(weight_ref, part_ref, out_ref, plain_ref, density_ref, even_ref, odd_ref, turned_ref):
     zero = jnp.zeros((8, NROW), jnp.float32)
-    for ref in (even_ref, odd_ref):
-        ref[0:8] = zero
-        ref[8 + SPAN :] = zero
     turned_ref[0:8] = zero
     turned_ref[8 + NROW :] = zero
-    lane = lax.broadcasted_iota(jnp.int32, (STRIP, NROW), 1)
+    lane = lax.broadcasted_iota(jnp.int32, (8, NROW), 1)
     not_first = lane > 0
     not_last = lane < NROW - 1
     share = 1.0 / (4.0 + MASS)
 
-    def begin(start, block):
-        density_ref[start : start + block.shape[0]] = block
-        even_ref[8 + start : 8 + start + block.shape[0]] = block * share
-
-    begin(0, part_ref[OWN : OWN + HALO])
-    begin(HALO + OWN, part_ref[OWN + HALO :])
+    plain_ref[0:HALO] = part_ref[OWN : OWN + HALO]
+    plain_ref[HALO + OWN :] = part_ref[OWN + HALO :]
     for tile in range(OWN // TILE):
-        begin(HALO + tile * TILE, part_ref[tile * TILE : (tile + 1) * TILE])
+        part = part_ref[tile * TILE : (tile + 1) * TILE]
+        part = part if tile in (0, OWN // TILE - 1) else part.T
+        plain_ref[HALO + tile * TILE : HALO + (tile + 1) * TILE] = part
+
+    for t in range(STEPS):
+        block = plain_ref[pl.ds(t, 8, stride=STEPS)]
+        density_ref[8 * t : 8 * t + 8] = block
+        even_ref[8 * t : 8 * t + 8] = block * share
 
     def sweep(src, dst):
-        for start in range(8, 8 + SPAN, STRIP):
-            here = src[start : start + STRIP]
-            total = src[start - 1 : start - 1 + STRIP] + src[start + 1 : start + 1 + STRIP]
+        first = here = src[0:8]
+        behind = pltpu.roll(src[8 * STEPS - 8 :], 1, 0)
+        for t in range(STEPS):
+            ahead = src[8 * t + 8 : 8 * t + 16] if t < STEPS - 1 else pltpu.roll(first, 7, 0)
+            total = behind + ahead + density_ref[8 * t : 8 * t + 8]
             total += jnp.where(not_first, pltpu.roll(here, 1, 1), 0.0)
             total += jnp.where(not_last, pltpu.roll(here, NROW - 1, 1), 0.0)
-            total += density_ref[start - 8 : start - 8 + STRIP]
-            dst[start : start + STRIP] = total * share
+            dst[8 * t : 8 * t + 8] = total * share
+            behind, here = here, ahead
 
     def two_sweeps(_, carry):
         sweep(even_ref, odd_ref)
@@ -146,9 +269,11 @@
     lax.fori_loop(0, (SWEEPS - 1) // 2, two_sweeps, 0)
     sweep(even_ref, odd_ref)
     weight = weight_ref[0]
+    for t in range(STEPS):
+        plain_ref[pl.ds(t, 8, stride=STEPS)] = odd_ref[8 * t : 8 * t + 8] * weight
     for tile in range(OWN // TILE):
-        first = 8 + HALO + tile * TILE
-        turned_ref[8 : 8 + NROW] = (odd_ref[first : first + TILE] * weight).T
+        first = HALO + tile * TILE
+        turned_ref[8 : 8 + NROW] = plain_ref[first : first + TILE].T
         for band in range(BANDS):
             out_ref[BANDS - 1 - band, tile * ROWS : (tile + 1) * ROWS] = turned_ref[
                 R * band + 7 : R * band + 7 + ROWS
@@ -166,8 +291,9 @@
         out_shape=jax.ShapeDtypeStruct((BANDS, MSG, TILE), jnp.float32),
         scratch_shapes=[
             pltpu.VMEM((SPAN, NROW), jnp.float32),
-            pltpu.VMEM((SPAN + 16, NROW), jnp.float32),
-            pltpu.VMEM((SPAN + 16, NROW), jnp.float32),
+            pltpu.VMEM((SPAN, NROW), jnp.float32),
+            pltpu.VMEM((SPAN, NROW), jnp.float32),
+            pltpu.VMEM((SPAN, NROW), jnp.float32),
             pltpu.VMEM((NROW + 16, TILE), jnp.float32),
         ],
         compiler_params=pltpu.CompilerParams(vmem_limit_bytes=24 * 2**20),
@@ -256,7 +382,7 @@
                 out_ref[entry, :, columns[t]] = state[entry]
         return carry
 
-    lax.fori_loop(0, BANDS, group_body, 0)
+    lax.fori_loop(0, BANDS, group_body, 0, unroll=4)
 
 
 def recent_kernel(back, own_ref, other_ref, one_ref, one_other_ref, out_ref):
@@ -332,16 +458,12 @@
     return lax.ppermute(block, "plane", [(i, i ^ 1) for i in range(PLANES)])
 
 
-def along_band(block, steps, first):
+def exchanged(block, step, first):
     route = []
     for plane in range(PLANES):
-        for y in range(SIDE):
-            for z in range(SIDE):
-                if (plane % 2 == 0) == first:
-                    target = SIDE * y + (z + steps) % SIDE
-                else:
-                    target = SIDE * ((y + steps) % SIDE) + z
-                route.append((plane * BANDS + SIDE * y + z, plane * BANDS + target))
+        side = 1 if (plane % 2 == 0) == first else SIDE
+        for band in range(BANDS):
+            route.append((plane * BANDS + band, plane * BANDS + (band ^ (step * side))))
     return lax.ppermute(block, ("plane", "band"), route)
 
 
@@ -360,22 +482,24 @@
 
 
 def reduced_density(slabs, slot_block):
-    *parts, power = partial_densities(slabs, slot_block)
-    codes = {}
-    for step, after in ((2, 1), (1, 3), (3, 0)):
-        code = coded(parts[step], power)
-        code, parts[after] = lax.optimization_barrier((code, parts[after]))
-        codes[step] = along_band(code, step, True)
-    powers = [power_of(codes[step]) for step in (1, 2, 3)]
+    far, edges, power = far_sums(slabs, slot_block)
+    code = coded(far, power)
+    code, edges = lax.optimization_barrier((code, edges))
+    codes = {FAR: exchanged(code, FAR, True)}
+    *parts, power = near_sums(slabs, slot_block, edges)
+    parts = dict(zip(NEAR, parts))
+    for step in NEAR[:2]:
+        codes[step] = exchanged(coded(parts[step], power), step, True)
+    powers = [power_of(codes[step]) for step in ORDER[:3]]
     power = functools.reduce(jnp.maximum, powers, power)
-    factors = [jnp.exp2(power - TOP) for power in powers]
+    factors = {step: jnp.exp2(x - TOP) for step, x in zip(ORDER, powers)}
     sums = {}
-    for other in (2, 1, 3, 0):
+    for other in ORDER:
         total = parts[0][other]
-        for step in (1, 2, 3):
-            total += decoded(codes[step][other], factors[step - 1])
-        sums[other] = total if other == 0 else along_band(coded(total, power), other, False)
-    for other in (1, 2, 3):
+        for step in ORDER[:3]:
+            total += decoded(codes[step][other], factors[step])
+        sums[other] = total if other == 0 else exchanged(coded(total, power), other, False)
+    for other in ORDER[:3]:
         total = sums[0]
         factor = jnp.exp2(power_of(sums[other]) - TOP)
         sums[0] = total + decoded(sums[other], factor)

time: 80 us -> 73.8 us (0.922)
  waiting for transfers between devices: 25.2 us -> 22 us
  other arithmetic: 2.62 us -> 1.2 us
  starting transfers between devices: 22.6 us -> 21.4 us
    ppermute x6, waiting for transfers between devices: 18.7 us -> 15 us  [exchanged(): return lax.ppermute(block, ('plane', 'band'), route)]
    pallas_call x3, Pallas kernels: 7.67 us -> 5.29 us  [chain_call(): pl.pallas_call(kernel, in_specs=[vmem] * len(operands), out_specs=vmem, o...]
    pallas_call x1 -> x2, Pallas kernels: 6.79 us -> 8.4 us  [sum_call(): pl.pallas_call(kernel, in_specs=[pl.BlockSpec(memory_space=pltpu.SMEM), p...]
    convert_element_type x4 -> x3, other arithmetic: 1.66 us -> 0.95 us  [coded(): return jnp.where(row == OWN, power, scaled).astype(jnp.float16)]
  transfers between devices with their start and end apart: 13 -> 13, of which waited for: 7 -> 7; matrix products, arithmetic and copies ran while one was open for 0% -> 1% of each run, Pallas kernels for 6% -> 11%
where the time goes in v3:
time: 73.8 us; the launch traced here: 73.3 us
  waiting for transfers between devices  22 us (30%)
  starting transfers between devices  21.4 us (29%)
  Pallas kernels  17.5 us (24%)
  blocking collectives  9.87 us (13%)
  other arithmetic  1.2 us (2%)
  between operations  0.78 us (1%)
    ppermute x6, waiting for transfers between devices, exchanged(): return lax.ppermute(block, ('plane', 'band'), route)  15 us
    ppermute x4, starting transfers between devices, from_other_core(): return lax.ppermute(block, 'plane', [(i, i ^ 1) for i in range(PLANES)])  10 us
    all_to_all x1, blocking collectives, body(): lax.all_to_all(messages, 'band', split_axis=0, concat_axis=0, axis_index_...  9.87 us
    ppermute x6, starting transfers between devices, exchanged(): return lax.ppermute(block, ('plane', 'band'), route)  8.66 us
    pallas_call x2, Pallas kernels, sum_call(): pl.pallas_call(kernel, in_specs=[pl.BlockSpec(memory_space=pltpu.SMEM), p...  8.4 us
    ppermute x3, waiting for transfers between devices, from_chip(): lax.ppermute(block, 'plane', [(i, (i + 2 * back) % PLANES) for i in range...  6.37 us
    pallas_call x3, Pallas kernels, chain_call(): pl.pallas_call(kernel, in_specs=[vmem] * len(operands), out_specs=vmem, o...  5.29 us
    pallas_call x1, Pallas kernels, relaxed(): pl.pallas_call(relax_kernel, in_specs=[pl.BlockSpec(memory_space=pltpu.SM...  3.8 us
  transfers between devices with their start and end apart: 13, of which 7 were waited for; matrix products, arithmetic and copies ran while one was open for 1% of the time, Pallas kernels for 11%

profile of v3, /device:TPU:7, one launch (start us, length us, event | category | flops | bytes accessed | tf_op | source)
XLA Modules:
  0.0 73.3 jit_solution(11620468802398500903)
XLA Ops:
  0.0 3.1 %far_sums.1 = (f32[4,560,128]{2,1,0:T(8,128)S(1)}, f32[16,48,128]{2,1,0:T(8,128)S(1)}, f32[1,128]{1,0:T(1,128)S(1)}) custom-call(s32[1,64]{1,0:T(1,128)} %slot_ref.3, bf16[64,4,8192]{2,1,0:T(4,128)(2,1)} %bitcast.114), custom_call_target="tpu_custom_call" | custom-call | tf_op jit(solution)/shard_map/far_sums/pallas_call | solution.py:195
  3.3 0.5 copy-done
  3.8 2.9 %collective-permute-start.2 = (f16[4,560,128]{2,1,0:T(8,128)(2,1)S(1)}, f16[4,560,128]{2,1,0:T(8,128)(2,1)S(1)}, u32[]{:S(2)}, u32[]{:S(2)}) collective-permute-start(f16[4,560,128]{2,1,0:T(8,128)(2,1)S(1)} %select_convert_fusion.2), channel_id=1, source_target_pairs={{0,2},{1,3},{2,0},{3,1},{4,6},{5,7},{6,4},{7,5},{8,10},{9,11},{10,... | collective-permute-start | bytes 1720328 | tf_op jit(solution)/shard_map/ppermute | solution.py:467
  6.8 5.3 %near_sums.1 = (f32[4,560,128]{2,1,0:T(8,128)S(1)}, f32[4,560,128]{2,1,0:T(8,128)S(1)}, f32[4,560,128]{2,1,0:T(8,128)S(1)}, f32[1,128]{1,0:T(1,128)S(1)}) custom-call(s32[1,64]{1,0:T(1,128)} %slot_ref.3, bf16[64,4,8192]{2,1,0:T(4,128)(2,1)} %bitcast.115, f32[16,48,128]{2,1,0:T(8,128)} %copy-done), custom_call_target="tpu_custom_call" | custom-call | tf_op jit(solution)/shard_map/near_sums/pallas_call | solution.py:195
  12.5 0.5 collective-permute-start
  12.9 0.5 collective-permute-start.1
  13.4 0.8 %collective-permute-done.2 = f16[4,560,128]{2,1,0:T(8,128)(2,1)S(1)} collective-permute-done((f16[4,560,128]{2,1,0:T(8,128)(2,1)S(1)}, f16[4,560,128]{2,1,0:T(8,128)(2,1)S(1)}, u32[]{:S(2)}, u32[]{:S(2)}) %collective-permute-start.2) | collective-permute-done | bytes 573472 | tf_op jit(solution)/shard_map/ppermute | solution.py:467
  14.2 7.2 %collective-permute-done = f16[4,560,128]{2,1,0:T(8,128)(2,1)S(1)} collective-permute-done((f16[4,560,128]{2,1,0:T(8,128)(2,1)S(1)}, f16[4,560,128]{2,1,0:T(8,128)(2,1)S(1)}, u32[]{:S(2)}, u32[]{:S(2)}) %collective-permute-start) | collective-permute-done | bytes 573472 | tf_op jit(solution)/shard_map/ppermute | solution.py:467
  21.4 1.6 %collective-permute-done.1 = f16[4,560,128]{2,1,0:T(8,128)(2,1)S(1)} collective-permute-done((f16[4,560,128]{2,1,0:T(8,128)(2,1)S(1)}, f16[4,560,128]{2,1,0:T(8,128)(2,1)S(1)}, u32[]{:S(2)}, u32[]{:S(2)}) %collective-permute-start.1) | collective-permute-done | bytes 573472 | tf_op jit(solution)/shard_map/ppermute | solution.py:467
  23.4 1.4 %collective-permute-start.3 = (f16[560,128]{1,0:T(8,128)(2,1)S(1)}, f16[560,128]{1,0:T(8,128)(2,1)S(1)}, u32[]{:S(2)}, u32[]{:S(2)}) collective-permute-start(f16[560,128]{1,0:T(8,128)(2,1)S(1)} %get-tuple-element.25), channel_id=1, source_target_pairs={{0,4},{1,5},{2,6},{3,7},{4,0},{5,1},{6,2},{7,3},{8,12},{9,13},{10,... | collective-permute-start | bytes 430088 | tf_op jit(solution)/shard_map/ppermute | solution.py:467
  25.5 3.4 %collective-permute-start.5 = (f16[560,128]{1,0:T(8,128)(2,1)S(1)}, f16[560,128]{1,0:T(8,128)(2,1)S(1)}, u32[]{:S(2)}, u32[]{:S(2)}) collective-permute-start(f16[560,128]{1,0:T(8,128)(2,1)S(1)} %get-tuple-element.26), channel_id=1, source_target_pairs={{0,8},{1,9},{2,10},{3,11},{4,12},{5,13},{6,14},{7,15},{8,0},{9,1},... | collective-permute-start | bytes 430088 | tf_op jit(solution)/shard_map/ppermute | solution.py:467
  28.9 3.3 %collective-permute-done.5 = f16[560,128]{1,0:T(8,128)(2,1)S(1)} collective-permute-done((f16[560,128]{1,0:T(8,128)(2,1)S(1)}, f16[560,128]{1,0:T(8,128)(2,1)S(1)}, u32[]{:S(2)}, u32[]{:S(2)}) %collective-permute-start.5) | collective-permute-done | bytes 143392 | tf_op jit(solution)/shard_map/ppermute | solution.py:467
  32.2 2.2 %collective-permute-done.4 = f16[560,128]{1,0:T(8,128)(2,1)S(1)} collective-permute-done((f16[560,128]{1,0:T(8,128)(2,1)S(1)}, f16[560,128]{1,0:T(8,128)(2,1)S(1)}, u32[]{:S(2)}, u32[]{:S(2)}) %collective-permute-start.4) | collective-permute-done | bytes 143392 | tf_op jit(solution)/shard_map/ppermute | solution.py:467
  34.5 3.8 %relaxed.1 = f32[16,40,128]{2,1,0:T(8,128)S(1)} custom-call(f32[1]{0:T(128)S(6)} %copy.4.weight_ref, f32[560,128]{1,0:T(8,128)S(1)} %fusion.21.part_ref), custom_call_target="tpu_custom_call" | custom-call | tf_op jit(solution)/shard_map/relaxed/pallas_call | solution.py:284
  38.3 9.9 %all_to_all.5 = f32[16,40,128]{2,1,0:T(8,128)S(1)} all-to-all(f32[16,40,128]{2,1,0:T(8,128)S(1)} %relaxed.1), channel_id=1, replica_groups={{15,14,13,12,11,10,9,8,7,6,5,4,3,2,1,0},{31,30,29,28,27,26,25,24,23,22,..., dimensions={0} | all-to-all | bytes 655360 | tf_op jit(solution)/shard_map/all_to_all | solution.py:513
  48.2 0.6 collective-permute-start.11
  48.8 2.1 %collective-permute-start.7 = (f32[640,128]{1,0:T(8,128)S(1)}, f32[640,128]{1,0:T(8,128)S(1)}, u32[]{:S(2)}, u32[]{:S(2)}) collective-permute-start(f32[640,128]{1,0:T(8,128)S(1)} %bitcast.108), channel_id=1, source_target_pairs={{0,32},{16,48},{32,64},{48,80},{64,96},{80,112},{96,0},{112,16},{1... | collective-permute-start | bytes 983048 | tf_op jit(solution)/shard_map/ppermute | solution.py:454
  50.9 6.4 %collective-permute-done.11.own_ref = f32[640,128]{1,0:T(8,128)S(1)} collective-permute-done((f32[640,128]{1,0:T(8,128)S(1)}, f32[640,128]{1,0:T(8,128)S(1)}, u32[]{:S(2)}, u32[]{:S(2)}) %collective-permute-start.11) | collective-permute-done | bytes 327712 | tf_op jit(solution)/shard_map/ppermute | solution.py:454
  57.2 9.4 %collective-permute-start.12 = (f32[640,128]{1,0:T(8,128)S(1)}, f32[640,128]{1,0:T(8,128)S(1)}, u32[]{:S(2)}, u32[]{:S(2)}) collective-permute-start(f32[640,128]{1,0:T(8,128)S(1)} %collective-permute-done.11.own_ref), channel_id=1, source_target_pairs={{0,16},{16,0},{32,48},{48,32},{64,80},{80,64},{96,112},{112,96},{1... | collective-permute-start | bytes 983048 | tf_op jit(solution)/shard_map/ppermute | solution.py:458
  66.7 0.5 collective-permute-start.8
  67.3 0.7 collective-permute-done.12.other_ref
  67.9 1.0 %chain_first.1.first_ref = f32[6,8,8192]{2,1,0:T(8,128)S(1)} custom-call(f32[640,128]{1,0:T(8,128)S(1)} %collective-permute-done.11.own_ref, f32[640,128]{1,0:T(8,128)S(1)} %collective-permute-done.12.other_ref), custom_call_target="tpu_custom_call" | custom-call | flops 5242880 | bytes 2228224 | tf_op jit(solution)/shard_map/chain_first/pallas_call | solution.py:438
  69.0 1.9 %chain_recent.1.state_ref = f32[6,8,8192]{2,1,0:T(8,128)S(1)} custom-call(f32[640,128]{1,0:T(8,128)S(1)} %bitcast.111, f32[640,128]{1,0:T(8,128)S(1)} %collective-permute-done.6.other_ref, f32[640,128]{1,0:T(8,128)S(1)} %collective-permute-done.7.one_ref, f32[640,128]{1,0:T(8,128)S(1)} %collective-permute-done.8.one_other_ref), custom_call_target="tpu_custom_call" | custom-call | flops 5242880 | bytes 2883584 | tf_op jit(solution)/shard_map/chain_recent/pallas_call | solution.py:438
  70.9 2.4 %chain_finish.1 = f32[1,6,8,8192]{3,2,1,0:T(8,128)} custom-call(f32[6,8,8192]{2,1,0:T(8,128)S(1)} %chain_recent.1.state_ref, f32[640,128]{1,0:T(8,128)S(1)} %collective-permute-done.9.own_ref, f32[640,128]{1,0:T(8,128)S(1)} %collective-permute-done.10.other_ref, f32[6,8,8192]{2,1,0:T(8,128)S(1)} %chain_first.1.first_ref), custom_call_target="tpu_custom_call" | custom-call | flops 5242880 | bytes 5373952 | tf_op jit(solution)/shard_map/chain_finish/pallas_call | solution.py:438
  (25 shorter events, 1.3 us)
Async XLA Ops:
  3.1 0.7 %copy-start = (f32[16,48,128]{2,1,0:T(8,128)}, f32[16,48,128]{2,1,0:T(8,128)S(1)}, u32[]{:S(2)}) copy-start(f32[16,48,128]{2,1,0:T(8,128)S(1)} %get-tuple-element.17.far_edges_ref) | copy-start | bytes 1179652
  3.8 10.4 %collective-permute-start.2 = (f16[4,560,128]{2,1,0:T(8,128)(2,1)S(1)}, f16[4,560,128]{2,1,0:T(8,128)(2,1)S(1)}, u32[]{:S(2)}, u32[]{:S(2)}) collective-permute-start(f16[4,560,128]{2,1,0:T(8,128)(2,1)S(1)} %select_convert_fusion.2), channel_id=1, source_target_pairs={{0,2},{1,3},{2,0},{3,1},{4,6},{5,7},{6,4},{7,5},{8,10},{9,11},{10,... | collective-permute-start | bytes 1720328 | tf_op jit(solution)/shard_map/ppermute | solution.py:467
  12.5 8.9 %collective-permute-start = (f16[4,560,128]{2,1,0:T(8,128)(2,1)S(1)}, f16[4,560,128]{2,1,0:T(8,128)(2,1)S(1)}, u32[]{:S(2)}, u32[]{:S(2)}) collective-permute-start(f16[4,560,128]{2,1,0:T(8,128)(2,1)S(1)} %get-tuple-element.28), channel_id=1, source_target_pairs={{0,1},{1,0},{2,3},{3,2},{4,5},{5,4},{6,7},{7,6},{8,9},{9,8},{10,11... | collective-permute-start | bytes 1720328 | tf_op jit(solution)/shard_map/ppermute | solution.py:467
  12.9 10.1 %collective-permute-start.1 = (f16[4,560,128]{2,1,0:T(8,128)(2,1)S(1)}, f16[4,560,128]{2,1,0:T(8,128)(2,1)S(1)}, u32[]{:S(2)}, u32[]{:S(2)}) collective-permute-start(f16[4,560,128]{2,1,0:T(8,128)(2,1)S(1)} %get-tuple-element.29), channel_id=1, source_target_pairs={{0,3},{1,2},{2,1},{3,0},{4,7},{5,6},{6,5},{7,4},{8,11},{9,10},{10,... | collective-permute-start | bytes 1720328 | tf_op jit(solution)/shard_map/ppermute | solution.py:467
  23.4 5.5 %collective-permute-start.3 = (f16[560,128]{1,0:T(8,128)(2,1)S(1)}, f16[560,128]{1,0:T(8,128)(2,1)S(1)}, u32[]{:S(2)}, u32[]{:S(2)}) collective-permute-start(f16[560,128]{1,0:T(8,128)(2,1)S(1)} %get-tuple-element.25), channel_id=1, source_target_pairs={{0,4},{1,5},{2,6},{3,7},{4,0},{5,1},{6,2},{7,3},{8,12},{9,13},{10,... | collective-permute-start | bytes 430088 | tf_op jit(solution)/shard_map/ppermute | solution.py:467
  25.5 6.7 %collective-permute-start.5 = (f16[560,128]{1,0:T(8,128)(2,1)S(1)}, f16[560,128]{1,0:T(8,128)(2,1)S(1)}, u32[]{:S(2)}, u32[]{:S(2)}) collective-permute-start(f16[560,128]{1,0:T(8,128)(2,1)S(1)} %get-tuple-element.26), channel_id=1, source_target_pairs={{0,8},{1,9},{2,10},{3,11},{4,12},{5,13},{6,14},{7,15},{8,0},{9,1},... | collective-permute-start | bytes 430088 | tf_op jit(solution)/shard_map/ppermute | solution.py:467
  28.9 5.5 %collective-permute-start.4 = (f16[560,128]{1,0:T(8,128)(2,1)S(1)}, f16[560,128]{1,0:T(8,128)(2,1)S(1)}, u32[]{:S(2)}, u32[]{:S(2)}) collective-permute-start(f16[560,128]{1,0:T(8,128)(2,1)S(1)} %get-tuple-element.27), channel_id=1, source_target_pairs={{0,12},{1,13},{2,14},{3,15},{4,8},{5,9},{6,10},{7,11},{8,4},{9,5},... | collective-permute-start | bytes 430088 | tf_op jit(solution)/shard_map/ppermute | solution.py:467
  48.2 9.1 %collective-permute-start.11 = (f32[640,128]{1,0:T(8,128)S(1)}, f32[640,128]{1,0:T(8,128)S(1)}, u32[]{:S(2)}, u32[]{:S(2)}) collective-permute-start(f32[640,128]{1,0:T(8,128)S(1)} %bitcast.107), channel_id=1, source_target_pairs={{0,96},{16,112},{32,0},{48,16},{64,32},{80,48},{96,64},{112,80},{1... | collective-permute-start | bytes 983048 | tf_op jit(solution)/shard_map/ppermute | solution.py:454
  48.8 17.9 %collective-permute-start.7 = (f32[640,128]{1,0:T(8,128)S(1)}, f32[640,128]{1,0:T(8,128)S(1)}, u32[]{:S(2)}, u32[]{:S(2)}) collective-permute-start(f32[640,128]{1,0:T(8,128)S(1)} %bitcast.108), channel_id=1, source_target_pairs={{0,32},{16,48},{32,64},{48,80},{64,96},{80,112},{96,0},{112,16},{1... | collective-permute-start | bytes 983048 | tf_op jit(solution)/shard_map/ppermute | solution.py:454
  50.9 16.3 %collective-permute-start.9 = (f32[640,128]{1,0:T(8,128)S(1)}, f32[640,128]{1,0:T(8,128)S(1)}, u32[]{:S(2)}, u32[]{:S(2)}) collective-permute-start(f32[640,128]{1,0:T(8,128)S(1)} %bitcast.109), channel_id=1, source_target_pairs={{0,64},{16,80},{32,96},{48,112},{64,0},{80,16},{96,32},{112,48},{1... | collective-permute-start | bytes 983048 | tf_op jit(solution)/shard_map/ppermute | solution.py:454
  57.2 10.7 %collective-permute-start.12 = (f32[640,128]{1,0:T(8,128)S(1)}, f32[640,128]{1,0:T(8,128)S(1)}, u32[]{:S(2)}, u32[]{:S(2)}) collective-permute-start(f32[640,128]{1,0:T(8,128)S(1)} %collective-permute-done.11.own_ref), channel_id=1, source_target_pairs={{0,16},{16,0},{32,48},{48,32},{64,80},{80,64},{96,112},{112,96},{1... | collective-permute-start | bytes 983048 | tf_op jit(solution)/shard_map/ppermute | solution.py:458
  66.7 2.3 %collective-permute-start.6 = (f32[640,128]{1,0:T(8,128)S(1)}, f32[640,128]{1,0:T(8,128)S(1)}, u32[]{:S(2)}, u32[]{:S(2)}) collective-permute-start(f32[640,128]{1,0:T(8,128)S(1)} %bitcast.110), channel_id=1, source_target_pairs={{0,16},{16,0},{32,48},{48,32},{64,80},{80,64},{96,112},{112,96},{1... | collective-permute-start | bytes 983048 | tf_op jit(solution)/shard_map/ppermute | solution.py:458
  66.7 2.3 %collective-permute-start.8 = (f32[640,128]{1,0:T(8,128)S(1)}, f32[640,128]{1,0:T(8,128)S(1)}, u32[]{:S(2)}, u32[]{:S(2)}) collective-permute-start(f32[640,128]{1,0:T(8,128)S(1)} %collective-permute-done.7.one_ref), channel_id=1, source_target_pairs={{0,16},{16,0},{32,48},{48,32},{64,80},{80,64},{96,112},{112,96},{1... | collective-permute-start | bytes 983048 | tf_op jit(solution)/shard_map/ppermute | solution.py:458
  67.2 3.7 %collective-permute-start.10 = (f32[640,128]{1,0:T(8,128)S(1)}, f32[640,128]{1,0:T(8,128)S(1)}, u32[]{:S(2)}, u32[]{:S(2)}) collective-permute-start(f32[640,128]{1,0:T(8,128)S(1)} %collective-permute-done.9.own_ref), channel_id=1, source_target_pairs={{0,16},{16,0},{32,48},{48,32},{64,80},{80,64},{96,112},{112,96},{1... | collective-permute-start | bytes 983048 | tf_op jit(solution)/shard_map/ppermute | solution.py:458

commit v4 on v3

--- a/solution.py
+++ b/solution.py
@@ -25,7 +25,7 @@
 ROWS = R + 2
 MSG = ROWS * OWN // TILE
 TOP = 13.0
-VMEM_BYTES = 54 * 2**20
+VMEM_BYTES = 53 * 2**20
 
 
 FAR, NEAR = 2, (1, 3, 0)
@@ -135,8 +135,8 @@
         low, high, most = store_part(
             out_ref, other, slabs[:, TILE : TILE + OWN], select_ref, turned_ref, most
         )
-        edges_ref[relay.place(after(band)), 0:HALO] = high
-        edges_ref[relay.place(before(band)), HALO:] = low
+        edges_ref[other, 0:HALO] = high
+        edges_ref[other, HALO:] = low
         outer = summed_turned(outer_tiles(slabs), select_ref)
         left, right = outer[TILE - HALO : TILE], outer[TILE : TILE + HALO]
         out_ref[other, OWN : OWN + HALO] = left
@@ -163,7 +163,10 @@
     for slot in range(len(NEAR) * SIDE):
         fetch(slot).start()
     fill_select(slot_ref, select_ref, turned_ref)
-    edges[...] = far_edges_ref[...]
+    for other in range(SIDE):
+        band = relay.band_at(FAR, other)
+        edges[relay.place(after(band)), 0:HALO] = far_edges_ref[other, 0:HALO]
+        edges[relay.place(before(band)), HALO:] = far_edges_ref[other, HALO:]
 
     def chunks(index, most):
         def chunk(other, most):
@@ -216,7 +219,8 @@
 def far_sums(slabs, slot_block):
     held = pltpu.VMEM((SIDE, SLOTS, BLK, OWN + 2 * TILE), jnp.bfloat16)
     operands = (slot_block, slabs)
-    return sum_call(far_kernel, "far_sums", operands, 1, [EDGES, POWER], [held], (SIDE, 3))
+    edges = pltpu.VMEM((SIDE, 2 * HALO, NROW), jnp.float32)
+    return sum_call(far_kernel, "far_sums", operands, 1, [edges, POWER], [held], (SIDE, 3))
 
 
 def near_sums(slabs, slot_block, edges):
@@ -302,6 +306,7 @@
 
 
 GROUP = OWN // TILE
+PART = NCOL // SIDE
 
 
 def plane_maps(ref, starts, is_first, is_last):
@@ -351,7 +356,7 @@
     )
 
 
-def chain_step(state_ref, out_ref, pieces, first_ref=None, last=False):
+def chain_step(state_ref, out_ref, pieces, first_ref=None, final_ref=None, sems=None):
     lane = lax.broadcasted_iota(jnp.int32, (R, TILE), 1)
     is_first = lane == 0
     is_last = lane == TILE - 1
@@ -376,13 +381,32 @@
                 state = after_map(state, one[t])
             if first_ref is not None:
                 state = after_state(state, [first_ref[entry, :, columns[t]] for entry in range(6)])
-            if last:
+            if final_ref is not None:
                 state = tuple(x - 1.0 if e in (0, 3) else x for e, x in enumerate(state))
             for entry in range(6):
                 out_ref[entry, :, columns[t]] = state[entry]
         return carry
 
-    lax.fori_loop(0, BANDS, group_body, 0, unroll=4)
+    def columns_of(part):
+        return pl.ds(pl.multiple_of(part * PART, PART), PART)
+
+    def copy_out(part):
+        columns = columns_of(part)
+        return pltpu.make_async_copy(
+            out_ref.at[:, :, columns], final_ref.at[:, :, columns], sems.at[part]
+        )
+
+    def part_body(part, carry):
+        for group in range(SIDE):
+            group_body(part * SIDE + group, 0)
+        if final_ref is not None:
+            copy_out(SIDE - 1 - part).start()
+        return carry
+
+    lax.fori_loop(0, SIDE, part_body, 0)
+    if final_ref is not None:
+        for part in range(SIDE):
+            copy_out(part).wait()
 
 
 def recent_kernel(back, own_ref, other_ref, one_ref, one_other_ref, out_ref):
@@ -412,33 +436,35 @@
             chain_step(None, out_ref, pieces)
 
 
-def finish_kernel(back, state_ref, own_ref, other_ref, first_ref, out_ref):
+def finish_kernel(back, state_ref, own_ref, other_ref, first_ref, final_ref, out_ref, sems):
     me = lax.axis_index("plane")
     chip, core = me // 2, lax.rem(me, 2)
-    out_ref = out_ref.at[0]
+    final_ref = final_ref.at[0]
 
     @pl.when(chip < back)
     def _():
-        chain_step(state_ref, out_ref, [], last=True)
+        chain_step(state_ref, out_ref, [], None, final_ref, sems)
 
     for which in (0, 1):
         pieces = [own_ref, other_ref] if which else [other_ref, own_ref]
 
         @pl.when(jnp.logical_and(chip == back, core == which))
         def _():
-            chain_step(state_ref, out_ref, pieces, last=True)
+            chain_step(state_ref, out_ref, pieces, None, final_ref, sems)
 
         @pl.when(jnp.logical_and(chip > back, core == which))
         def _():
-            chain_step(state_ref, out_ref, pieces, first_ref, last=True)
-
-
-def chain_call(kernel, name, operands, shape):
+            chain_step(state_ref, out_ref, pieces, first_ref, final_ref, sems)
+
+
+def chain_call(kernel, name, operands, shape, last=False):
     vmem = pl.BlockSpec(memory_space=pltpu.VMEM)
+    scratch = [pltpu.VMEM((6, R, NCOL), jnp.float32), pltpu.SemaphoreType.DMA((SIDE,))]
     return pl.pallas_call(
         kernel,
         in_specs=[vmem] * len(operands),
-        out_specs=vmem,
+        out_specs=pl.BlockSpec(memory_space=pl.ANY) if last else vmem,
+        scratch_shapes=scratch if last else [],
         out_shape=jax.ShapeDtypeStruct(shape, jnp.float32),
         cost_estimate=pl.CostEstimate(
             flops=80 * R * NCOL,
@@ -494,12 +520,12 @@
     power = functools.reduce(jnp.maximum, powers, power)
     factors = {step: jnp.exp2(x - TOP) for step, x in zip(ORDER, powers)}
     sums = {}
-    for other in ORDER:
+    for other in (2, 1, 3, 0):
         total = parts[0][other]
-        for step in ORDER[:3]:
+        for step in (3, 1, 2):
             total += decoded(codes[step][other], factors[step])
         sums[other] = total if other == 0 else exchanged(coded(total, power), other, False)
-    for other in ORDER[:3]:
+    for other in (2, 1, 3):
         total = sums[0]
         factor = jnp.exp2(power_of(sums[other]) - TOP)
         sums[0] = total + decoded(sums[other], factor)
@@ -523,7 +549,7 @@
     first = chain_call(first, "chain_first", (three, from_other_core(three)), shape)
     finish = functools.partial(finish_kernel, 2)
     operands = (recent, two, from_other_core(two), first)
-    return chain_call(finish, "chain_finish", operands, (1,) + shape)
+    return chain_call(finish, "chain_finish", operands, (1,) + shape, last=True)
 
 
 def solution(mesh):

time: 73.8 us -> 71.4 us (0.967)
  waiting for transfers between devices: 22 us -> 20.3 us
    ppermute x6, waiting for transfers between devices: 15 us -> 13.6 us  [exchanged(): return lax.ppermute(block, ('plane', 'band'), route)]
  transfers between devices with their start and end apart: 13 -> 13, of which waited for: 7 -> 6; matrix products, arithmetic and copies ran while one was open for 1% -> 1% of each run, Pallas kernels for 11% -> 11%
where the time goes in v4:
time: 71.4 us; the launch traced here: 70.8 us
  starting transfers between devices  21.1 us (30%)
  waiting for transfers between devices  20.3 us (28%)
  Pallas kernels  17.1 us (24%)
  blocking collectives  9.87 us (14%)
  other arithmetic  1.22 us (2%)
  between operations  0.79 us (1%)
    ppermute x6, waiting for transfers between devices, exchanged(): return lax.ppermute(block, ('plane', 'band'), route)  13.6 us
    ppermute x4, starting transfers between devices, from_other_core(): return lax.ppermute(block, 'plane', [(i, i ^ 1) for i in range(PLANES)])  10.3 us
    all_to_all x1, blocking collectives, body(): lax.all_to_all(messages, 'band', split_axis=0, concat_axis=0, axis_index_...  9.87 us
    pallas_call x2, Pallas kernels, sum_call(): pl.pallas_call(kernel, in_specs=[pl.BlockSpec(memory_space=pltpu.SMEM), p...  8.28 us
    ppermute x6, starting transfers between devices, exchanged(): return lax.ppermute(block, ('plane', 'band'), route)  8.07 us
    ppermute x3, waiting for transfers between devices, from_chip(): lax.ppermute(block, 'plane', [(i, (i + 2 * back) % PLANES) for i in range...  6.09 us
    pallas_call x3, Pallas kernels, chain_call(): pl.pallas_call(kernel, in_specs=[vmem] * len(operands), out_specs=pl.Bloc...  4.98 us
    pallas_call x1, Pallas kernels, relaxed(): pl.pallas_call(relax_kernel, in_specs=[pl.BlockSpec(memory_space=pltpu.SM...  3.8 us
  transfers between devices with their start and end apart: 13, of which 6 were waited for; matrix products, arithmetic and copies ran while one was open for 1% of the time, Pallas kernels for 11%

profile of v4, /device:TPU:7, one launch (start us, length us, event | category | flops | bytes accessed | tf_op | source)
XLA Modules:
  0.0 70.8 jit_solution(12693965510883163355)
XLA Ops:
  0.0 3.1 %far_sums.1 = (f32[4,560,128]{2,1,0:T(8,128)S(1)}, f32[4,48,128]{2,1,0:T(8,128)S(1)}, f32[1,128]{1,0:T(1,128)S(1)}) custom-call(s32[1,64]{1,0:T(1,128)} %slot_ref.3, bf16[64,4,8192]{2,1,0:T(4,128)(2,1)} %bitcast.114), custom_call_target="tpu_custom_call" | custom-call | tf_op jit(solution)/shard_map/far_sums/pallas_call | solution.py:198
  3.3 0.4 copy-done
  3.7 2.9 %collective-permute-start.2 = (f16[4,560,128]{2,1,0:T(8,128)(2,1)S(1)}, f16[4,560,128]{2,1,0:T(8,128)(2,1)S(1)}, u32[]{:S(2)}, u32[]{:S(2)}) collective-permute-start(f16[4,560,128]{2,1,0:T(8,128)(2,1)S(1)} %select_convert_fusion.2), channel_id=1, source_target_pairs={{0,2},{1,3},{2,0},{3,1},{4,6},{5,7},{6,4},{7,5},{8,10},{9,11},{10,... | collective-permute-start | bytes 1720328 | tf_op jit(solution)/shard_map/ppermute | solution.py:493
  6.7 5.2 %near_sums.1 = (f32[4,560,128]{2,1,0:T(8,128)S(1)}, f32[4,560,128]{2,1,0:T(8,128)S(1)}, f32[4,560,128]{2,1,0:T(8,128)S(1)}, f32[1,128]{1,0:T(1,128)S(1)}) custom-call(s32[1,64]{1,0:T(1,128)} %slot_ref.3, bf16[64,4,8192]{2,1,0:T(4,128)(2,1)} %bitcast.115, f32[4,48,128]{2,1,0:T(8,128)} %copy-done), custom_call_target="tpu_custom_call" | custom-call | tf_op jit(solution)/shard_map/near_sums/pallas_call | solution.py:198
  12.2 0.9 %collective-permute-start = (f16[4,560,128]{2,1,0:T(8,128)(2,1)S(1)}, f16[4,560,128]{2,1,0:T(8,128)(2,1)S(1)}, u32[]{:S(2)}, u32[]{:S(2)}) collective-permute-start(f16[4,560,128]{2,1,0:T(8,128)(2,1)S(1)} %get-tuple-element.28), channel_id=1, source_target_pairs={{0,3},{1,2},{2,1},{3,0},{4,7},{5,6},{6,5},{7,4},{8,11},{9,10},{10,... | collective-permute-start | bytes 1720328 | tf_op jit(solution)/shard_map/ppermute | solution.py:493
  13.1 1.0 %collective-permute-done.2 = f16[4,560,128]{2,1,0:T(8,128)(2,1)S(1)} collective-permute-done((f16[4,560,128]{2,1,0:T(8,128)(2,1)S(1)}, f16[4,560,128]{2,1,0:T(8,128)(2,1)S(1)}, u32[]{:S(2)}, u32[]{:S(2)}) %collective-permute-start.2) | collective-permute-done | bytes 573472 | tf_op jit(solution)/shard_map/ppermute | solution.py:493
  14.1 8.3 %collective-permute-done = f16[4,560,128]{2,1,0:T(8,128)(2,1)S(1)} collective-permute-done((f16[4,560,128]{2,1,0:T(8,128)(2,1)S(1)}, f16[4,560,128]{2,1,0:T(8,128)(2,1)S(1)}, u32[]{:S(2)}, u32[]{:S(2)}) %collective-permute-start) | collective-permute-done | bytes 573472 | tf_op jit(solution)/shard_map/ppermute | solution.py:493
  22.4 0.4 fusion.15
  22.8 3.4 %collective-permute-start.3 = (f16[560,128]{1,0:T(8,128)(2,1)S(1)}, f16[560,128]{1,0:T(8,128)(2,1)S(1)}, u32[]{:S(2)}, u32[]{:S(2)}) collective-permute-start(f16[560,128]{1,0:T(8,128)(2,1)S(1)} %get-tuple-element.25), channel_id=1, source_target_pairs={{0,8},{1,9},{2,10},{3,11},{4,12},{5,13},{6,14},{7,15},{8,0},{9,1},... | collective-permute-start | bytes 430088 | tf_op jit(solution)/shard_map/ppermute | solution.py:493
  26.9 0.5 collective-permute-start.5
  27.4 0.4 collective-permute-start.4
  27.8 0.9 %collective-permute-done.3 = f16[560,128]{1,0:T(8,128)(2,1)S(1)} collective-permute-done((f16[560,128]{1,0:T(8,128)(2,1)S(1)}, f16[560,128]{1,0:T(8,128)(2,1)S(1)}, u32[]{:S(2)}, u32[]{:S(2)}) %collective-permute-start.3) | collective-permute-done | bytes 143392 | tf_op jit(solution)/shard_map/ppermute | solution.py:493
  28.7 3.4 %collective-permute-done.5 = f16[560,128]{1,0:T(8,128)(2,1)S(1)} collective-permute-done((f16[560,128]{1,0:T(8,128)(2,1)S(1)}, f16[560,128]{1,0:T(8,128)(2,1)S(1)}, u32[]{:S(2)}, u32[]{:S(2)}) %collective-permute-start.5) | collective-permute-done | bytes 143392 | tf_op jit(solution)/shard_map/ppermute | solution.py:493
  32.3 3.8 %relaxed.1 = f32[16,40,128]{2,1,0:T(8,128)S(1)} custom-call(f32[1]{0:T(128)S(6)} %copy.4.weight_ref, f32[560,128]{1,0:T(8,128)S(1)} %fusion.21.part_ref), custom_call_target="tpu_custom_call" | custom-call | tf_op jit(solution)/shard_map/relaxed/pallas_call | solution.py:288
  36.1 9.9 %all_to_all.5 = f32[16,40,128]{2,1,0:T(8,128)S(1)} all-to-all(f32[16,40,128]{2,1,0:T(8,128)S(1)} %relaxed.1), channel_id=1, replica_groups={{15,14,13,12,11,10,9,8,7,6,5,4,3,2,1,0},{31,30,29,28,27,26,25,24,23,22,..., dimensions={0} | all-to-all | bytes 655360 | tf_op jit(solution)/shard_map/all_to_all | solution.py:539
  46.0 0.5 collective-permute-start.11
  46.5 2.1 %collective-permute-start.7 = (f32[640,128]{1,0:T(8,128)S(1)}, f32[640,128]{1,0:T(8,128)S(1)}, u32[]{:S(2)}, u32[]{:S(2)}) collective-permute-start(f32[640,128]{1,0:T(8,128)S(1)} %bitcast.108), channel_id=1, source_target_pairs={{0,32},{16,48},{32,64},{48,80},{64,96},{80,112},{96,0},{112,16},{1... | collective-permute-start | bytes 983048 | tf_op jit(solution)/shard_map/ppermute | solution.py:480
  48.7 6.1 %collective-permute-done.11.own_ref = f32[640,128]{1,0:T(8,128)S(1)} collective-permute-done((f32[640,128]{1,0:T(8,128)S(1)}, f32[640,128]{1,0:T(8,128)S(1)}, u32[]{:S(2)}, u32[]{:S(2)}) %collective-permute-start.11) | collective-permute-done | bytes 327712 | tf_op jit(solution)/shard_map/ppermute | solution.py:480
  54.8 9.7 %collective-permute-start.12 = (f32[640,128]{1,0:T(8,128)S(1)}, f32[640,128]{1,0:T(8,128)S(1)}, u32[]{:S(2)}, u32[]{:S(2)}) collective-permute-start(f32[640,128]{1,0:T(8,128)S(1)} %collective-permute-done.11.own_ref), channel_id=1, source_target_pairs={{0,16},{16,0},{32,48},{48,32},{64,80},{80,64},{96,112},{112,96},{1... | collective-permute-start | bytes 983048 | tf_op jit(solution)/shard_map/ppermute | solution.py:484
  64.5 0.5 collective-permute-start.8
  65.1 0.7 collective-permute-done.12.other_ref
  65.8 1.0 %chain_first.1.first_ref = f32[6,8,8192]{2,1,0:T(8,128)S(1)} custom-call(f32[640,128]{1,0:T(8,128)S(1)} %collective-permute-done.11.own_ref, f32[640,128]{1,0:T(8,128)S(1)} %collective-permute-done.12.other_ref), custom_call_target="tpu_custom_call" | custom-call | flops 5242880 | bytes 2228224 | tf_op jit(solution)/shard_map/chain_first/pallas_call | solution.py:463
  66.8 1.9 %chain_recent.1.state_ref = f32[6,8,8192]{2,1,0:T(8,128)S(1)} custom-call(f32[640,128]{1,0:T(8,128)S(1)} %bitcast.111, f32[640,128]{1,0:T(8,128)S(1)} %collective-permute-done.6.other_ref, f32[640,128]{1,0:T(8,128)S(1)} %collective-permute-done.7.one_ref, f32[640,128]{1,0:T(8,128)S(1)} %collective-permute-done.8.one_other_ref), custom_call_target="tpu_custom_call" | custom-call | flops 5242880 | bytes 2883584 | tf_op jit(solution)/shard_map/chain_recent/pallas_call | solution.py:463
  68.7 2.1 %chain_finish.1 = f32[1,6,8,8192]{3,2,1,0:T(8,128)} custom-call(f32[6,8,8192]{2,1,0:T(8,128)S(1)} %chain_recent.1.state_ref, f32[640,128]{1,0:T(8,128)S(1)} %collective-permute-done.9.own_ref, f32[640,128]{1,0:T(8,128)S(1)} %collective-permute-done.10.other_ref, f32[6,8,8192]{2,1,0:T(8,128)S(1)} %chain_first.1.first_ref), custom_call_target="tpu_custom_call" | custom-call | flops 5242880 | bytes 5373952 | tf_op jit(solution)/shard_map/chain_finish/pallas_call | solution.py:463
  (25 shorter events, 0.9 us)
Async XLA Ops:
  3.1 0.6 copy-start
  3.7 10.4 %collective-permute-start.2 = (f16[4,560,128]{2,1,0:T(8,128)(2,1)S(1)}, f16[4,560,128]{2,1,0:T(8,128)(2,1)S(1)}, u32[]{:S(2)}, u32[]{:S(2)}) collective-permute-start(f16[4,560,128]{2,1,0:T(8,128)(2,1)S(1)} %select_convert_fusion.2), channel_id=1, source_target_pairs={{0,2},{1,3},{2,0},{3,1},{4,6},{5,7},{6,4},{7,5},{8,10},{9,11},{10,... | collective-permute-start | bytes 1720328 | tf_op jit(solution)/shard_map/ppermute | solution.py:493
  12.2 10.1 %collective-permute-start = (f16[4,560,128]{2,1,0:T(8,128)(2,1)S(1)}, f16[4,560,128]{2,1,0:T(8,128)(2,1)S(1)}, u32[]{:S(2)}, u32[]{:S(2)}) collective-permute-start(f16[4,560,128]{2,1,0:T(8,128)(2,1)S(1)} %get-tuple-element.28), channel_id=1, source_target_pairs={{0,3},{1,2},{2,1},{3,0},{4,7},{5,6},{6,5},{7,4},{8,11},{9,10},{10,... | collective-permute-start | bytes 1720328 | tf_op jit(solution)/shard_map/ppermute | solution.py:493
  13.1 9.3 %collective-permute-start.1 = (f16[4,560,128]{2,1,0:T(8,128)(2,1)S(1)}, f16[4,560,128]{2,1,0:T(8,128)(2,1)S(1)}, u32[]{:S(2)}, u32[]{:S(2)}) collective-permute-start(f16[4,560,128]{2,1,0:T(8,128)(2,1)S(1)} %get-tuple-element.29), channel_id=1, source_target_pairs={{0,1},{1,0},{2,3},{3,2},{4,5},{5,4},{6,7},{7,6},{8,9},{9,8},{10,11... | collective-permute-start | bytes 1720328 | tf_op jit(solution)/shard_map/ppermute | solution.py:493
  22.8 5.9 %collective-permute-start.3 = (f16[560,128]{1,0:T(8,128)(2,1)S(1)}, f16[560,128]{1,0:T(8,128)(2,1)S(1)}, u32[]{:S(2)}, u32[]{:S(2)}) collective-permute-start(f16[560,128]{1,0:T(8,128)(2,1)S(1)} %get-tuple-element.25), channel_id=1, source_target_pairs={{0,8},{1,9},{2,10},{3,11},{4,12},{5,13},{6,14},{7,15},{8,0},{9,1},... | collective-permute-start | bytes 430088 | tf_op jit(solution)/shard_map/ppermute | solution.py:493
  26.9 5.2 %collective-permute-start.5 = (f16[560,128]{1,0:T(8,128)(2,1)S(1)}, f16[560,128]{1,0:T(8,128)(2,1)S(1)}, u32[]{:S(2)}, u32[]{:S(2)}) collective-permute-start(f16[560,128]{1,0:T(8,128)(2,1)S(1)} %get-tuple-element.26), channel_id=1, source_target_pairs={{0,12},{1,13},{2,14},{3,15},{4,8},{5,9},{6,10},{7,11},{8,4},{9,5},... | collective-permute-start | bytes 430088 | tf_op jit(solution)/shard_map/ppermute | solution.py:493
  27.4 4.7 %collective-permute-start.4 = (f16[560,128]{1,0:T(8,128)(2,1)S(1)}, f16[560,128]{1,0:T(8,128)(2,1)S(1)}, u32[]{:S(2)}, u32[]{:S(2)}) collective-permute-start(f16[560,128]{1,0:T(8,128)(2,1)S(1)} %get-tuple-element.27), channel_id=1, source_target_pairs={{0,4},{1,5},{2,6},{3,7},{4,0},{5,1},{6,2},{7,3},{8,12},{9,13},{10,... | collective-permute-start | bytes 430088 | tf_op jit(solution)/shard_map/ppermute | solution.py:493
  46.0 8.8 %collective-permute-start.11 = (f32[640,128]{1,0:T(8,128)S(1)}, f32[640,128]{1,0:T(8,128)S(1)}, u32[]{:S(2)}, u32[]{:S(2)}) collective-permute-start(f32[640,128]{1,0:T(8,128)S(1)} %bitcast.107), channel_id=1, source_target_pairs={{0,96},{16,112},{32,0},{48,16},{64,32},{80,48},{96,64},{112,80},{1... | collective-permute-start | bytes 983048 | tf_op jit(solution)/shard_map/ppermute | solution.py:480
  46.5 18.0 %collective-permute-start.7 = (f32[640,128]{1,0:T(8,128)S(1)}, f32[640,128]{1,0:T(8,128)S(1)}, u32[]{:S(2)}, u32[]{:S(2)}) collective-permute-start(f32[640,128]{1,0:T(8,128)S(1)} %bitcast.108), channel_id=1, source_target_pairs={{0,32},{16,48},{32,64},{48,80},{64,96},{80,112},{96,0},{112,16},{1... | collective-permute-start | bytes 983048 | tf_op jit(solution)/shard_map/ppermute | solution.py:480
  48.7 16.3 %collective-permute-start.9 = (f32[640,128]{1,0:T(8,128)S(1)}, f32[640,128]{1,0:T(8,128)S(1)}, u32[]{:S(2)}, u32[]{:S(2)}) collective-permute-start(f32[640,128]{1,0:T(8,128)S(1)} %bitcast.109), channel_id=1, source_target_pairs={{0,64},{16,80},{32,96},{48,112},{64,0},{80,16},{96,32},{112,48},{1... | collective-permute-start | bytes 983048 | tf_op jit(solution)/shard_map/ppermute | solution.py:480
  54.8 11.0 %collective-permute-start.12 = (f32[640,128]{1,0:T(8,128)S(1)}, f32[640,128]{1,0:T(8,128)S(1)}, u32[]{:S(2)}, u32[]{:S(2)}) collective-permute-start(f32[640,128]{1,0:T(8,128)S(1)} %collective-permute-done.11.own_ref), channel_id=1, source_target_pairs={{0,16},{16,0},{32,48},{48,32},{64,80},{80,64},{96,112},{112,96},{1... | collective-permute-start | bytes 983048 | tf_op jit(solution)/shard_map/ppermute | solution.py:484
  64.5 2.3 %collective-permute-start.6 = (f32[640,128]{1,0:T(8,128)S(1)}, f32[640,128]{1,0:T(8,128)S(1)}, u32[]{:S(2)}, u32[]{:S(2)}) collective-permute-start(f32[640,128]{1,0:T(8,128)S(1)} %bitcast.110), channel_id=1, source_target_pairs={{0,16},{16,0},{32,48},{48,32},{64,80},{80,64},{96,112},{112,96},{1... | collective-permute-start | bytes 983048 | tf_op jit(solution)/shard_map/ppermute | solution.py:484
  64.5 2.3 %collective-permute-start.8 = (f32[640,128]{1,0:T(8,128)S(1)}, f32[640,128]{1,0:T(8,128)S(1)}, u32[]{:S(2)}, u32[]{:S(2)}) collective-permute-start(f32[640,128]{1,0:T(8,128)S(1)} %collective-permute-done.7.one_ref), channel_id=1, source_target_pairs={{0,16},{16,0},{32,48},{48,32},{64,80},{80,64},{96,112},{112,96},{1... | collective-permute-start | bytes 983048 | tf_op jit(solution)/shard_map/ppermute | solution.py:484
  65.0 3.7 %collective-permute-start.10 = (f32[640,128]{1,0:T(8,128)S(1)}, f32[640,128]{1,0:T(8,128)S(1)}, u32[]{:S(2)}, u32[]{:S(2)}) collective-permute-start(f32[640,128]{1,0:T(8,128)S(1)} %collective-permute-done.9.own_ref), channel_id=1, source_target_pairs={{0,16},{16,0},{32,48},{48,32},{64,80},{80,64},{96,112},{112,96},{1... | collective-permute-start | bytes 983048 | tf_op jit(solution)/shard_map/ppermute | solution.py:484

commit v5 on v4

--- a/solution.py
+++ b/solution.py
@@ -28,7 +28,7 @@
 VMEM_BYTES = 53 * 2**20
 
 
-FAR, NEAR = 2, (1, 3, 0)
+FAR, NEAR = 2, (1, 3)
 ORDER = (1, 3, 2, 0)
 
 
@@ -55,12 +55,13 @@
     return lax.rem(band + 1, BANDS)
 
 
-def fill_select(slot_ref, select_ref, turned_ref):
+def fill_select(slot_ref, slots, slot_sem, select_ref, turned_ref):
+    pltpu.make_async_copy(slot_ref, slots, slot_sem).wait()
     lane = lax.broadcasted_iota(jnp.int32, (8, NROW), 1)
     sub = lax.broadcasted_iota(jnp.int32, (8, NROW), 0)
     picks = []
     for pair in range(SLOTS // 2):
-        block = jnp.where(sub < BLK, slot_ref[0, 2 * pair], slot_ref[0, 2 * pair + 1])
+        block = jnp.where(sub < BLK, slots[0, 2 * pair], slots[0, 2 * pair + 1])
         row = block * BLK + (sub & (BLK - 1))
         picks.append(jnp.where(lane == row, 1.0, 0.0))
     select = jnp.concatenate(picks, 0)
@@ -103,34 +104,39 @@
     return jnp.ceil(jnp.log2(jnp.maximum(most, 2.0**-100)))[0:1]
 
 
-def far_kernel(slot_ref, slab_ref, out_ref, edges_ref, power_ref, held, select_ref, turned_ref, sems):
+def window_kernel(step, slot_ref, slab_ref, out_ref, edges_ref, power_ref, *scratch):
+    held, select_ref, turned_ref, slots, sems, slot_sem = scratch
+    pltpu.make_async_copy(slot_ref, slots, slot_sem).start()
     relay = Relay()
 
-    def fetches(other):
-        band = relay.band_at(FAR, other)
-        pieces = [
-            (before(band) * OWN + OWN - TILE, TILE, 0),
-            (band * OWN, OWN, TILE),
-            (after(band) * OWN, TILE, TILE + OWN),
-        ]
-        return [
-            pltpu.make_async_copy(
+    def fetch(other, act):
+        band = relay.band_at(step, other)
+
+        def copy(first, width, to, piece):
+            return pltpu.make_async_copy(
                 slab_ref.at[:, :, pl.ds(pl.multiple_of(first, TILE), width)],
                 held.at[other, :, :, pl.ds(to, width)],
                 sems.at[other, piece],
             )
-            for piece, (first, width, to) in enumerate(pieces)
-        ]
+
+        inside = jnp.logical_and(band > 0, band < BANDS - 1)
+
+        @pl.when(inside)
+        def _():
+            act(copy(band * OWN - TILE, OWN + 2 * TILE, 0, 0))
+
+        @pl.when(jnp.logical_not(inside))
+        def _():
+            act(copy(band * OWN, OWN, TILE, 0))
+            act(copy(before(band) * OWN + OWN - TILE, TILE, 0, 1))
+            act(copy(after(band) * OWN, TILE, TILE + OWN, 2))
 
     for other in range(SIDE):
-        for copy in fetches(other):
-            copy.start()
-    fill_select(slot_ref, select_ref, turned_ref)
+        fetch(other, lambda copy: copy.start())
+    fill_select(slot_ref, slots, slot_sem, select_ref, turned_ref)
 
     def chunk(other, most):
-        for copy in fetches(other):
-            copy.wait()
-        band = relay.band_at(FAR, other)
+        fetch(other, lambda copy: copy.wait())
         slabs = held[other].reshape(SLOTS * BLK, OWN + 2 * TILE)
         low, high, most = store_part(
             out_ref, other, slabs[:, TILE : TILE + OWN], select_ref, turned_ref, most
@@ -147,26 +153,31 @@
     power_ref[...] = power_above(most)
 
 
+def own_kernel(slot_ref, slab_ref, weight_ref, out_ref, edges_ref, power_ref, row_ref, *scratch):
+    row_ref[...] = jnp.full((1, NROW), weight_ref[0], jnp.float32)
+    window_kernel(0, slot_ref, slab_ref, out_ref, edges_ref, power_ref, *scratch)
+
+
 def near_kernel(slot_ref, slab_ref, far_edges_ref, *refs):
     out_refs, refs = refs[: len(NEAR)], refs[len(NEAR) :]
-    power_ref, held, edges, select_ref, turned_ref, sems = refs
+    power_ref, held, edges, far_edges, edge_sem, *refs = refs
+    select_ref, turned_ref, slots, sems, slot_sem = refs
+    pltpu.make_async_copy(slot_ref, slots, slot_sem).start()
     relay = Relay()
 
     def band_of(slot):
-        step = jnp.where(slot < SIDE, NEAR[0], jnp.where(slot < 2 * SIDE, NEAR[1], NEAR[2]))
+        step = jnp.where(slot < SIDE, NEAR[0], jnp.where(slot < 2 * SIDE, NEAR[1], 0))
         return relay.band_at(step, lax.rem(slot, SIDE))
 
     def fetch(slot):
         columns = pl.ds(pl.multiple_of(band_of(slot) * OWN, OWN), OWN)
         return pltpu.make_async_copy(slab_ref.at[:, :, columns], held.at[slot], sems.at[slot])
 
-    for slot in range(len(NEAR) * SIDE):
+    for slot in range(len(NEAR) * SIDE + SIDE):
         fetch(slot).start()
-    fill_select(slot_ref, select_ref, turned_ref)
-    for other in range(SIDE):
-        band = relay.band_at(FAR, other)
-        edges[relay.place(after(band)), 0:HALO] = far_edges_ref[other, 0:HALO]
-        edges[relay.place(before(band)), HALO:] = far_edges_ref[other, HALO:]
+    fill_select(slot_ref, slots, slot_sem, select_ref, turned_ref)
+    far_copy = pltpu.make_async_copy(far_edges_ref, far_edges, edge_sem)
+    far_copy.start()
 
     def chunks(index, most):
         def chunk(other, most):
@@ -185,6 +196,23 @@
     most = jnp.zeros((8, NROW), jnp.float32)
     for index in range(len(NEAR)):
         most = chunks(index, most)
+
+    def rim_chunk(other, carry):
+        slot = len(NEAR) * SIDE + other
+        fetch(slot).wait()
+        band = band_of(slot)
+        slabs = held[slot].reshape(SLOTS * BLK, OWN)
+        outer = summed_turned(outer_tiles(slabs), select_ref)
+        edges[relay.place(after(band)), 0:HALO] = outer[2 * TILE - HALO :]
+        edges[relay.place(before(band)), HALO:] = outer[:HALO]
+        return carry
+
+    lax.fori_loop(0, SIDE, rim_chunk, 0)
+    far_copy.wait()
+    for other in range(SIDE):
+        band = relay.band_at(FAR, other)
+        edges[relay.place(after(band)), 0:HALO] = far_edges[other, 0:HALO]
+        edges[relay.place(before(band)), HALO:] = far_edges[other, HALO:]
     for index, step in enumerate(NEAR):
         for other in range(SIDE):
             block = edges[SIDE * step + other]
@@ -193,19 +221,21 @@
     power_ref[...] = power_above(most)
 
 
-def sum_call(kernel, name, operands, parts, more, held, sems):
+def sum_call(kernel, name, operands, parts, more, held, sems, third=pltpu.VMEM):
     vmem = pl.BlockSpec(memory_space=pltpu.VMEM)
     return pl.pallas_call(
         kernel,
-        in_specs=[pl.BlockSpec(memory_space=pltpu.SMEM), pl.BlockSpec(memory_space=pl.ANY)]
-        + [vmem] * (len(operands) - 2),
+        in_specs=[pl.BlockSpec(memory_space=pl.ANY)] * 2
+        + [pl.BlockSpec(memory_space=third)] * (len(operands) - 2),
         out_specs=[vmem] * (parts + len(more)),
         out_shape=[pltpu.VMEM((SIDE, SPAN, NROW), jnp.float32)] * parts + more,
         scratch_shapes=held
         + [
             pltpu.VMEM((SLOTS * BLK, NROW), jnp.bfloat16),
             pltpu.VMEM((NROW, SLOTS * BLK), jnp.bfloat16),
+            pltpu.SMEM((1, SLOTS), jnp.int32),
             pltpu.SemaphoreType.DMA(sems),
+            pltpu.SemaphoreType.DMA,
         ],
         compiler_params=pltpu.CompilerParams(vmem_limit_bytes=VMEM_BYTES),
         name=name,
@@ -216,18 +246,28 @@
 EDGES = pltpu.VMEM((BANDS, 2 * HALO, NROW), jnp.float32)
 
 
+FAR_EDGES = pltpu.VMEM((SIDE, 2 * HALO, NROW), jnp.float32)
+WINDOW = pltpu.VMEM((SIDE, SLOTS, BLK, OWN + 2 * TILE), jnp.bfloat16)
+
+
 def far_sums(slabs, slot_block):
-    held = pltpu.VMEM((SIDE, SLOTS, BLK, OWN + 2 * TILE), jnp.bfloat16)
-    operands = (slot_block, slabs)
-    edges = pltpu.VMEM((SIDE, 2 * HALO, NROW), jnp.float32)
-    return sum_call(far_kernel, "far_sums", operands, 1, [edges, POWER], [held], (SIDE, 3))
+    kernel = functools.partial(window_kernel, FAR)
+    more = [FAR_EDGES, POWER]
+    return sum_call(kernel, "far_sums", (slot_block, slabs), 1, more, [WINDOW], (SIDE, 3))
+
+
+def own_sums(slabs, slot_block, weight):
+    operands = (slot_block, slabs, weight)
+    more = [FAR_EDGES, POWER, POWER]
+    return sum_call(own_kernel, "own_sums", operands, 1, more, [WINDOW], (SIDE, 3), pltpu.SMEM)
 
 
 def near_sums(slabs, slot_block, edges):
-    count = SIDE * len(NEAR)
+    count = SIDE * len(NEAR) + SIDE
     held = pltpu.VMEM((count, SLOTS, BLK, OWN), jnp.bfloat16)
     operands = (slot_block, slabs, edges)
-    return sum_call(near_kernel, "near_sums", operands, 3, [POWER], [held, EDGES], (count,))
+    scratch = [held, EDGES, FAR_EDGES, pltpu.SemaphoreType.DMA]
+    return sum_call(near_kernel, "near_sums", operands, 2, [POWER], scratch, (count,), pl.ANY)
 
 
 STEPS = SPAN // 8
@@ -272,7 +312,7 @@
 
     lax.fori_loop(0, (SWEEPS - 1) // 2, two_sweeps, 0)
     sweep(even_ref, odd_ref)
-    weight = weight_ref[0]
+    weight = jnp.broadcast_to(weight_ref[...], (8, NROW))
     for t in range(STEPS):
         plain_ref[pl.ds(t, 8, stride=STEPS)] = odd_ref[8 * t : 8 * t + 8] * weight
     for tile in range(OWN // TILE):
@@ -288,7 +328,7 @@
     return pl.pallas_call(
         relax_kernel,
         in_specs=[
-            pl.BlockSpec(memory_space=pltpu.SMEM),
+            pl.BlockSpec(memory_space=pltpu.VMEM),
             pl.BlockSpec(memory_space=pltpu.VMEM),
         ],
         out_specs=pl.BlockSpec(memory_space=pltpu.VMEM),
@@ -507,15 +547,16 @@
     return code.astype(jnp.float32) * factor
 
 
-def reduced_density(slabs, slot_block):
+def reduced_density(slabs, slot_block, weight):
     far, edges, power = far_sums(slabs, slot_block)
     code = coded(far, power)
-    code, edges = lax.optimization_barrier((code, edges))
+    code, later_slots = lax.optimization_barrier((code, slot_block))
     codes = {FAR: exchanged(code, FAR, True)}
-    *parts, power = near_sums(slabs, slot_block, edges)
+    *parts, power = near_sums(slabs, later_slots, edges)
     parts = dict(zip(NEAR, parts))
-    for step in NEAR[:2]:
+    for step in NEAR:
         codes[step] = exchanged(coded(parts[step], power), step, True)
+    parts[0], _, power, weight = own_sums(slabs, slot_block, weight)
     powers = [power_of(codes[step]) for step in ORDER[:3]]
     power = functools.reduce(jnp.maximum, powers, power)
     factors = {step: jnp.exp2(x - TOP) for step, x in zip(ORDER, powers)}
@@ -529,12 +570,12 @@
         total = sums[0]
         factor = jnp.exp2(power_of(sums[other]) - TOP)
         sums[0] = total + decoded(sums[other], factor)
-    return sums[0]
+    return sums[0], weight
 
 
 def body(slabs, slot_block, lens_weight):
-    density = reduced_density(slabs[0], slot_block)
-    messages = relaxed(density, lens_weight)
+    density, weight = reduced_density(slabs[0], slot_block, lens_weight)
+    messages = relaxed(density, weight)
     backwards = [list(range(BANDS))[::-1]]
     rows = lax.all_to_all(
         messages, "band", split_axis=0, concat_axis=0, axis_index_groups=backwards, tiled=True

time: 71.4 us -> 69.3 us (0.971)
  waiting for transfers between devices: 20.3 us -> 16.2 us
  Pallas kernels: 17.1 us -> 18.3 us
  starting transfers between devices: 21.1 us -> 21.9 us
    ppermute x6, waiting for transfers between devices: 13.6 us -> 10.1 us  [exchanged(): return lax.ppermute(block, ('plane', 'band'), route)]
    pallas_call x3 -> x4, Pallas kernels: 12.1 us -> 13.3 us  [the longest x3 9.51 us: sum_call(): pl.pallas_call(kernel, in_specs=[pl.BlockSpec(memory_space=pl.ANY)] * 2 +...]
  transfers between devices with their start and end apart: 13 -> 13, of which waited for: 6 -> 5; matrix products, arithmetic and copies ran while one was open for 1% -> 1% of each run, Pallas kernels for 11% -> 15%
where the time goes in v5:
time: 69.3 us; the launch traced here: 68.7 us
  starting transfers between devices  21.9 us (32%)
  Pallas kernels  18.3 us (26%)
  waiting for transfers between devices  16.2 us (23%)
  blocking collectives  10.3 us (15%)
  other arithmetic  1.24 us (2%)
  between operations  0.81 us (1%)
    ppermute x4, starting transfers between devices, from_other_core(): return lax.ppermute(block, 'plane', [(i, i ^ 1) for i in range(PLANES)])  10.9 us
    all_to_all x1, blocking collectives, body(): lax.all_to_all(messages, 'band', split_axis=0, concat_axis=0, axis_index_...  10.3 us
    ppermute x6, waiting for transfers between devices, exchanged(): return lax.ppermute(block, ('plane', 'band'), route)  10.1 us
    pallas_call x3, Pallas kernels, sum_call(): pl.pallas_call(kernel, in_specs=[pl.BlockSpec(memory_space=pl.ANY)] * 2 +...  9.51 us
    ppermute x6, starting transfers between devices, exchanged(): return lax.ppermute(block, ('plane', 'band'), route)  8.26 us
    ppermute x3, waiting for transfers between devices, from_chip(): lax.ppermute(block, 'plane', [(i, (i + 2 * back) % PLANES) for i in range...  5.48 us
    pallas_call x3, Pallas kernels, chain_call(): pl.pallas_call(kernel, in_specs=[vmem] * len(operands), out_specs=pl.Bloc...  4.98 us
    pallas_call x1, Pallas kernels, relaxed(): pl.pallas_call(relax_kernel, in_specs=[pl.BlockSpec(memory_space=pltpu.VM...  3.8 us
  transfers between devices with their start and end apart: 13, of which 5 were waited for; matrix products, arithmetic and copies ran while one was open for 1% of the time, Pallas kernels for 15%

profile of v5, /device:TPU:7, one launch (start us, length us, event | category | flops | bytes accessed | tf_op | source)
XLA Modules:
  0.0 68.7 jit_solution(12922689926078538648)
XLA Ops:
  0.0 2.4 %far_sums.1 = (f32[4,560,128]{2,1,0:T(8,128)S(1)}, f32[4,48,128]{2,1,0:T(8,128)S(1)}, f32[1,128]{1,0:T(1,128)S(1)}) custom-call(s32[1,64]{1,0:T(1,128)} %slot_ref.4, bf16[64,4,8192]{2,1,0:T(4,128)(2,1)} %bitcast.114), custom_call_target="tpu_custom_call" | custom-call | tf_op jit(solution)/shard_map/far_sums/pallas_call | solution.py:226
  2.6 3.0 %collective-permute-start.2 = (f16[4,560,128]{2,1,0:T(8,128)(2,1)S(1)}, f16[4,560,128]{2,1,0:T(8,128)(2,1)S(1)}, u32[]{:S(2)}, u32[]{:S(2)}) collective-permute-start(f16[4,560,128]{2,1,0:T(8,128)(2,1)S(1)} %select_convert_fusion.2), channel_id=1, source_target_pairs={{0,2},{1,3},{2,0},{3,1},{4,6},{5,7},{6,4},{7,5},{8,10},{9,11},{10,... | collective-permute-start | bytes 1720328 | tf_op jit(solution)/shard_map/ppermute | solution.py:533
  5.6 4.2 %near_sums.1 = (f32[4,560,128]{2,1,0:T(8,128)S(1)}, f32[4,560,128]{2,1,0:T(8,128)S(1)}, f32[1,128]{1,0:T(1,128)S(1)}) custom-call(s32[1,64]{1,0:T(1,128)} %slot_ref.4, bf16[64,4,8192]{2,1,0:T(4,128)(2,1)} %bitcast.115, f32[4,48,128]{2,1,0:T(8,128)} %copy-done), custom_call_target="tpu_custom_call" | custom-call | tf_op jit(solution)/shard_map/near_sums/pallas_call | solution.py:226
  9.9 0.4 select_convert_fusion.1
  10.2 0.9 %collective-permute-start = (f16[4,560,128]{2,1,0:T(8,128)(2,1)S(1)}, f16[4,560,128]{2,1,0:T(8,128)(2,1)S(1)}, u32[]{:S(2)}, u32[]{:S(2)}) collective-permute-start(f16[4,560,128]{2,1,0:T(8,128)(2,1)S(1)} %get-tuple-element.32), channel_id=1, source_target_pairs={{0,3},{1,2},{2,1},{3,0},{4,7},{5,6},{6,5},{7,4},{8,11},{9,10},{10,... | collective-permute-start | bytes 1720328 | tf_op jit(solution)/shard_map/ppermute | solution.py:533
  11.8 2.9 %own_sums.1 = (f32[4,560,128]{2,1,0:T(8,128)S(1)}, f32[4,48,128]{2,1,0:T(8,128)}, f32[1,128]{1,0:T(1,128)S(1)}, f32[1,128]{1,0:T(1,128)S(1)}) custom-call(s32[1,64]{1,0:T(1,128)} %slot_ref.4, bf16[64,4,8192]{2,1,0:T(4,128)(2,1)} %bitcast.116, f32[1]{0:T(128)S(6)} %copy.4.weight_ref), custom_call_target="tpu_custom_call" | custom-call | tf_op jit(solution)/shard_map/own_sums/pallas_call | solution.py:226
  14.7 5.7 %collective-permute-done = f16[4,560,128]{2,1,0:T(8,128)(2,1)S(1)} collective-permute-done((f16[4,560,128]{2,1,0:T(8,128)(2,1)S(1)}, f16[4,560,128]{2,1,0:T(8,128)(2,1)S(1)}, u32[]{:S(2)}, u32[]{:S(2)}) %collective-permute-start) | collective-permute-done | bytes 573472 | tf_op jit(solution)/shard_map/ppermute | solution.py:533
  20.4 0.4 fusion.15
  20.8 3.4 %collective-permute-start.3 = (f16[560,128]{1,0:T(8,128)(2,1)S(1)}, f16[560,128]{1,0:T(8,128)(2,1)S(1)}, u32[]{:S(2)}, u32[]{:S(2)}) collective-permute-start(f16[560,128]{1,0:T(8,128)(2,1)S(1)} %get-tuple-element.29), channel_id=1, source_target_pairs={{0,8},{1,9},{2,10},{3,11},{4,12},{5,13},{6,14},{7,15},{8,0},{9,1},... | collective-permute-start | bytes 430088 | tf_op jit(solution)/shard_map/ppermute | solution.py:533
  24.3 0.5 collective-permute-start.5
  24.8 0.5 collective-permute-start.4
  25.2 1.5 %collective-permute-done.3 = f16[560,128]{1,0:T(8,128)(2,1)S(1)} collective-permute-done((f16[560,128]{1,0:T(8,128)(2,1)S(1)}, f16[560,128]{1,0:T(8,128)(2,1)S(1)}, u32[]{:S(2)}, u32[]{:S(2)}) %collective-permute-start.3) | collective-permute-done | bytes 143392 | tf_op jit(solution)/shard_map/ppermute | solution.py:533
  26.8 2.9 %collective-permute-done.5 = f16[560,128]{1,0:T(8,128)(2,1)S(1)} collective-permute-done((f16[560,128]{1,0:T(8,128)(2,1)S(1)}, f16[560,128]{1,0:T(8,128)(2,1)S(1)}, u32[]{:S(2)}, u32[]{:S(2)}) %collective-permute-start.5) | collective-permute-done | bytes 143392 | tf_op jit(solution)/shard_map/ppermute | solution.py:533
  29.8 3.8 %relaxed.1 = f32[16,40,128]{2,1,0:T(8,128)S(1)} custom-call(f32[1,128]{1,0:T(1,128)S(1)} %get-tuple-element.16.weight_ref, f32[560,128]{1,0:T(8,128)S(1)} %fusion.21.part_ref), custom_call_target="tpu_custom_call" | custom-call | tf_op jit(solution)/shard_map/relaxed/pallas_call | solution.py:328
  33.6 10.3 %all_to_all.5 = f32[16,40,128]{2,1,0:T(8,128)S(1)} all-to-all(f32[16,40,128]{2,1,0:T(8,128)S(1)} %relaxed.1), channel_id=1, replica_groups={{15,14,13,12,11,10,9,8,7,6,5,4,3,2,1,0},{31,30,29,28,27,26,25,24,23,22,..., dimensions={0} | all-to-all | bytes 655360 | tf_op jit(solution)/shard_map/all_to_all | solution.py:580
  43.9 0.6 collective-permute-start.11
  44.5 2.1 %collective-permute-start.7 = (f32[640,128]{1,0:T(8,128)S(1)}, f32[640,128]{1,0:T(8,128)S(1)}, u32[]{:S(2)}, u32[]{:S(2)}) collective-permute-start(f32[640,128]{1,0:T(8,128)S(1)} %bitcast.108), channel_id=1, source_target_pairs={{0,32},{16,48},{32,64},{48,80},{64,96},{80,112},{96,0},{112,16},{1... | collective-permute-start | bytes 983048 | tf_op jit(solution)/shard_map/ppermute | solution.py:520
  46.6 5.5 %collective-permute-done.11.own_ref = f32[640,128]{1,0:T(8,128)S(1)} collective-permute-done((f32[640,128]{1,0:T(8,128)S(1)}, f32[640,128]{1,0:T(8,128)S(1)}, u32[]{:S(2)}, u32[]{:S(2)}) %collective-permute-start.11) | collective-permute-done | bytes 327712 | tf_op jit(solution)/shard_map/ppermute | solution.py:520
  52.1 10.3 %collective-permute-start.12 = (f32[640,128]{1,0:T(8,128)S(1)}, f32[640,128]{1,0:T(8,128)S(1)}, u32[]{:S(2)}, u32[]{:S(2)}) collective-permute-start(f32[640,128]{1,0:T(8,128)S(1)} %collective-permute-done.11.own_ref), channel_id=1, source_target_pairs={{0,16},{16,0},{32,48},{48,32},{64,80},{80,64},{96,112},{112,96},{1... | collective-permute-start | bytes 983048 | tf_op jit(solution)/shard_map/ppermute | solution.py:524
  62.4 0.5 collective-permute-start.8
  63.0 0.7 collective-permute-done.12.other_ref
  63.7 1.0 %chain_first.1.first_ref = f32[6,8,8192]{2,1,0:T(8,128)S(1)} custom-call(f32[640,128]{1,0:T(8,128)S(1)} %collective-permute-done.11.own_ref, f32[640,128]{1,0:T(8,128)S(1)} %collective-permute-done.12.other_ref), custom_call_target="tpu_custom_call" | custom-call | flops 5242880 | bytes 2228224 | tf_op jit(solution)/shard_map/chain_first/pallas_call | solution.py:503
  64.7 1.9 %chain_recent.1.state_ref = f32[6,8,8192]{2,1,0:T(8,128)S(1)} custom-call(f32[640,128]{1,0:T(8,128)S(1)} %bitcast.111, f32[640,128]{1,0:T(8,128)S(1)} %collective-permute-done.6.other_ref, f32[640,128]{1,0:T(8,128)S(1)} %collective-permute-done.7.one_ref, f32[640,128]{1,0:T(8,128)S(1)} %collective-permute-done.8.one_other_ref), custom_call_target="tpu_custom_call" | custom-call | flops 5242880 | bytes 2883584 | tf_op jit(solution)/shard_map/chain_recent/pallas_call | solution.py:503
  66.6 2.1 %chain_finish.1 = f32[1,6,8,8192]{3,2,1,0:T(8,128)} custom-call(f32[6,8,8192]{2,1,0:T(8,128)S(1)} %chain_recent.1.state_ref, f32[640,128]{1,0:T(8,128)S(1)} %collective-permute-done.9.own_ref, f32[640,128]{1,0:T(8,128)S(1)} %collective-permute-done.10.other_ref, f32[6,8,8192]{2,1,0:T(8,128)S(1)} %chain_first.1.first_ref), custom_call_target="tpu_custom_call" | custom-call | flops 5242880 | bytes 5373952 | tf_op jit(solution)/shard_map/chain_finish/pallas_call | solution.py:503
  (26 shorter events, 0.6 us)
Async XLA Ops:
  2.4 3.2 %copy-start = (f32[4,48,128]{2,1,0:T(8,128)}, f32[4,48,128]{2,1,0:T(8,128)S(1)}, u32[]{:S(2)}) copy-start(f32[4,48,128]{2,1,0:T(8,128)S(1)} %get-tuple-element.21.far_edges_ref) | copy-start | bytes 294916
  2.6 12.0 %collective-permute-start.2 = (f16[4,560,128]{2,1,0:T(8,128)(2,1)S(1)}, f16[4,560,128]{2,1,0:T(8,128)(2,1)S(1)}, u32[]{:S(2)}, u32[]{:S(2)}) collective-permute-start(f16[4,560,128]{2,1,0:T(8,128)(2,1)S(1)} %select_convert_fusion.2), channel_id=1, source_target_pairs={{0,2},{1,3},{2,0},{3,1},{4,6},{5,7},{6,4},{7,5},{8,10},{9,11},{10,... | collective-permute-start | bytes 1720328 | tf_op jit(solution)/shard_map/ppermute | solution.py:533
  10.2 10.1 %collective-permute-start = (f16[4,560,128]{2,1,0:T(8,128)(2,1)S(1)}, f16[4,560,128]{2,1,0:T(8,128)(2,1)S(1)}, u32[]{:S(2)}, u32[]{:S(2)}) collective-permute-start(f16[4,560,128]{2,1,0:T(8,128)(2,1)S(1)} %get-tuple-element.32), channel_id=1, source_target_pairs={{0,3},{1,2},{2,1},{3,0},{4,7},{5,6},{6,5},{7,4},{8,11},{9,10},{10,... | collective-permute-start | bytes 1720328 | tf_op jit(solution)/shard_map/ppermute | solution.py:533
  11.1 9.3 %collective-permute-start.1 = (f16[4,560,128]{2,1,0:T(8,128)(2,1)S(1)}, f16[4,560,128]{2,1,0:T(8,128)(2,1)S(1)}, u32[]{:S(2)}, u32[]{:S(2)}) collective-permute-start(f16[4,560,128]{2,1,0:T(8,128)(2,1)S(1)} %get-tuple-element.33), channel_id=1, source_target_pairs={{0,1},{1,0},{2,3},{3,2},{4,5},{5,4},{6,7},{7,6},{8,9},{9,8},{10,11... | collective-permute-start | bytes 1720328 | tf_op jit(solution)/shard_map/ppermute | solution.py:533
  20.8 5.9 %collective-permute-start.3 = (f16[560,128]{1,0:T(8,128)(2,1)S(1)}, f16[560,128]{1,0:T(8,128)(2,1)S(1)}, u32[]{:S(2)}, u32[]{:S(2)}) collective-permute-start(f16[560,128]{1,0:T(8,128)(2,1)S(1)} %get-tuple-element.29), channel_id=1, source_target_pairs={{0,8},{1,9},{2,10},{3,11},{4,12},{5,13},{6,14},{7,15},{8,0},{9,1},... | collective-permute-start | bytes 430088 | tf_op jit(solution)/shard_map/ppermute | solution.py:533
  24.3 5.4 %collective-permute-start.5 = (f16[560,128]{1,0:T(8,128)(2,1)S(1)}, f16[560,128]{1,0:T(8,128)(2,1)S(1)}, u32[]{:S(2)}, u32[]{:S(2)}) collective-permute-start(f16[560,128]{1,0:T(8,128)(2,1)S(1)} %get-tuple-element.30), channel_id=1, source_target_pairs={{0,12},{1,13},{2,14},{3,15},{4,8},{5,9},{6,10},{7,11},{8,4},{9,5},... | collective-permute-start | bytes 430088 | tf_op jit(solution)/shard_map/ppermute | solution.py:533
  24.8 4.9 %collective-permute-start.4 = (f16[560,128]{1,0:T(8,128)(2,1)S(1)}, f16[560,128]{1,0:T(8,128)(2,1)S(1)}, u32[]{:S(2)}, u32[]{:S(2)}) collective-permute-start(f16[560,128]{1,0:T(8,128)(2,1)S(1)} %get-tuple-element.31), channel_id=1, source_target_pairs={{0,4},{1,5},{2,6},{3,7},{4,0},{5,1},{6,2},{7,3},{8,12},{9,13},{10,... | collective-permute-start | bytes 430088 | tf_op jit(solution)/shard_map/ppermute | solution.py:533
  43.9 8.2 %collective-permute-start.11 = (f32[640,128]{1,0:T(8,128)S(1)}, f32[640,128]{1,0:T(8,128)S(1)}, u32[]{:S(2)}, u32[]{:S(2)}) collective-permute-start(f32[640,128]{1,0:T(8,128)S(1)} %bitcast.107), channel_id=1, source_target_pairs={{0,96},{16,112},{32,0},{48,16},{64,32},{80,48},{96,64},{112,80},{1... | collective-permute-start | bytes 983048 | tf_op jit(solution)/shard_map/ppermute | solution.py:520
  44.5 18.0 %collective-permute-start.7 = (f32[640,128]{1,0:T(8,128)S(1)}, f32[640,128]{1,0:T(8,128)S(1)}, u32[]{:S(2)}, u32[]{:S(2)}) collective-permute-start(f32[640,128]{1,0:T(8,128)S(1)} %bitcast.108), channel_id=1, source_target_pairs={{0,32},{16,48},{32,64},{48,80},{64,96},{80,112},{96,0},{112,16},{1... | collective-permute-start | bytes 983048 | tf_op jit(solution)/shard_map/ppermute | solution.py:520
  46.6 16.3 %collective-permute-start.9 = (f32[640,128]{1,0:T(8,128)S(1)}, f32[640,128]{1,0:T(8,128)S(1)}, u32[]{:S(2)}, u32[]{:S(2)}) collective-permute-start(f32[640,128]{1,0:T(8,128)S(1)} %bitcast.109), channel_id=1, source_target_pairs={{0,64},{16,80},{32,96},{48,112},{64,0},{80,16},{96,32},{112,48},{1... | collective-permute-start | bytes 983048 | tf_op jit(solution)/shard_map/ppermute | solution.py:520
  52.1 11.6 %collective-permute-start.12 = (f32[640,128]{1,0:T(8,128)S(1)}, f32[640,128]{1,0:T(8,128)S(1)}, u32[]{:S(2)}, u32[]{:S(2)}) collective-permute-start(f32[640,128]{1,0:T(8,128)S(1)} %collective-permute-done.11.own_ref), channel_id=1, source_target_pairs={{0,16},{16,0},{32,48},{48,32},{64,80},{80,64},{96,112},{112,96},{1... | collective-permute-start | bytes 983048 | tf_op jit(solution)/shard_map/ppermute | solution.py:524
  62.4 2.3 %collective-permute-start.6 = (f32[640,128]{1,0:T(8,128)S(1)}, f32[640,128]{1,0:T(8,128)S(1)}, u32[]{:S(2)}, u32[]{:S(2)}) collective-permute-start(f32[640,128]{1,0:T(8,128)S(1)} %bitcast.110), channel_id=1, source_target_pairs={{0,16},{16,0},{32,48},{48,32},{64,80},{80,64},{96,112},{112,96},{1... | collective-permute-start | bytes 983048 | tf_op jit(solution)/shard_map/ppermute | solution.py:524
  62.4 2.3 %collective-permute-start.8 = (f32[640,128]{1,0:T(8,128)S(1)}, f32[640,128]{1,0:T(8,128)S(1)}, u32[]{:S(2)}, u32[]{:S(2)}) collective-permute-start(f32[640,128]{1,0:T(8,128)S(1)} %collective-permute-done.7.one_ref), channel_id=1, source_target_pairs={{0,16},{16,0},{32,48},{48,32},{64,80},{80,64},{96,112},{112,96},{1... | collective-permute-start | bytes 983048 | tf_op jit(solution)/shard_map/ppermute | solution.py:524
  62.9 3.7 %collective-permute-start.10 = (f32[640,128]{1,0:T(8,128)S(1)}, f32[640,128]{1,0:T(8,128)S(1)}, u32[]{:S(2)}, u32[]{:S(2)}) collective-permute-start(f32[640,128]{1,0:T(8,128)S(1)} %collective-permute-done.9.own_ref), channel_id=1, source_target_pairs={{0,16},{16,0},{32,48},{48,32},{64,80},{80,64},{96,112},{112,96},{1... | collective-permute-start | bytes 983048 | tf_op jit(solution)/shard_map/ppermute | solution.py:524

commit v6 on v5

--- a/solution.py
+++ b/solution.py
@@ -396,7 +396,7 @@
     )
 
 
-def chain_step(state_ref, out_ref, pieces, first_ref=None, final_ref=None, sems=None):
+def chain_step(state_ref, out_ref, pieces, middle_ref=None, final_ref=None, sems=None):
     lane = lax.broadcasted_iota(jnp.int32, (R, TILE), 1)
     is_first = lane == 0
     is_last = lane == TILE - 1
@@ -417,10 +417,11 @@
             else:
                 state = tuple(state_ref[entry, :, columns[t]] for entry in range(6))
                 rest = maps
+            if middle_ref is not None:
+                middle = [middle_ref[entry, :, columns[t]] for entry in range(6)]
+                state = after_state(state, middle)
             for one in rest:
                 state = after_map(state, one[t])
-            if first_ref is not None:
-                state = after_state(state, [first_ref[entry, :, columns[t]] for entry in range(6)])
             if final_ref is not None:
                 state = tuple(x - 1.0 if e in (0, 3) else x for e, x in enumerate(state))
             for entry in range(6):
@@ -465,7 +466,7 @@
             chain_step(None, out_ref, near + far)
 
 
-def first_kernel(back, own_ref, other_ref, out_ref):
+def middle_kernel(back, own_ref, other_ref, out_ref):
     me = lax.axis_index("plane")
     chip, core = me // 2, lax.rem(me, 2)
     for which in (0, 1):
@@ -476,25 +477,25 @@
             chain_step(None, out_ref, pieces)
 
 
-def finish_kernel(back, state_ref, own_ref, other_ref, first_ref, final_ref, out_ref, sems):
+def finish_kernel(back, state_ref, own_ref, other_ref, middle_ref, final_ref, out_ref, sems):
     me = lax.axis_index("plane")
     chip, core = me // 2, lax.rem(me, 2)
     final_ref = final_ref.at[0]
 
-    @pl.when(chip < back)
+    @pl.when(chip < back - 1)
     def _():
         chain_step(state_ref, out_ref, [], None, final_ref, sems)
 
+    @pl.when(chip == back - 1)
+    def _():
+        chain_step(state_ref, out_ref, [], middle_ref, final_ref, sems)
+
     for which in (0, 1):
         pieces = [own_ref, other_ref] if which else [other_ref, own_ref]
 
-        @pl.when(jnp.logical_and(chip == back, core == which))
+        @pl.when(jnp.logical_and(chip >= back, core == which))
         def _():
-            chain_step(state_ref, out_ref, pieces, None, final_ref, sems)
-
-        @pl.when(jnp.logical_and(chip > back, core == which))
-        def _():
-            chain_step(state_ref, out_ref, pieces, first_ref, final_ref, sems)
+            chain_step(state_ref, out_ref, pieces, middle_ref, final_ref, sems)
 
 
 def chain_call(kernel, name, operands, shape, last=False):
@@ -586,10 +587,10 @@
     recent = functools.partial(recent_kernel, 1)
     operands = (rows, from_other_core(rows), one, from_other_core(one))
     recent = chain_call(recent, "chain_recent", operands, shape)
-    first = functools.partial(first_kernel, 3)
-    first = chain_call(first, "chain_first", (three, from_other_core(three)), shape)
-    finish = functools.partial(finish_kernel, 2)
-    operands = (recent, two, from_other_core(two), first)
+    middle = functools.partial(middle_kernel, 2)
+    middle = chain_call(middle, "chain_middle", (two, from_other_core(two)), shape)
+    finish = functools.partial(finish_kernel, 3)
+    operands = (recent, three, from_other_core(three), middle)
     return chain_call(finish, "chain_finish", operands, (1,) + shape, last=True)
 
 

time: 69.3 us -> 67.8 us (0.978)
  waiting for transfers between devices: 16.2 us -> 14.7 us
    ppermute x3, waiting for transfers between devices: 5.48 us -> 4.58 us  [from_chip(): lax.ppermute(block, 'plane', [(i, (i + 2 * back) % PLANES) for i in range...]
  transfers between devices with their start and end apart: 13 -> 13, of which waited for: 5 -> 4; matrix products, arithmetic and copies ran while one was open for 1% -> 1% of each run, Pallas kernels for 15% -> 15%
where the time goes in v6:
time: 67.8 us; the launch traced here: 67.7 us
  starting transfers between devices  22.3 us (33%)
  Pallas kernels  18.3 us (27%)
  waiting for transfers between devices  14.7 us (22%)
  blocking collectives  10.3 us (15%)
  other arithmetic  1.24 us (2%)
  between operations  0.81 us (1%)
    ppermute x4, starting transfers between devices, from_other_core(): return lax.ppermute(block, 'plane', [(i, i ^ 1) for i in range(PLANES)])  11.1 us
    all_to_all x1, blocking collectives, body(): lax.all_to_all(messages, 'band', split_axis=0, concat_axis=0, axis_index_...  10.3 us
    ppermute x6, waiting for transfers between devices, exchanged(): return lax.ppermute(block, ('plane', 'band'), route)  10.1 us
    pallas_call x3, Pallas kernels, sum_call(): pl.pallas_call(kernel, in_specs=[pl.BlockSpec(memory_space=pl.ANY)] * 2 +...  9.51 us
    ppermute x6, starting transfers between devices, exchanged(): return lax.ppermute(block, ('plane', 'band'), route)  8.26 us
    pallas_call x3, Pallas kernels, chain_call(): pl.pallas_call(kernel, in_specs=[vmem] * len(operands), out_specs=pl.Bloc...  5.02 us
    ppermute x3, waiting for transfers between devices, from_chip(): lax.ppermute(block, 'plane', [(i, (i + 2 * back) % PLANES) for i in range...  4.58 us
    pallas_call x1, Pallas kernels, relaxed(): pl.pallas_call(relax_kernel, in_specs=[pl.BlockSpec(memory_space=pltpu.VM...  3.8 us
  transfers between devices with their start and end apart: 13, of which 4 were waited for; matrix products, arithmetic and copies ran while one was open for 1% of the time, Pallas kernels for 15%

profile of v6, /device:TPU:7, one launch (start us, length us, event | category | flops | bytes accessed | tf_op | source)
XLA Modules:
  0.0 67.7 jit_solution(16792726284581460909)
XLA Ops:
  0.0 2.4 %far_sums.1 = (f32[4,560,128]{2,1,0:T(8,128)S(1)}, f32[4,48,128]{2,1,0:T(8,128)S(1)}, f32[1,128]{1,0:T(1,128)S(1)}) custom-call(s32[1,64]{1,0:T(1,128)} %slot_ref.4, bf16[64,4,8192]{2,1,0:T(4,128)(2,1)} %bitcast.114), custom_call_target="tpu_custom_call" | custom-call | tf_op jit(solution)/shard_map/far_sums/pallas_call | solution.py:226
  2.6 3.0 %collective-permute-start.2 = (f16[4,560,128]{2,1,0:T(8,128)(2,1)S(1)}, f16[4,560,128]{2,1,0:T(8,128)(2,1)S(1)}, u32[]{:S(2)}, u32[]{:S(2)}) collective-permute-start(f16[4,560,128]{2,1,0:T(8,128)(2,1)S(1)} %select_convert_fusion.2), channel_id=1, source_target_pairs={{0,2},{1,3},{2,0},{3,1},{4,6},{5,7},{6,4},{7,5},{8,10},{9,11},{10,... | collective-permute-start | bytes 1720328 | tf_op jit(solution)/shard_map/ppermute | solution.py:534
  5.6 4.2 %near_sums.1 = (f32[4,560,128]{2,1,0:T(8,128)S(1)}, f32[4,560,128]{2,1,0:T(8,128)S(1)}, f32[1,128]{1,0:T(1,128)S(1)}) custom-call(s32[1,64]{1,0:T(1,128)} %slot_ref.4, bf16[64,4,8192]{2,1,0:T(4,128)(2,1)} %bitcast.115, f32[4,48,128]{2,1,0:T(8,128)} %copy-done), custom_call_target="tpu_custom_call" | custom-call | tf_op jit(solution)/shard_map/near_sums/pallas_call | solution.py:226
  9.9 0.4 select_convert_fusion.1
  10.2 0.9 %collective-permute-start = (f16[4,560,128]{2,1,0:T(8,128)(2,1)S(1)}, f16[4,560,128]{2,1,0:T(8,128)(2,1)S(1)}, u32[]{:S(2)}, u32[]{:S(2)}) collective-permute-start(f16[4,560,128]{2,1,0:T(8,128)(2,1)S(1)} %get-tuple-element.32), channel_id=1, source_target_pairs={{0,3},{1,2},{2,1},{3,0},{4,7},{5,6},{6,5},{7,4},{8,11},{9,10},{10,... | collective-permute-start | bytes 1720328 | tf_op jit(solution)/shard_map/ppermute | solution.py:534
  11.8 2.9 %own_sums.1 = (f32[4,560,128]{2,1,0:T(8,128)S(1)}, f32[4,48,128]{2,1,0:T(8,128)}, f32[1,128]{1,0:T(1,128)S(1)}, f32[1,128]{1,0:T(1,128)S(1)}) custom-call(s32[1,64]{1,0:T(1,128)} %slot_ref.4, bf16[64,4,8192]{2,1,0:T(4,128)(2,1)} %bitcast.116, f32[1]{0:T(128)S(6)} %copy.4.weight_ref), custom_call_target="tpu_custom_call" | custom-call | tf_op jit(solution)/shard_map/own_sums/pallas_call | solution.py:226
  14.7 5.7 %collective-permute-done = f16[4,560,128]{2,1,0:T(8,128)(2,1)S(1)} collective-permute-done((f16[4,560,128]{2,1,0:T(8,128)(2,1)S(1)}, f16[4,560,128]{2,1,0:T(8,128)(2,1)S(1)}, u32[]{:S(2)}, u32[]{:S(2)}) %collective-permute-start) | collective-permute-done | bytes 573472 | tf_op jit(solution)/shard_map/ppermute | solution.py:534
  20.4 0.4 fusion.15
  20.8 3.4 %collective-permute-start.3 = (f16[560,128]{1,0:T(8,128)(2,1)S(1)}, f16[560,128]{1,0:T(8,128)(2,1)S(1)}, u32[]{:S(2)}, u32[]{:S(2)}) collective-permute-start(f16[560,128]{1,0:T(8,128)(2,1)S(1)} %get-tuple-element.29), channel_id=1, source_target_pairs={{0,8},{1,9},{2,10},{3,11},{4,12},{5,13},{6,14},{7,15},{8,0},{9,1},... | collective-permute-start | bytes 430088 | tf_op jit(solution)/shard_map/ppermute | solution.py:534
  24.3 0.5 collective-permute-start.5
  24.8 0.5 collective-permute-start.4
  25.2 1.5 %collective-permute-done.3 = f16[560,128]{1,0:T(8,128)(2,1)S(1)} collective-permute-done((f16[560,128]{1,0:T(8,128)(2,1)S(1)}, f16[560,128]{1,0:T(8,128)(2,1)S(1)}, u32[]{:S(2)}, u32[]{:S(2)}) %collective-permute-start.3) | collective-permute-done | bytes 143392 | tf_op jit(solution)/shard_map/ppermute | solution.py:534
  26.8 2.9 %collective-permute-done.5 = f16[560,128]{1,0:T(8,128)(2,1)S(1)} collective-permute-done((f16[560,128]{1,0:T(8,128)(2,1)S(1)}, f16[560,128]{1,0:T(8,128)(2,1)S(1)}, u32[]{:S(2)}, u32[]{:S(2)}) %collective-permute-start.5) | collective-permute-done | bytes 143392 | tf_op jit(solution)/shard_map/ppermute | solution.py:534
  29.8 3.8 %relaxed.1 = f32[16,40,128]{2,1,0:T(8,128)S(1)} custom-call(f32[1,128]{1,0:T(1,128)S(1)} %get-tuple-element.16.weight_ref, f32[560,128]{1,0:T(8,128)S(1)} %fusion.21.part_ref), custom_call_target="tpu_custom_call" | custom-call | tf_op jit(solution)/shard_map/relaxed/pallas_call | solution.py:328
  33.6 10.3 %all_to_all.5 = f32[16,40,128]{2,1,0:T(8,128)S(1)} all-to-all(f32[16,40,128]{2,1,0:T(8,128)S(1)} %relaxed.1), channel_id=1, replica_groups={{15,14,13,12,11,10,9,8,7,6,5,4,3,2,1,0},{31,30,29,28,27,26,25,24,23,22,..., dimensions={0} | all-to-all | bytes 655360 | tf_op jit(solution)/shard_map/all_to_all | solution.py:581
  43.9 1.1 %collective-permute-start.11 = (f32[640,128]{1,0:T(8,128)S(1)}, f32[640,128]{1,0:T(8,128)S(1)}, u32[]{:S(2)}, u32[]{:S(2)}) collective-permute-start(f32[640,128]{1,0:T(8,128)S(1)} %bitcast.107), channel_id=1, source_target_pairs={{0,64},{16,80},{32,96},{48,112},{64,0},{80,16},{96,32},{112,48},{1... | collective-permute-start | bytes 983048 | tf_op jit(solution)/shard_map/ppermute | solution.py:521
  45.1 1.8 %collective-permute-start.7 = (f32[640,128]{1,0:T(8,128)S(1)}, f32[640,128]{1,0:T(8,128)S(1)}, u32[]{:S(2)}, u32[]{:S(2)}) collective-permute-start(f32[640,128]{1,0:T(8,128)S(1)} %bitcast.108), channel_id=1, source_target_pairs={{0,32},{16,48},{32,64},{48,80},{64,96},{80,112},{96,0},{112,16},{1... | collective-permute-start | bytes 983048 | tf_op jit(solution)/shard_map/ppermute | solution.py:521
  46.9 4.6 %collective-permute-done.11.own_ref = f32[640,128]{1,0:T(8,128)S(1)} collective-permute-done((f32[640,128]{1,0:T(8,128)S(1)}, f32[640,128]{1,0:T(8,128)S(1)}, u32[]{:S(2)}, u32[]{:S(2)}) %collective-permute-start.11) | collective-permute-done | bytes 327712 | tf_op jit(solution)/shard_map/ppermute | solution.py:521
  51.5 7.7 %collective-permute-start.12 = (f32[640,128]{1,0:T(8,128)S(1)}, f32[640,128]{1,0:T(8,128)S(1)}, u32[]{:S(2)}, u32[]{:S(2)}) collective-permute-start(f32[640,128]{1,0:T(8,128)S(1)} %collective-permute-done.11.own_ref), channel_id=1, source_target_pairs={{0,16},{16,0},{32,48},{48,32},{64,80},{80,64},{96,112},{112,96},{1... | collective-permute-start | bytes 983048 | tf_op jit(solution)/shard_map/ppermute | solution.py:525
  59.2 1.3 %collective-permute-start.8 = (f32[640,128]{1,0:T(8,128)S(1)}, f32[640,128]{1,0:T(8,128)S(1)}, u32[]{:S(2)}, u32[]{:S(2)}) collective-permute-start(f32[640,128]{1,0:T(8,128)S(1)} %collective-permute-done.7.one_ref), channel_id=1, source_target_pairs={{0,16},{16,0},{32,48},{48,32},{64,80},{80,64},{96,112},{112,96},{1... | collective-permute-start | bytes 983048 | tf_op jit(solution)/shard_map/ppermute | solution.py:525
  60.4 2.1 %collective-permute-start.10 = (f32[640,128]{1,0:T(8,128)S(1)}, f32[640,128]{1,0:T(8,128)S(1)}, u32[]{:S(2)}, u32[]{:S(2)}) collective-permute-start(f32[640,128]{1,0:T(8,128)S(1)} %collective-permute-done.9.own_ref), channel_id=1, source_target_pairs={{0,16},{16,0},{32,48},{48,32},{64,80},{80,64},{96,112},{112,96},{1... | collective-permute-start | bytes 983048 | tf_op jit(solution)/shard_map/ppermute | solution.py:525
  62.6 1.0 %chain_middle.1.middle_ref = f32[6,8,8192]{2,1,0:T(8,128)S(1)} custom-call(f32[640,128]{1,0:T(8,128)S(1)} %collective-permute-done.11.own_ref, f32[640,128]{1,0:T(8,128)S(1)} %collective-permute-done.12.other_ref), custom_call_target="tpu_custom_call" | custom-call | flops 5242880 | bytes 2228224 | tf_op jit(solution)/shard_map/chain_middle/pallas_call | solution.py:504
  63.6 1.9 %chain_recent.1.state_ref = f32[6,8,8192]{2,1,0:T(8,128)S(1)} custom-call(f32[640,128]{1,0:T(8,128)S(1)} %bitcast.111, f32[640,128]{1,0:T(8,128)S(1)} %collective-permute-done.6.other_ref, f32[640,128]{1,0:T(8,128)S(1)} %collective-permute-done.7.one_ref, f32[640,128]{1,0:T(8,128)S(1)} %collective-permute-done.8.one_other_ref), custom_call_target="tpu_custom_call" | custom-call | flops 5242880 | bytes 2883584 | tf_op jit(solution)/shard_map/chain_recent/pallas_call | solution.py:504
  65.6 2.1 %chain_finish.1 = f32[1,6,8,8192]{3,2,1,0:T(8,128)} custom-call(f32[6,8,8192]{2,1,0:T(8,128)S(1)} %chain_recent.1.state_ref, f32[640,128]{1,0:T(8,128)S(1)} %collective-permute-done.9.own_ref, f32[640,128]{1,0:T(8,128)S(1)} %collective-permute-done.10.other_ref, f32[6,8,8192]{2,1,0:T(8,128)S(1)} %chain_middle.1.middle_ref), custom_call_target="tpu_custom_call" | custom-call | flops 5242880 | bytes 5373952 | tf_op jit(solution)/shard_map/chain_finish/pallas_call | solution.py:504
  (26 shorter events, 0.5 us)
Async XLA Ops:
  2.4 3.2 %copy-start = (f32[4,48,128]{2,1,0:T(8,128)}, f32[4,48,128]{2,1,0:T(8,128)S(1)}, u32[]{:S(2)}) copy-start(f32[4,48,128]{2,1,0:T(8,128)S(1)} %get-tuple-element.21.far_edges_ref) | copy-start | bytes 294916
  2.6 12.0 %collective-permute-start.2 = (f16[4,560,128]{2,1,0:T(8,128)(2,1)S(1)}, f16[4,560,128]{2,1,0:T(8,128)(2,1)S(1)}, u32[]{:S(2)}, u32[]{:S(2)}) collective-permute-start(f16[4,560,128]{2,1,0:T(8,128)(2,1)S(1)} %select_convert_fusion.2), channel_id=1, source_target_pairs={{0,2},{1,3},{2,0},{3,1},{4,6},{5,7},{6,4},{7,5},{8,10},{9,11},{10,... | collective-permute-start | bytes 1720328 | tf_op jit(solution)/shard_map/ppermute | solution.py:534
  10.2 10.1 %collective-permute-start = (f16[4,560,128]{2,1,0:T(8,128)(2,1)S(1)}, f16[4,560,128]{2,1,0:T(8,128)(2,1)S(1)}, u32[]{:S(2)}, u32[]{:S(2)}) collective-permute-start(f16[4,560,128]{2,1,0:T(8,128)(2,1)S(1)} %get-tuple-element.32), channel_id=1, source_target_pairs={{0,3},{1,2},{2,1},{3,0},{4,7},{5,6},{6,5},{7,4},{8,11},{9,10},{10,... | collective-permute-start | bytes 1720328 | tf_op jit(solution)/shard_map/ppermute | solution.py:534
  11.1 9.3 %collective-permute-start.1 = (f16[4,560,128]{2,1,0:T(8,128)(2,1)S(1)}, f16[4,560,128]{2,1,0:T(8,128)(2,1)S(1)}, u32[]{:S(2)}, u32[]{:S(2)}) collective-permute-start(f16[4,560,128]{2,1,0:T(8,128)(2,1)S(1)} %get-tuple-element.33), channel_id=1, source_target_pairs={{0,1},{1,0},{2,3},{3,2},{4,5},{5,4},{6,7},{7,6},{8,9},{9,8},{10,11... | collective-permute-start | bytes 1720328 | tf_op jit(solution)/shard_map/ppermute | solution.py:534
  20.8 5.9 %collective-permute-start.3 = (f16[560,128]{1,0:T(8,128)(2,1)S(1)}, f16[560,128]{1,0:T(8,128)(2,1)S(1)}, u32[]{:S(2)}, u32[]{:S(2)}) collective-permute-start(f16[560,128]{1,0:T(8,128)(2,1)S(1)} %get-tuple-element.29), channel_id=1, source_target_pairs={{0,8},{1,9},{2,10},{3,11},{4,12},{5,13},{6,14},{7,15},{8,0},{9,1},... | collective-permute-start | bytes 430088 | tf_op jit(solution)/shard_map/ppermute | solution.py:534
  24.3 5.4 %collective-permute-start.5 = (f16[560,128]{1,0:T(8,128)(2,1)S(1)}, f16[560,128]{1,0:T(8,128)(2,1)S(1)}, u32[]{:S(2)}, u32[]{:S(2)}) collective-permute-start(f16[560,128]{1,0:T(8,128)(2,1)S(1)} %get-tuple-element.30), channel_id=1, source_target_pairs={{0,12},{1,13},{2,14},{3,15},{4,8},{5,9},{6,10},{7,11},{8,4},{9,5},... | collective-permute-start | bytes 430088 | tf_op jit(solution)/shard_map/ppermute | solution.py:534
  24.8 4.9 %collective-permute-start.4 = (f16[560,128]{1,0:T(8,128)(2,1)S(1)}, f16[560,128]{1,0:T(8,128)(2,1)S(1)}, u32[]{:S(2)}, u32[]{:S(2)}) collective-permute-start(f16[560,128]{1,0:T(8,128)(2,1)S(1)} %get-tuple-element.31), channel_id=1, source_target_pairs={{0,4},{1,5},{2,6},{3,7},{4,0},{5,1},{6,2},{7,3},{8,12},{9,13},{10,... | collective-permute-start | bytes 430088 | tf_op jit(solution)/shard_map/ppermute | solution.py:534
  43.9 7.5 %collective-permute-start.11 = (f32[640,128]{1,0:T(8,128)S(1)}, f32[640,128]{1,0:T(8,128)S(1)}, u32[]{:S(2)}, u32[]{:S(2)}) collective-permute-start(f32[640,128]{1,0:T(8,128)S(1)} %bitcast.107), channel_id=1, source_target_pairs={{0,64},{16,80},{32,96},{48,112},{64,0},{80,16},{96,32},{112,48},{1... | collective-permute-start | bytes 983048 | tf_op jit(solution)/shard_map/ppermute | solution.py:521
  45.1 14.1 %collective-permute-start.7 = (f32[640,128]{1,0:T(8,128)S(1)}, f32[640,128]{1,0:T(8,128)S(1)}, u32[]{:S(2)}, u32[]{:S(2)}) collective-permute-start(f32[640,128]{1,0:T(8,128)S(1)} %bitcast.108), channel_id=1, source_target_pairs={{0,32},{16,48},{32,64},{48,80},{64,96},{80,112},{96,0},{112,16},{1... | collective-permute-start | bytes 983048 | tf_op jit(solution)/shard_map/ppermute | solution.py:521
  46.9 13.6 %collective-permute-start.9 = (f32[640,128]{1,0:T(8,128)S(1)}, f32[640,128]{1,0:T(8,128)S(1)}, u32[]{:S(2)}, u32[]{:S(2)}) collective-permute-start(f32[640,128]{1,0:T(8,128)S(1)} %bitcast.109), channel_id=1, source_target_pairs={{0,96},{16,112},{32,0},{48,16},{64,32},{80,48},{96,64},{112,80},{1... | collective-permute-start | bytes 983048 | tf_op jit(solution)/shard_map/ppermute | solution.py:521
  51.5 11.1 %collective-permute-start.12 = (f32[640,128]{1,0:T(8,128)S(1)}, f32[640,128]{1,0:T(8,128)S(1)}, u32[]{:S(2)}, u32[]{:S(2)}) collective-permute-start(f32[640,128]{1,0:T(8,128)S(1)} %collective-permute-done.11.own_ref), channel_id=1, source_target_pairs={{0,16},{16,0},{32,48},{48,32},{64,80},{80,64},{96,112},{112,96},{1... | collective-permute-start | bytes 983048 | tf_op jit(solution)/shard_map/ppermute | solution.py:525
  59.2 4.4 %collective-permute-start.6 = (f32[640,128]{1,0:T(8,128)S(1)}, f32[640,128]{1,0:T(8,128)S(1)}, u32[]{:S(2)}, u32[]{:S(2)}) collective-permute-start(f32[640,128]{1,0:T(8,128)S(1)} %bitcast.110), channel_id=1, source_target_pairs={{0,16},{16,0},{32,48},{48,32},{64,80},{80,64},{96,112},{112,96},{1... | collective-permute-start | bytes 983048 | tf_op jit(solution)/shard_map/ppermute | solution.py:525
  59.2 4.4 %collective-permute-start.8 = (f32[640,128]{1,0:T(8,128)S(1)}, f32[640,128]{1,0:T(8,128)S(1)}, u32[]{:S(2)}, u32[]{:S(2)}) collective-permute-start(f32[640,128]{1,0:T(8,128)S(1)} %collective-permute-done.7.one_ref), channel_id=1, source_target_pairs={{0,16},{16,0},{32,48},{48,32},{64,80},{80,64},{96,112},{112,96},{1... | collective-permute-start | bytes 983048 | tf_op jit(solution)/shard_map/ppermute | solution.py:525
  60.4 5.1 %collective-permute-start.10 = (f32[640,128]{1,0:T(8,128)S(1)}, f32[640,128]{1,0:T(8,128)S(1)}, u32[]{:S(2)}, u32[]{:S(2)}) collective-permute-start(f32[640,128]{1,0:T(8,128)S(1)} %collective-permute-done.9.own_ref), channel_id=1, source_target_pairs={{0,16},{16,0},{32,48},{48,32},{64,80},{80,64},{96,112},{112,96},{1... | collective-permute-start | bytes 983048 | tf_op jit(solution)/shard_map/ppermute | solution.py:525

commit v7 on v6

--- a/solution.py
+++ b/solution.py
@@ -19,7 +19,7 @@
 MASS = 0.05
 
 OWN = NCOL // BANDS
-HALO = 24
+HALO = 20
 SPAN = OWN + 2 * HALO
 TILE = 128
 ROWS = R + 2
@@ -147,7 +147,7 @@
         left, right = outer[TILE - HALO : TILE], outer[TILE : TILE + HALO]
         out_ref[other, OWN : OWN + HALO] = left
         out_ref[other, OWN + HALO :] = right
-        return larger(larger(most, left), right)
+        return larger(most, jnp.concatenate([left, right], axis=0))
 
     most = lax.fori_loop(0, SIDE, chunk, jnp.zeros((8, NROW), jnp.float32))
     power_ref[...] = power_above(most)

time: 67.8 us -> 67.6 us (level)
  no operation moved by 1% of the time
where the time goes in v7:
time: 67.6 us; the launch traced here: 67.4 us
  starting transfers between devices  22.2 us (33%)
  Pallas kernels  18.3 us (27%)
  waiting for transfers between devices  14.6 us (22%)
  blocking collectives  10.2 us (15%)
  other arithmetic  1.22 us (2%)
  between operations  0.81 us (1%)
    ppermute x4, starting transfers between devices, from_other_core(): return lax.ppermute(block, 'plane', [(i, i ^ 1) for i in range(PLANES)])  11.1 us
    all_to_all x1, blocking collectives, body(): lax.all_to_all(messages, 'band', split_axis=0, concat_axis=0, axis_index_...  10.2 us
    ppermute x6, waiting for transfers between devices, exchanged(): return lax.ppermute(block, ('plane', 'band'), route)  10 us
    pallas_call x3, Pallas kernels, sum_call(): pl.pallas_call(kernel, in_specs=[pl.BlockSpec(memory_space=pl.ANY)] * 2 +...  9.5 us
    ppermute x6, starting transfers between devices, exchanged(): return lax.ppermute(block, ('plane', 'band'), route)  8.17 us
    pallas_call x3, Pallas kernels, chain_call(): pl.pallas_call(kernel, in_specs=[vmem] * len(operands), out_specs=pl.Bloc...  5.02 us
    ppermute x3, waiting for transfers between devices, from_chip(): lax.ppermute(block, 'plane', [(i, (i + 2 * back) % PLANES) for i in range...  4.58 us
    pallas_call x1, Pallas kernels, relaxed(): pl.pallas_call(relax_kernel, in_specs=[pl.BlockSpec(memory_space=pltpu.VM...  3.76 us
  transfers between devices with their start and end apart: 13, of which 4 were waited for; matrix products, arithmetic and copies ran while one was open for 1% of the time, Pallas kernels for 15%

profile of v7, /device:TPU:7, one launch (start us, length us, event | category | flops | bytes accessed | tf_op | source)
XLA Modules:
  0.0 67.4 jit_solution(200627600465743247)
XLA Ops:
  0.0 2.4 %far_sums.1 = (f32[4,552,128]{2,1,0:T(8,128)S(1)}, f32[4,40,128]{2,1,0:T(8,128)S(1)}, f32[1,128]{1,0:T(1,128)S(1)}) custom-call(s32[1,64]{1,0:T(1,128)} %slot_ref.4, bf16[64,4,8192]{2,1,0:T(4,128)(2,1)} %bitcast.114), custom_call_target="tpu_custom_call" | custom-call | tf_op jit(solution)/shard_map/far_sums/pallas_call | solution.py:226
  2.6 3.0 %collective-permute-start.2 = (f16[4,552,128]{2,1,0:T(8,128)(2,1)S(1)}, f16[4,552,128]{2,1,0:T(8,128)(2,1)S(1)}, u32[]{:S(2)}, u32[]{:S(2)}) collective-permute-start(f16[4,552,128]{2,1,0:T(8,128)(2,1)S(1)} %select_convert_fusion.2), channel_id=1, source_target_pairs={{0,2},{1,3},{2,0},{3,1},{4,6},{5,7},{6,4},{7,5},{8,10},{9,11},{10,... | collective-permute-start | bytes 1695752 | tf_op jit(solution)/shard_map/ppermute | solution.py:534
  5.6 4.2 %near_sums.1 = (f32[4,552,128]{2,1,0:T(8,128)S(1)}, f32[4,552,128]{2,1,0:T(8,128)S(1)}, f32[1,128]{1,0:T(1,128)S(1)}) custom-call(s32[1,64]{1,0:T(1,128)} %slot_ref.4, bf16[64,4,8192]{2,1,0:T(4,128)(2,1)} %bitcast.115, f32[4,40,128]{2,1,0:T(8,128)} %copy-done), custom_call_target="tpu_custom_call" | custom-call | tf_op jit(solution)/shard_map/near_sums/pallas_call | solution.py:226
  9.9 0.4 select_convert_fusion.1
  10.2 0.9 %collective-permute-start = (f16[4,552,128]{2,1,0:T(8,128)(2,1)S(1)}, f16[4,552,128]{2,1,0:T(8,128)(2,1)S(1)}, u32[]{:S(2)}, u32[]{:S(2)}) collective-permute-start(f16[4,552,128]{2,1,0:T(8,128)(2,1)S(1)} %get-tuple-element.32), channel_id=1, source_target_pairs={{0,3},{1,2},{2,1},{3,0},{4,7},{5,6},{6,5},{7,4},{8,11},{9,10},{10,... | collective-permute-start | bytes 1695752 | tf_op jit(solution)/shard_map/ppermute | solution.py:534
  11.8 2.9 %own_sums.1 = (f32[4,552,128]{2,1,0:T(8,128)S(1)}, f32[4,40,128]{2,1,0:T(8,128)}, f32[1,128]{1,0:T(1,128)S(1)}, f32[1,128]{1,0:T(1,128)S(1)}) custom-call(s32[1,64]{1,0:T(1,128)} %slot_ref.4, bf16[64,4,8192]{2,1,0:T(4,128)(2,1)} %bitcast.116, f32[1]{0:T(128)S(6)} %copy.4.weight_ref), custom_call_target="tpu_custom_call" | custom-call | tf_op jit(solution)/shard_map/own_sums/pallas_call | solution.py:226
  14.7 5.6 %collective-permute-done = f16[4,552,128]{2,1,0:T(8,128)(2,1)S(1)} collective-permute-done((f16[4,552,128]{2,1,0:T(8,128)(2,1)S(1)}, f16[4,552,128]{2,1,0:T(8,128)(2,1)S(1)}, u32[]{:S(2)}, u32[]{:S(2)}) %collective-permute-start) | collective-permute-done | bytes 565280 | tf_op jit(solution)/shard_map/ppermute | solution.py:534
  20.3 0.4 fusion.15
  20.7 3.4 %collective-permute-start.3 = (f16[552,128]{1,0:T(8,128)(2,1)S(1)}, f16[552,128]{1,0:T(8,128)(2,1)S(1)}, u32[]{:S(2)}, u32[]{:S(2)}) collective-permute-start(f16[552,128]{1,0:T(8,128)(2,1)S(1)} %get-tuple-element.29), channel_id=1, source_target_pairs={{0,8},{1,9},{2,10},{3,11},{4,12},{5,13},{6,14},{7,15},{8,0},{9,1},... | collective-permute-start | bytes 423944 | tf_op jit(solution)/shard_map/ppermute | solution.py:534
  24.1 0.4 collective-permute-start.5
  24.6 0.5 collective-permute-start.4
  25.1 1.6 %collective-permute-done.3 = f16[552,128]{1,0:T(8,128)(2,1)S(1)} collective-permute-done((f16[552,128]{1,0:T(8,128)(2,1)S(1)}, f16[552,128]{1,0:T(8,128)(2,1)S(1)}, u32[]{:S(2)}, u32[]{:S(2)}) %collective-permute-start.3) | collective-permute-done | bytes 141344 | tf_op jit(solution)/shard_map/ppermute | solution.py:534
  26.6 2.9 %collective-permute-done.5 = f16[552,128]{1,0:T(8,128)(2,1)S(1)} collective-permute-done((f16[552,128]{1,0:T(8,128)(2,1)S(1)}, f16[552,128]{1,0:T(8,128)(2,1)S(1)}, u32[]{:S(2)}, u32[]{:S(2)}) %collective-permute-start.5) | collective-permute-done | bytes 141344 | tf_op jit(solution)/shard_map/ppermute | solution.py:534
  29.7 3.8 %relaxed.1 = f32[16,40,128]{2,1,0:T(8,128)S(1)} custom-call(f32[1,128]{1,0:T(1,128)S(1)} %get-tuple-element.16.weight_ref, f32[552,128]{1,0:T(8,128)S(1)} %fusion.21.part_ref), custom_call_target="tpu_custom_call" | custom-call | tf_op jit(solution)/shard_map/relaxed/pallas_call | solution.py:328
  33.5 10.2 %all_to_all.5 = f32[16,40,128]{2,1,0:T(8,128)S(1)} all-to-all(f32[16,40,128]{2,1,0:T(8,128)S(1)} %relaxed.1), channel_id=1, replica_groups={{15,14,13,12,11,10,9,8,7,6,5,4,3,2,1,0},{31,30,29,28,27,26,25,24,23,22,..., dimensions={0} | all-to-all | bytes 655360 | tf_op jit(solution)/shard_map/all_to_all | solution.py:581
  43.7 1.1 %collective-permute-start.11 = (f32[640,128]{1,0:T(8,128)S(1)}, f32[640,128]{1,0:T(8,128)S(1)}, u32[]{:S(2)}, u32[]{:S(2)}) collective-permute-start(f32[640,128]{1,0:T(8,128)S(1)} %bitcast.107), channel_id=1, source_target_pairs={{0,64},{16,80},{32,96},{48,112},{64,0},{80,16},{96,32},{112,48},{1... | collective-permute-start | bytes 983048 | tf_op jit(solution)/shard_map/ppermute | solution.py:521
  44.8 1.8 %collective-permute-start.7 = (f32[640,128]{1,0:T(8,128)S(1)}, f32[640,128]{1,0:T(8,128)S(1)}, u32[]{:S(2)}, u32[]{:S(2)}) collective-permute-start(f32[640,128]{1,0:T(8,128)S(1)} %bitcast.108), channel_id=1, source_target_pairs={{0,32},{16,48},{32,64},{48,80},{64,96},{80,112},{96,0},{112,16},{1... | collective-permute-start | bytes 983048 | tf_op jit(solution)/shard_map/ppermute | solution.py:521
  46.6 4.6 %collective-permute-done.11.own_ref = f32[640,128]{1,0:T(8,128)S(1)} collective-permute-done((f32[640,128]{1,0:T(8,128)S(1)}, f32[640,128]{1,0:T(8,128)S(1)}, u32[]{:S(2)}, u32[]{:S(2)}) %collective-permute-start.11) | collective-permute-done | bytes 327712 | tf_op jit(solution)/shard_map/ppermute | solution.py:521
  51.2 7.7 %collective-permute-start.12 = (f32[640,128]{1,0:T(8,128)S(1)}, f32[640,128]{1,0:T(8,128)S(1)}, u32[]{:S(2)}, u32[]{:S(2)}) collective-permute-start(f32[640,128]{1,0:T(8,128)S(1)} %collective-permute-done.11.own_ref), channel_id=1, source_target_pairs={{0,16},{16,0},{32,48},{48,32},{64,80},{80,64},{96,112},{112,96},{1... | collective-permute-start | bytes 983048 | tf_op jit(solution)/shard_map/ppermute | solution.py:525
  58.9 1.3 %collective-permute-start.8 = (f32[640,128]{1,0:T(8,128)S(1)}, f32[640,128]{1,0:T(8,128)S(1)}, u32[]{:S(2)}, u32[]{:S(2)}) collective-permute-start(f32[640,128]{1,0:T(8,128)S(1)} %collective-permute-done.7.one_ref), channel_id=1, source_target_pairs={{0,16},{16,0},{32,48},{48,32},{64,80},{80,64},{96,112},{112,96},{1... | collective-permute-start | bytes 983048 | tf_op jit(solution)/shard_map/ppermute | solution.py:525
  60.2 2.1 %collective-permute-start.10 = (f32[640,128]{1,0:T(8,128)S(1)}, f32[640,128]{1,0:T(8,128)S(1)}, u32[]{:S(2)}, u32[]{:S(2)}) collective-permute-start(f32[640,128]{1,0:T(8,128)S(1)} %collective-permute-done.9.own_ref), channel_id=1, source_target_pairs={{0,16},{16,0},{32,48},{48,32},{64,80},{80,64},{96,112},{112,96},{1... | collective-permute-start | bytes 983048 | tf_op jit(solution)/shard_map/ppermute | solution.py:525
  62.3 1.0 %chain_middle.1.middle_ref = f32[6,8,8192]{2,1,0:T(8,128)S(1)} custom-call(f32[640,128]{1,0:T(8,128)S(1)} %collective-permute-done.11.own_ref, f32[640,128]{1,0:T(8,128)S(1)} %collective-permute-done.12.other_ref), custom_call_target="tpu_custom_call" | custom-call | flops 5242880 | bytes 2228224 | tf_op jit(solution)/shard_map/chain_middle/pallas_call | solution.py:504
  63.3 1.9 %chain_recent.1.state_ref = f32[6,8,8192]{2,1,0:T(8,128)S(1)} custom-call(f32[640,128]{1,0:T(8,128)S(1)} %bitcast.111, f32[640,128]{1,0:T(8,128)S(1)} %collective-permute-done.6.other_ref, f32[640,128]{1,0:T(8,128)S(1)} %collective-permute-done.7.one_ref, f32[640,128]{1,0:T(8,128)S(1)} %collective-permute-done.8.one_other_ref), custom_call_target="tpu_custom_call" | custom-call | flops 5242880 | bytes 2883584 | tf_op jit(solution)/shard_map/chain_recent/pallas_call | solution.py:504
  65.3 2.1 %chain_finish.1 = f32[1,6,8,8192]{3,2,1,0:T(8,128)} custom-call(f32[6,8,8192]{2,1,0:T(8,128)S(1)} %chain_recent.1.state_ref, f32[640,128]{1,0:T(8,128)S(1)} %collective-permute-done.9.own_ref, f32[640,128]{1,0:T(8,128)S(1)} %collective-permute-done.10.other_ref, f32[6,8,8192]{2,1,0:T(8,128)S(1)} %chain_middle.1.middle_ref), custom_call_target="tpu_custom_call" | custom-call | flops 5242880 | bytes 5373952 | tf_op jit(solution)/shard_map/chain_finish/pallas_call | solution.py:504
  (26 shorter events, 0.5 us)
Async XLA Ops:
  2.4 3.2 %copy-start = (f32[4,40,128]{2,1,0:T(8,128)}, f32[4,40,128]{2,1,0:T(8,128)S(1)}, u32[]{:S(2)}) copy-start(f32[4,40,128]{2,1,0:T(8,128)S(1)} %get-tuple-element.21.far_edges_ref) | copy-start | bytes 245764
  2.6 12.0 %collective-permute-start.2 = (f16[4,552,128]{2,1,0:T(8,128)(2,1)S(1)}, f16[4,552,128]{2,1,0:T(8,128)(2,1)S(1)}, u32[]{:S(2)}, u32[]{:S(2)}) collective-permute-start(f16[4,552,128]{2,1,0:T(8,128)(2,1)S(1)} %select_convert_fusion.2), channel_id=1, source_target_pairs={{0,2},{1,3},{2,0},{3,1},{4,6},{5,7},{6,4},{7,5},{8,10},{9,11},{10,... | collective-permute-start | bytes 1695752 | tf_op jit(solution)/shard_map/ppermute | solution.py:534
  10.2 10.1 %collective-permute-start = (f16[4,552,128]{2,1,0:T(8,128)(2,1)S(1)}, f16[4,552,128]{2,1,0:T(8,128)(2,1)S(1)}, u32[]{:S(2)}, u32[]{:S(2)}) collective-permute-start(f16[4,552,128]{2,1,0:T(8,128)(2,1)S(1)} %get-tuple-element.32), channel_id=1, source_target_pairs={{0,3},{1,2},{2,1},{3,0},{4,7},{5,6},{6,5},{7,4},{8,11},{9,10},{10,... | collective-permute-start | bytes 1695752 | tf_op jit(solution)/shard_map/ppermute | solution.py:534
  11.1 9.2 %collective-permute-start.1 = (f16[4,552,128]{2,1,0:T(8,128)(2,1)S(1)}, f16[4,552,128]{2,1,0:T(8,128)(2,1)S(1)}, u32[]{:S(2)}, u32[]{:S(2)}) collective-permute-start(f16[4,552,128]{2,1,0:T(8,128)(2,1)S(1)} %get-tuple-element.33), channel_id=1, source_target_pairs={{0,1},{1,0},{2,3},{3,2},{4,5},{5,4},{6,7},{7,6},{8,9},{9,8},{10,11... | collective-permute-start | bytes 1695752 | tf_op jit(solution)/shard_map/ppermute | solution.py:534
  20.7 5.9 %collective-permute-start.3 = (f16[552,128]{1,0:T(8,128)(2,1)S(1)}, f16[552,128]{1,0:T(8,128)(2,1)S(1)}, u32[]{:S(2)}, u32[]{:S(2)}) collective-permute-start(f16[552,128]{1,0:T(8,128)(2,1)S(1)} %get-tuple-element.29), channel_id=1, source_target_pairs={{0,8},{1,9},{2,10},{3,11},{4,12},{5,13},{6,14},{7,15},{8,0},{9,1},... | collective-permute-start | bytes 423944 | tf_op jit(solution)/shard_map/ppermute | solution.py:534
  24.1 5.3 %collective-permute-start.5 = (f16[552,128]{1,0:T(8,128)(2,1)S(1)}, f16[552,128]{1,0:T(8,128)(2,1)S(1)}, u32[]{:S(2)}, u32[]{:S(2)}) collective-permute-start(f16[552,128]{1,0:T(8,128)(2,1)S(1)} %get-tuple-element.30), channel_id=1, source_target_pairs={{0,12},{1,13},{2,14},{3,15},{4,8},{5,9},{6,10},{7,11},{8,4},{9,5},... | collective-permute-start | bytes 423944 | tf_op jit(solution)/shard_map/ppermute | solution.py:534
  24.6 4.9 %collective-permute-start.4 = (f16[552,128]{1,0:T(8,128)(2,1)S(1)}, f16[552,128]{1,0:T(8,128)(2,1)S(1)}, u32[]{:S(2)}, u32[]{:S(2)}) collective-permute-start(f16[552,128]{1,0:T(8,128)(2,1)S(1)} %get-tuple-element.31), channel_id=1, source_target_pairs={{0,4},{1,5},{2,6},{3,7},{4,0},{5,1},{6,2},{7,3},{8,12},{9,13},{10,... | collective-permute-start | bytes 423944 | tf_op jit(solution)/shard_map/ppermute | solution.py:534
  43.7 7.5 %collective-permute-start.11 = (f32[640,128]{1,0:T(8,128)S(1)}, f32[640,128]{1,0:T(8,128)S(1)}, u32[]{:S(2)}, u32[]{:S(2)}) collective-permute-start(f32[640,128]{1,0:T(8,128)S(1)} %bitcast.107), channel_id=1, source_target_pairs={{0,64},{16,80},{32,96},{48,112},{64,0},{80,16},{96,32},{112,48},{1... | collective-permute-start | bytes 983048 | tf_op jit(solution)/shard_map/ppermute | solution.py:521
  44.8 14.1 %collective-permute-start.7 = (f32[640,128]{1,0:T(8,128)S(1)}, f32[640,128]{1,0:T(8,128)S(1)}, u32[]{:S(2)}, u32[]{:S(2)}) collective-permute-start(f32[640,128]{1,0:T(8,128)S(1)} %bitcast.108), channel_id=1, source_target_pairs={{0,32},{16,48},{32,64},{48,80},{64,96},{80,112},{96,0},{112,16},{1... | collective-permute-start | bytes 983048 | tf_op jit(solution)/shard_map/ppermute | solution.py:521
  46.6 13.6 %collective-permute-start.9 = (f32[640,128]{1,0:T(8,128)S(1)}, f32[640,128]{1,0:T(8,128)S(1)}, u32[]{:S(2)}, u32[]{:S(2)}) collective-permute-start(f32[640,128]{1,0:T(8,128)S(1)} %bitcast.109), channel_id=1, source_target_pairs={{0,96},{16,112},{32,0},{48,16},{64,32},{80,48},{96,64},{112,80},{1... | collective-permute-start | bytes 983048 | tf_op jit(solution)/shard_map/ppermute | solution.py:521
  51.2 11.1 %collective-permute-start.12 = (f32[640,128]{1,0:T(8,128)S(1)}, f32[640,128]{1,0:T(8,128)S(1)}, u32[]{:S(2)}, u32[]{:S(2)}) collective-permute-start(f32[640,128]{1,0:T(8,128)S(1)} %collective-permute-done.11.own_ref), channel_id=1, source_target_pairs={{0,16},{16,0},{32,48},{48,32},{64,80},{80,64},{96,112},{112,96},{1... | collective-permute-start | bytes 983048 | tf_op jit(solution)/shard_map/ppermute | solution.py:525
  58.9 4.4 %collective-permute-start.6 = (f32[640,128]{1,0:T(8,128)S(1)}, f32[640,128]{1,0:T(8,128)S(1)}, u32[]{:S(2)}, u32[]{:S(2)}) collective-permute-start(f32[640,128]{1,0:T(8,128)S(1)} %bitcast.110), channel_id=1, source_target_pairs={{0,16},{16,0},{32,48},{48,32},{64,80},{80,64},{96,112},{112,96},{1... | collective-permute-start | bytes 983048 | tf_op jit(solution)/shard_map/ppermute | solution.py:525
  58.9 4.4 %collective-permute-start.8 = (f32[640,128]{1,0:T(8,128)S(1)}, f32[640,128]{1,0:T(8,128)S(1)}, u32[]{:S(2)}, u32[]{:S(2)}) collective-permute-start(f32[640,128]{1,0:T(8,128)S(1)} %collective-permute-done.7.one_ref), channel_id=1, source_target_pairs={{0,16},{16,0},{32,48},{48,32},{64,80},{80,64},{96,112},{112,96},{1... | collective-permute-start | bytes 983048 | tf_op jit(solution)/shard_map/ppermute | solution.py:525
  60.2 5.1 %collective-permute-start.10 = (f32[640,128]{1,0:T(8,128)S(1)}, f32[640,128]{1,0:T(8,128)S(1)}, u32[]{:S(2)}, u32[]{:S(2)}) collective-permute-start(f32[640,128]{1,0:T(8,128)S(1)} %collective-permute-done.9.own_ref), channel_id=1, source_target_pairs={{0,16},{16,0},{32,48},{48,32},{64,80},{80,64},{96,112},{112,96},{1... | collective-permute-start | bytes 983048 | tf_op jit(solution)/shard_map/ppermute | solution.py:525
